TPU v7x, 32 devices: a whole 2x2x4 slice. The times are simulated.
32 devices in a mesh: noise: 4 (over y, x), row: 8 (over z, core).
Axes of the slice: x: 2, y: 2, z: 4, core: 2. Of those that a mesh axis runs over, the one named last changes fastest.
Arguments:
- activations: bfloat16 [16, 512, 768], P('noise', 'row'), may hold values from -6 to 6
- cond_scale: bfloat16 [16, 512, 768], P('noise', 'row'), may hold values from 0.25 to 16
- cond_shift: bfloat16 [16, 512, 768], P('noise', 'row'), may hold values from -4 to 4
- output_gate: bfloat16 [16, 512, 768], P('noise', 'row'), may hold values from -8 to 8
- pair_repr: bfloat16 [512, 512, 128], P('row', 'noise'), may hold values from -6 to 6
- bias_weight: bfloat16 [128, 8], replicated, may hold values from -1.5 to 1.5
- query_weight: bfloat16 [768, 384], P('noise'), may hold values from -0.21875 to 0.21875
- query_bias: bfloat16 [384], replicated, may hold values from -4 to 4
- key_weight: bfloat16 [768, 384], P('noise'), may hold values from -0.21875 to 0.21875
- value_weight: bfloat16 [768, 384], P('noise'), may hold values from -0.21875 to 0.21875
- output_weight: bfloat16 [384, 768], P('noise'), may hold values from -0.3125 to 0.3125
- token_mask: int32 [16, 512], P('noise', 'row'), may hold values from 0 to 1, as said below
Outputs:
- updated: bfloat16 [16, 512, 768], P('noise', 'row')
Inputs may be any that keep to these rules, and one draw needn't show every extreme that they name: `token_mask`: in each sample the tokens with mask 1 form a prefix of half of 512 tokens or more, and some sample has all 512 tokens.
All inputs are finite; a program needn't handle non-finite values.
Results may differ from a plain program's by a relative error of at most 0.012.
The roundings to bfloat16 on the way count: a program that leaves them out, or rounds other values in their place, can miss the bound.
Values may be sent and summed in bfloat16 or wider, within the bound.
No kernel may reach another device: no remote copies, remote signals or barrier semaphores. Data moves between devices by JAX's collectives and lax.ppermute only.
A program may use at most 128 MiB of HBM per device.

v0:
```python
import functools
import math

import jax
import jax.numpy as jnp
from jax import lax
from jax.experimental import pallas as pl
from jax.experimental.pallas import tpu as pltpu
from jax.sharding import PartitionSpec as P

epsilon = 1e-05
masked_score = -1e30
absent = 32768.0
log2_e = math.log2(math.e)
vmem_bytes = 40 * 2**20
wide_bytes = 60 * 2**20


def layer_norm(tensor):
    average = jnp.mean(tensor, axis=-1, keepdims=True)
    centred = tensor - average
    variance = jnp.mean(centred * centred, axis=-1, keepdims=True)
    return centred * lax.rsqrt(variance + epsilon)


def shift_kernel(
    activations_hbm,
    scale_hbm,
    shift_hbm,
    mask_hbm,
    query_hbm,
    key_hbm,
    output_hbm,
    shifted_hbm,
    sent_hbm,
    packed_hbm,
    columns_hbm,
    shifted,
    sent,
    packed,
    columns,
    activations,
    cond_scale,
    cond_shift,
    token_mask,
    query_weight,
    key_weight,
    output_weight,
    sems,
    sems_out,
):
    samples, rows, features = activations.shape
    copies = [pltpu.make_async_copy(mask_hbm, token_mask, sems.at[0])]
    for s in range(samples):
        for t, (source, target) in enumerate(
            ((activations_hbm, activations), (scale_hbm, cond_scale), (shift_hbm, cond_shift))
        ):
            copies.append(pltpu.make_async_copy(source.at[s], target.at[s], sems.at[1 + 3 * s + t]))
    copies.append(pltpu.make_async_copy(query_hbm, query_weight, sems.at[1 + 3 * samples]))
    copies.append(pltpu.make_async_copy(key_hbm, key_weight, sems.at[2 + 3 * samples]))
    copies.append(pltpu.make_async_copy(output_hbm, output_weight, sems.at[3 + 3 * samples]))
    for copy in copies:
        copy.start()
    diagonal = lax.broadcasted_iota(jnp.int32, (rows, rows), 0) == lax.broadcasted_iota(
        jnp.int32, (rows, rows), 1
    )
    copies[0].wait()
    written = []
    for s in range(samples):
        for copy in copies[1 + 3 * s : 4 + 3 * s]:
            copy.wait()
        normed = layer_norm(activations[s].astype(jnp.float32))
        result = cond_scale[s].astype(jnp.float32) * normed + cond_shift[s].astype(jnp.float32)
        flags = jnp.where(diagonal, token_mask[s : s + 1, :].astype(jnp.float32), 0.0)
        valid = jnp.sum(flags, axis=1, keepdims=True) > 0.0
        shifted[s] = result.astype(jnp.bfloat16)
        sent[s] = jnp.where(valid, result, absent).astype(jnp.bfloat16)
        for t, (source, target) in enumerate(((sent, sent_hbm), (shifted, shifted_hbm))):
            written.append(pltpu.make_async_copy(source.at[s], target.at[s], sems_out.at[2 * s + t]))
            written[-1].start()
    core = lax.rem(lax.axis_index("row"), 2)
    half, breadth = packed.shape[0], query_weight.shape[1]
    for w, weight in enumerate((query_weight, key_weight)):
        copies[1 + 3 * samples + w].wait()
        whole = weight[...].astype(jnp.float32)
        packed[:, w * breadth : (w + 1) * breadth] = jnp.where(
            core == 0, whole[:half], whole[half:]
        ).astype(jnp.bfloat16)
    written.append(pltpu.make_async_copy(packed, packed_hbm, sems_out.at[2 * samples]))
    written[-1].start()
    copies[-1].wait()
    columns[...] = jnp.where(core == 0, output_weight[:, :breadth], output_weight[:, breadth:])
    written.append(pltpu.make_async_copy(columns, columns_hbm, sems_out.at[2 * samples + 1]))
    written[-1].start()
    for copy in written:
        copy.wait()


def bias_kernel(pair_hbm, value_hbm, weights_hbm, parcel, pair, value_weight, weights, collected, sems):
    rows, columns, channels = pair.shape
    heads = weights.shape[0]
    per, batches = 8, 2
    batch = rows // batches
    copies = [pltpu.make_async_copy(weights_hbm, weights, sems.at[batches])]
    for i in range(batches):
        here = pl.ds(i * batch, batch)
        copies.append(pltpu.make_async_copy(pair_hbm.at[here], pair.at[here], sems.at[i]))
    copies.append(pltpu.make_async_copy(value_hbm, value_weight, sems.at[batches + 1]))
    for copy in copies:
        copy.start()
    copies[0].wait()
    record = 2 * heads
    extended = jnp.concatenate(
        [weights[...], jnp.full((heads, channels), 1.0 / channels, jnp.bfloat16)], axis=0
    )
    square = (channels, channels)
    diagonal = lax.broadcasted_iota(jnp.int32, square, 0) == lax.broadcasted_iota(jnp.int32, square, 1)
    centring = (jnp.where(diagonal, 1.0, 0.0) - 1.0 / channels).astype(jnp.bfloat16)
    lane = lax.broadcasted_iota(jnp.int32, (1, rows), 1)
    squares = jnp.zeros((columns, rows), jnp.float32)
    for i in range(rows // per):
        if i * per % batch == 0:
            copies[1 + i * per // batch].wait()
        block = pair[i * per : (i + 1) * per].reshape(per * columns, channels)
        centred = jnp.dot(block, centring, preferred_element_type=jnp.float32)
        summed = jnp.sum(centred * centred, axis=1, keepdims=True)
        result = lax.dot_general(
            extended, block, (((1,), (1,)), ((), ())), preferred_element_type=jnp.float32
        )
        for r in range(per):
            row = i * per + r
            collected[row * record : (row + 1) * record, :] = result[:, r * columns : (r + 1) * columns]
            squares = jnp.where(lane == row, summed[r * columns : (r + 1) * columns], squares)
    core = lax.rem(lax.axis_index("row"), 2)
    half = columns // 2
    average = collected[pl.ds(heads, rows, stride=record), :].T
    inverse = lax.rsqrt(squares / channels + epsilon)
    for p in range(heads // 2):
        own, other = [], []
        for h in (2 * p, 2 * p + 1):
            summed = jnp.sum(weights[h : h + 1, :].astype(jnp.float32), axis=1, keepdims=True)
            turned = (collected[pl.ds(h, rows, stride=record), :].T - average * summed) * inverse
            low, up = turned[:half], turned[half:]
            own.append(jnp.where(core == 0, low, up))
            other.append(jnp.where(core == 0, up, low))
        at = p * half
        parcel[at : at + half, :] = jnp.concatenate(own, axis=1).astype(jnp.bfloat16)
        at += heads // 2 * half
        parcel[at : at + half, :] = jnp.concatenate(other[::-1], axis=1).astype(jnp.bfloat16)
    copies[-1].wait()
    depth, breadth = value_weight.shape
    whole = value_weight[...].astype(jnp.float32)
    kept = jnp.where(core == 0, whole[: depth // 2], whole[depth // 2 :]).astype(jnp.bfloat16)
    for t in range(breadth // columns):
        at = heads * half + t * (depth // 2)
        parcel[at : at + depth // 2, :] = kept[:, t * columns : (t + 1) * columns]


def spread_queries(heads, queries, spread):
    count, head_features = queries.shape
    width = head_features // heads
    reach = spread.shape[1]
    lane = lax.broadcasted_iota(jnp.int32, (1, reach), 1)
    turned = jnp.concatenate([queries[count // 2 :], queries[: count // 2]], axis=0)
    for h in range(heads):
        start, free = (0, reach - 1) if h < heads // 2 else (head_features - reach, 0)
        inside = ((lane >= h * width - start) & (lane < (h + 1) * width - start)).astype(jnp.bfloat16)
        extra = (lane == free).astype(jnp.bfloat16)
        own = (turned if h % 2 else queries)[:, start : start + reach]
        spread[h * count : (h + 1) * count, :] = own * inside + extra


def attend_keys(heads, tokens, keys, values, bias_of, spread):
    head_features = values.shape[0]
    width = head_features // heads
    count, reach = spread.shape[0] // heads, spread.shape[1]
    used = heads // 2 * width
    penalty = jnp.where(tokens[:, 0:1].astype(jnp.float32) > absent / 2, masked_score, 0.0)
    lane = lax.broadcasted_iota(jnp.int32, (1, reach), 1)
    scores = []
    for part in range(2):
        start = part * (head_features - reach)
        inside = lane < used if part == 0 else lane >= reach - used
        extended = jnp.where(inside, keys[:, start : start + reach], penalty).astype(jnp.bfloat16)
        scores.append(
            lax.dot_general(
                extended,
                spread[part * heads // 2 * count : (part + 1) * heads // 2 * count, :],
                (((1,), (1,)), ((), ())),
                preferred_element_type=jnp.float32,
            )
        )
    sums, highs, totals = [], [], []
    for h in range(heads):
        at = h % (heads // 2) * count
        score = scores[h // (heads // 2)][:, at : at + count] * (log2_e / math.sqrt(width))
        score = score + bias_of(h) * log2_e
        high = jnp.max(score, axis=0, keepdims=True)
        probs = jnp.exp2(score - high)
        totals.append(jnp.sum(probs, axis=0, keepdims=True))
        highs.append(high)
        sums.append(
            jnp.dot(
                values[h * width : (h + 1) * width],
                probs.astype(jnp.bfloat16),
                preferred_element_type=jnp.float32,
            )
        )
    return sums, highs, totals


def bias_picker(parcel, swapped, steps, first, rows):
    chip = lax.axis_index("row") // 2
    place = lax.axis_index("noise")
    left = lax.broadcasted_iota(jnp.int32, (1, 2 * rows), 1) < rows

    here = jnp.where(chip % 2 == 1, (chip + 1) // 2, lax.rem(steps - chip // 2, steps))

    def pick(b, h):
        position = lax.rem(here - (first + b) + steps, steps)
        outward = (position > 0) & (position <= steps // 2)
        origin = jnp.where(outward, 2 * position - 1, 2 * lax.rem(steps - position, steps))
        part = origin ^ place
        at = slice(h // 2 * rows, (h // 2 + 1) * rows)
        pairs = parcel[part, at].astype(jnp.float32), swapped[part, at].astype(jnp.float32)
        return jnp.where(left, pairs[h % 2], pairs[1 - h % 2])

    return pick


def early_kernel(steps, heads, weights_mine, weights_other, query_bias, shifted, parcel, swapped, swapped_value, *refs):
    blocks = refs[: steps - 1]
    partial, queries, key_weight, value_weight, full, full_value, spread = refs[steps - 1 :]
    samples, rows, features = shifted.shape
    noise_size = swapped_value.shape[0]
    half = weights_mine.shape[1] - samples * rows // noise_size
    breadth = key_weight.shape[1]
    width = breadth // heads
    core = lax.rem(lax.axis_index("row"), 2)
    place = lax.axis_index("noise")
    below = parcel.shape[1] - breadth // 128 * half
    for part, value, skipped, of_core in (
        (weights_mine, parcel, below, core),
        (weights_other, swapped_value, 0, 1 - core),
    ):
        for k in range(noise_size):
            start = ((place ^ k) * 2 + of_core) * half
            down = pl.ds(pl.multiple_of(start, math.gcd(half, 32)), half)
            full[down, :] = part[k, 0:half].astype(full.dtype)
            for t in range(breadth // 128):
                at = skipped + t * half
                full_value[down, t * 128 : (t + 1) * 128] = value[k, at : at + half].astype(full.dtype)
    key_weight[...] = full[:, breadth : 2 * breadth].astype(jnp.bfloat16)
    value_weight[...] = full_value[...].astype(jnp.float32).T.astype(jnp.bfloat16)
    for side, tokens in enumerate((shifted[...], weights_other[:, half:])):
        result = jnp.dot(
            tokens.reshape(samples * rows, features),
            full[:, 0:breadth].astype(jnp.bfloat16),
            preferred_element_type=jnp.float32,
        ) + query_bias[...].astype(jnp.float32)
        queries[:, side * rows : (side + 1) * rows] = result.astype(jnp.bfloat16).reshape(
            samples, rows, breadth
        )
    pick = bias_picker(parcel, swapped, steps, 0, rows)
    for s in range(samples):
        tokens = jnp.concatenate([block[s] for block in blocks], axis=0)
        keys = jnp.dot(tokens, key_weight[...], preferred_element_type=jnp.float32)
        values = lax.dot_general(
            value_weight[...], tokens, (((1,), (1,)), ((), ())), preferred_element_type=jnp.float32
        ).astype(jnp.bfloat16)
        spread_queries(heads, queries[s], spread)
        sums, highs, totals = attend_keys(
            heads,
            tokens,
            keys,
            values,
            lambda h: jnp.concatenate([pick(b, h) for b in range(steps - 1)], axis=0),
            spread,
        )
        for h in range(heads):
            partial[s, h * width : (h + 1) * width] = sums[h]
            partial[s, breadth + h : breadth + h + 1] = highs[h]
            partial[s, breadth + heads + h : breadth + heads + h + 1] = totals[h]


def late_kernel(steps, heads, first, partial, queries, key_weight, value_weight, parcel, swapped, block, keep, give, merged, spread):
    samples = merged.shape[0]
    rows = block.shape[1]
    breadth = key_weight.shape[1]
    width = breadth // heads
    pick = bias_picker(parcel, swapped, steps, steps - 1, rows)
    tokens = block[first : first + samples].reshape(samples * rows, block.shape[2])
    keys = jnp.dot(tokens, key_weight[...], preferred_element_type=jnp.float32)
    values = lax.dot_general(
        value_weight[...], tokens, (((1,), (1,)), ((), ())), preferred_element_type=jnp.float32
    ).astype(jnp.bfloat16)
    for s in range(samples):
        here = slice(s * rows, (s + 1) * rows)
        spread_queries(heads, queries[first + s], spread)
        sums, highs, totals = attend_keys(
            heads, tokens[here], keys[here], values[:, here], lambda h: pick(0, h), spread
        )
        before = partial.at[first + s]
        for h in range(heads):
            at_high = slice(breadth + h, breadth + h + 1)
            at_total = slice(breadth + heads + h, breadth + heads + h + 1)
            high = jnp.maximum(before[at_high], highs[h])
            old, new = jnp.exp2(before[at_high] - high), jnp.exp2(highs[h] - high)
            across = slice(h * width, (h + 1) * width)
            merged[s, across] = before[across] * old + sums[h] * new
            merged[s, at_high] = high
            merged[s, at_total] = before[at_total] * old + totals[h] * new
    half = merged.shape[2] // 2
    left = lax.broadcasted_iota(jnp.int32, (1, 2 * half), 1) < half
    row = lax.broadcasted_iota(jnp.int32, (merged.shape[1], 1), 0)
    head = jnp.where(row < breadth, row // width, (row - breadth) % heads)
    even = head % 2 == 0
    for pair in range(samples // 2):
        a, b = merged[2 * pair], merged[2 * pair + 1]
        lefts = jnp.where(left, a, pltpu.roll(b, half, 1))
        rights = jnp.where(left, pltpu.roll(a, half, 1), b)
        keep[pair] = jnp.where(even, lefts, rights)
        give[pair] = jnp.where(even, rights, lefts)


def finish_kernel(heads, first, output_mine, output_other, activations, output_gate, keep, got, *refs):
    updated_hbm, updated, output_weight, sems = refs[-4:]
    noise_size, part_rows, part_columns = output_mine.shape
    breadth = output_weight.shape[0]
    width = breadth // heads
    samples, rows, _ = updated.shape
    core = lax.rem(lax.axis_index("row"), 2)
    place = lax.axis_index("noise")
    for k in range(noise_size):
        down = pl.ds(pl.multiple_of((place ^ k) * part_rows, math.gcd(part_rows, 32)), part_rows)
        for part, of_core in ((output_mine, core), (output_other, 1 - core)):
            along = pl.ds(pl.multiple_of(of_core * part_columns, 128), part_columns)
            output_weight[down, along] = part[k].astype(output_weight.dtype)
    writes = []
    for pair in range(samples // 2):
        own, other = keep.at[pair], got.at[pair]
        parts = []
        for h in range(heads):
            at_high = slice(breadth + h, breadth + h + 1)
            at_total = slice(breadth + heads + h, breadth + heads + h + 1)
            across = slice(h * width, (h + 1) * width)
            high = jnp.maximum(own[at_high], other[at_high])
            mine, theirs = jnp.exp2(own[at_high] - high), jnp.exp2(other[at_high] - high)
            total = own[at_total] * mine + other[at_total] * theirs
            parts.append((own[across] * mine + other[across] * theirs) / total)
        attended = jnp.concatenate(parts, axis=0).T.astype(jnp.bfloat16)
        projected = jnp.dot(
            attended, output_weight[...].astype(jnp.bfloat16), preferred_element_type=jnp.float32
        )
        for side in range(2):
            s = 2 * pair + side
            gate = jax.nn.sigmoid(output_gate[first + s].astype(jnp.float32))
            updated[s] = (
                activations[first + s].astype(jnp.float32)
                + gate * projected[side * rows : (side + 1) * rows]
            ).astype(jnp.bfloat16)
            writes.append(pltpu.make_async_copy(updated.at[s], updated_hbm.at[first + s], sems.at[s]))
            writes[-1].start()
    for write in writes:
        write.wait()


def swap_cores(array):
    return lax.ppermute(array, "row", [(i, i ^ 1) for i in range(lax.axis_size("row"))])


def ring_chip(position, steps):
    return 2 * position - 1 if 0 < position <= steps // 2 else 2 * ((steps - position) % steps)


def next_chip(array):
    steps = lax.axis_size("row") // 2
    order = [ring_chip(p, steps) for p in range(steps)]
    pairs = [
        (2 * order[p] + c, 2 * order[(p + 1) % steps] + c) for p in range(steps) for c in range(2)
    ]
    return lax.ppermute(array, "row", pairs)


def from_noise(array, k):
    if k == 0:
        return array
    return lax.ppermute(array, "noise", [(i, i ^ k) for i in range(lax.axis_size("noise"))])


def body(
    activations,
    cond_scale,
    cond_shift,
    output_gate,
    pair_repr,
    bias_weight,
    query_weight,
    query_bias,
    key_weight,
    value_weight,
    output_weight,
    token_mask,
):
    samples, rows, features = activations.shape
    heads = bias_weight.shape[1]
    head_features = query_weight.shape[1]
    noise_size = lax.axis_size("noise")
    steps = lax.axis_size("row") // 2
    assert noise_size == steps and pair_repr.shape[1] == 2 * rows
    bf16, f32 = jnp.bfloat16, jnp.float32
    params = pltpu.CompilerParams(vmem_limit_bytes=vmem_bytes)
    struct = jax.ShapeDtypeStruct
    after = lax.optimization_barrier
    half = query_weight.shape[0] // 2

    in_hbm = pl.BlockSpec(memory_space=pltpu.HBM)
    packed_shape, columns_shape = (half, 2 * head_features), (output_weight.shape[0], features // 2)
    shifted, sent, packed, output_columns = pl.pallas_call(
        shift_kernel,
        in_specs=[in_hbm] * 7,
        out_specs=[in_hbm] * 4,
        out_shape=[struct(activations.shape, bf16)] * 2
        + [struct(packed_shape, bf16), struct(columns_shape, bf16)],
        scratch_shapes=[pltpu.VMEM(activations.shape, bf16)] * 2
        + [pltpu.VMEM(packed_shape, bf16), pltpu.VMEM(columns_shape, bf16)]
        + [pltpu.VMEM(activations.shape, bf16)] * 3
        + [pltpu.VMEM(token_mask.shape, jnp.int32)]
        + [pltpu.VMEM(query_weight.shape, bf16)] * 2
        + [pltpu.VMEM(output_weight.shape, bf16)]
        + [pltpu.SemaphoreType.DMA((3 * samples + 4,)), pltpu.SemaphoreType.DMA((2 * samples + 2,))],
        compiler_params=pltpu.CompilerParams(vmem_limit_bytes=wide_bytes),
        name="shift",
    )(activations, cond_scale, cond_shift, token_mask, query_weight, key_weight, output_weight)

    ring = [sent, next_chip(sent)]
    weights = [packed] + [from_noise(packed, k) for k in range(noise_size - 1, 0, -1)][::-1]
    output_next = from_noise(output_columns, 1)
    head_weights, _ = after((bias_weight.T, packed))
    columns = pair_repr.shape[1]
    tile_rows = heads * rows
    parcel = pl.pallas_call(
        bias_kernel,
        in_specs=[in_hbm] * 3,
        out_shape=struct((tile_rows + 3 * half, columns), bf16),
        scratch_shapes=[
            pltpu.VMEM(pair_repr.shape, bf16),
            pltpu.VMEM(value_weight.shape, bf16),
            pltpu.VMEM(head_weights.shape, bf16),
            pltpu.VMEM((rows * 2 * heads, columns), f32),
            pltpu.SemaphoreType.DMA((4,)),
        ],
        compiler_params=pltpu.CompilerParams(vmem_limit_bytes=wide_bytes),
        name="bias",
    )(pair_repr, value_weight, head_weights)
    ring[1], weights, parcel, output_next = after((ring[1], weights, parcel, output_next))
    ring.append(next_chip(ring[1]))
    output_mine = jnp.stack([output_columns, output_next])
    tokens = shifted.reshape(noise_size, samples * rows // noise_size, features)
    weights_mine = jnp.concatenate([jnp.stack(weights), tokens], axis=1)
    weights_other = swap_cores(weights_mine)
    parcels = [from_noise(parcel, k) for k in range(noise_size)]

    for _ in range(steps - 3):
        ring.append(next_chip(ring[-1]))
    last = ring.pop()
    parcel_mine = jnp.stack(parcels)
    swapped = swap_cores(parcel_mine[:, tile_rows // 2 : tile_rows])
    swapped_value = swap_cores(parcel_mine[:, tile_rows:])
    for k in range(1, noise_size.bit_length() - 1):
        output_mine = jnp.concatenate([output_mine, from_noise(output_mine, 2**k)], axis=0)
    output_other = swap_cores(output_mine)

    bias_row = query_bias.reshape(1, head_features)
    record = head_features + 2 * heads
    full_type = f32 if half % 16 else bf16
    output_type = f32 if output_weight.shape[0] % 16 else bf16
    spread = pltpu.VMEM((heads * 2 * rows, 256), bf16)
    partial, queries, key_full, value_full = pl.pallas_call(
        functools.partial(early_kernel, steps, heads),
        out_shape=[
            struct((samples, record, 2 * rows), f32),
            struct((samples, 2 * rows, head_features), bf16),
            struct((features, head_features), bf16),
            struct((head_features, features), bf16),
        ],
        scratch_shapes=[
            pltpu.VMEM((features, 2 * head_features), full_type),
            pltpu.VMEM((features, head_features), full_type),
            spread,
        ],
        compiler_params=params,
        name="early",
    )(weights_mine, weights_other, bias_row, shifted, parcel_mine, swapped, swapped_value, *ring)
    keep, got = [], []
    chunks = 2
    each = samples // chunks
    for c in range(chunks):
        kept, give = pl.pallas_call(
            functools.partial(late_kernel, steps, heads, c * each),
            out_shape=[struct((each // 2, record, 2 * rows), f32)] * 2,
            scratch_shapes=[pltpu.VMEM((each, record, 2 * rows), f32), spread],
            compiler_params=params,
            name="late",
        )(partial, queries, key_full, value_full, parcel_mine, swapped, last)
        keep.append(kept)
        got.append(swap_cores(give))
    updated = []
    for c in range(chunks):
        operands = [output_mine, output_other, activations, output_gate, keep[c], got[c], *updated]
        updated = [
            pl.pallas_call(
                functools.partial(finish_kernel, heads, c * each),
                in_specs=[pl.BlockSpec(memory_space=pltpu.VMEM)] * 6 + [in_hbm] * len(updated),
                out_specs=in_hbm,
                out_shape=struct(activations.shape, bf16),
                input_output_aliases={6: 0} if updated else {},
                scratch_shapes=[
                    pltpu.VMEM((each, rows, features), bf16),
                    pltpu.VMEM((head_features, features), output_type),
                    pltpu.SemaphoreType.DMA((each,)),
                ],
                compiler_params=params,
                name="finish",
            )(*operands)
        ]
    return updated[0]


def solution(mesh):
    return jax.shard_map(
        body,
        mesh=mesh,
        in_specs=(
            P("noise", "row", None),
            P("noise", "row", None),
            P("noise", "row", None),
            P("noise", "row", None),
            P("row", "noise", None),
            P(),
            P("noise", None),
            P(),
            P("noise", None),
            P("noise", None),
            P("noise", None),
            P("noise", "row"),
        ),
        out_specs=P("noise", "row", None),
        check_vma=False,
    )
```

profile of v0, /device:TPU:0, one launch (start us, length us, event | category | flops | bytes accessed | tf_op | source)
XLA Modules:
  0.0 45.7 jit_solution(7801091011982263947)
XLA Ops:
  0.0 2.8 %shift.1 = (bf16[4,64,768]{2,1,0:T(8,128)(2,1)}, bf16[4,64,768]{2,1,0:T(8,128)(2,1)}, bf16[96,768]{1,0:T(8,128)(2,1)}, bf16[96,384]{1,0:T(8,128)(2,1)}) custom-call(bf16[4,64,768]{2,1,0:T(8,128)(2,1)} %activations.3, bf16[4,64,768]{2,1,0:T(8,128)(2,1)} %scale_hbm.1, bf16[4,64,768]{2,1,0:T(8,128)(2,1)} %shift_hbm.1, s32[4,64]{1,0:T(4,128)} %mask_hbm.1, ...), custom_call_target="tpu_custom_call" | custom-call | tf_op jit(solution)/shard_map/shift/pallas_call | solution.py:419
  2.9 0.0 copy-start.2
  2.9 0.0 copy-start.6
  2.9 3.1 %collective-permute-start = (bf16[4,64,768]{2,1,0:T(8,128)(2,1)}, bf16[4,64,768]{2,1,0:T(8,128)(2,1)S(1)}, u32[]{:S(2)}, u32[]{:S(2)}) collective-permute-start(bf16[4,64,768]{2,1,0:T(8,128)(2,1)} %get-tuple-element.26.refs_0_), channel_id=1, source_target_pairs={{0,2},{1,3},{2,6},{3,7},{6,4},{7,5},{4,0},{5,1},{8,10},{9,11},{10,... | collective-permute-start | bytes 1179656 | tf_op jit(solution)/shard_map/ppermute | solution.py:382
  6.0 1.5 %collective-permute-start.1 = (bf16[96,768]{1,0:T(8,128)(2,1)}, bf16[96,768]{1,0:T(8,128)(2,1)S(1)}, u32[]{:S(2)}, u32[]{:S(2)}) collective-permute-start(bf16[96,768]{1,0:T(8,128)(2,1)} %get-tuple-element.30), channel_id=1, source_target_pairs={{0,8},{8,0},{16,24},{24,16},{1,9},{9,1},{17,25},{25,17},{2,10},{10... | collective-permute-start | bytes 442376 | tf_op jit(solution)/shard_map/ppermute | solution.py:388
  7.4 1.5 %collective-permute-start.2 = (bf16[96,768]{1,0:T(8,128)(2,1)}, bf16[96,768]{1,0:T(8,128)(2,1)S(1)}, u32[]{:S(2)}, u32[]{:S(2)}) collective-permute-start(bf16[96,768]{1,0:T(8,128)(2,1)} %get-tuple-element.30), channel_id=1, source_target_pairs={{0,16},{8,24},{16,0},{24,8},{1,17},{9,25},{17,1},{25,9},{2,18},{10... | collective-permute-start | bytes 442376 | tf_op jit(solution)/shard_map/ppermute | solution.py:388
  9.0 0.5 %collective-permute-start.3 = (bf16[96,768]{1,0:T(8,128)(2,1)}, bf16[96,768]{1,0:T(8,128)(2,1)S(1)}, u32[]{:S(2)}, u32[]{:S(2)}) collective-permute-start(bf16[96,768]{1,0:T(8,128)(2,1)} %get-tuple-element.30), channel_id=1, source_target_pairs={{0,24},{8,16},{16,8},{24,0},{1,25},{9,17},{17,9},{25,1},{2,26},{10... | collective-permute-start | bytes 442376 | tf_op jit(solution)/shard_map/ppermute | solution.py:388
  9.4 1.5 %collective-permute-start.4 = (bf16[96,384]{1,0:T(8,128)(2,1)}, bf16[96,384]{1,0:T(8,128)(2,1)S(1)}, u32[]{:S(2)}, u32[]{:S(2)}) collective-permute-start(bf16[96,384]{1,0:T(8,128)(2,1)} %get-tuple-element.25), channel_id=1, source_target_pairs={{0,8},{8,0},{16,24},{24,16},{1,9},{9,1},{17,25},{25,17},{2,10},{10... | collective-permute-start | bytes 221192 | tf_op jit(solution)/shard_map/ppermute | solution.py:388
  10.9 0.0 copy-start.5
  10.9 4.6 %bias.1 = bf16[800,128]{1,0:T(8,128)(2,1)} custom-call(bf16[64,128,128]{2,1,0:T(8,128)(2,1)} %pair_hbm.1, bf16[192,384]{1,0:T(8,128)(2,1)} %value_hbm.1, bf16[8,128]{1,0:T(8,128)(2,1)} %bitcast.23), custom_call_target="tpu_custom_call" | custom-call | tf_op jit(solution)/shard_map/bias/pallas_call | solution.py:442
  15.5 0.0 copy-start.4
  15.5 0.7 %collective-permute-done.4 = bf16[96,384]{1,0:T(8,128)(2,1)S(1)} collective-permute-done((bf16[96,384]{1,0:T(8,128)(2,1)}, bf16[96,384]{1,0:T(8,128)(2,1)S(1)}, u32[]{:S(2)}, u32[]{:S(2)}) %collective-permute-start.4) | collective-permute-done | bytes 73760 | tf_op jit(solution)/shard_map/ppermute | solution.py:388
  16.2 0.0 collective-permute-done.1
  16.2 0.0 collective-permute-done.2
  16.2 0.2 collective-permute-done.3
  16.4 0.0 collective-permute-done.refs_1_
  16.4 0.0 copy-done.2
  16.4 0.0 copy-done.6
  16.4 0.1 pad_maximum_fusion.weights_mine
  16.5 0.0 copy-start.7
  16.5 0.0 copy-start.3
  16.5 0.1 collective-permute-start.7
  16.6 2.6 %collective-permute-start.13 = (bf16[4,64,768]{2,1,0:T(8,128)(2,1)S(1)}, bf16[4,64,768]{2,1,0:T(8,128)(2,1)S(1)}, u32[]{:S(2)}, u32[]{:S(2)}) collective-permute-start(bf16[4,64,768]{2,1,0:T(8,128)(2,1)S(1)} %collective-permute-done.refs_1_), channel_id=1, source_target_pairs={{0,2},{1,3},{2,6},{3,7},{6,4},{7,5},{4,0},{5,1},{8,10},{9,11},{10,... | collective-permute-start | bytes 1179656 | tf_op jit(solution)/shard_map/ppermute | solution.py:382
  19.2 0.0 copy-done.4
  19.2 2.3 %collective-permute-start.10 = (bf16[800,128]{1,0:T(8,128)(2,1)S(1)}, bf16[800,128]{1,0:T(8,128)(2,1)S(1)}, u32[]{:S(2)}, u32[]{:S(2)}) collective-permute-start(bf16[800,128]{1,0:T(8,128)(2,1)S(1)} %copy-done.4), channel_id=1, source_target_pairs={{0,24},{8,16},{16,8},{24,0},{1,25},{9,17},{17,9},{25,1},{2,26},{10... | collective-permute-start | bytes 614408 | tf_op jit(solution)/shard_map/ppermute | solution.py:388
  21.5 0.5 %collective-permute-start.8 = (bf16[800,128]{1,0:T(8,128)(2,1)S(1)}, bf16[800,128]{1,0:T(8,128)(2,1)S(1)}, u32[]{:S(2)}, u32[]{:S(2)}) collective-permute-start(bf16[800,128]{1,0:T(8,128)(2,1)S(1)} %copy-done.4), channel_id=1, source_target_pairs={{0,8},{8,0},{16,24},{24,16},{1,9},{9,1},{17,25},{25,17},{2,10},{10... | collective-permute-start | bytes 614408 | tf_op jit(solution)/shard_map/ppermute | solution.py:388
  22.1 0.6 %collective-permute-start.9 = (bf16[800,128]{1,0:T(8,128)(2,1)S(1)}, bf16[800,128]{1,0:T(8,128)(2,1)S(1)}, u32[]{:S(2)}, u32[]{:S(2)}) collective-permute-start(bf16[800,128]{1,0:T(8,128)(2,1)S(1)} %copy-done.4), channel_id=1, source_target_pairs={{0,16},{8,24},{16,0},{24,8},{1,17},{9,25},{17,1},{25,9},{2,18},{10... | collective-permute-start | bytes 614408 | tf_op jit(solution)/shard_map/ppermute | solution.py:388
  22.7 0.0 copy-done.5
  22.7 5.3 %collective-permute-done.10 = bf16[800,128]{1,0:T(8,128)(2,1)S(1)} collective-permute-done((bf16[800,128]{1,0:T(8,128)(2,1)S(1)}, bf16[800,128]{1,0:T(8,128)(2,1)S(1)}, u32[]{:S(2)}, u32[]{:S(2)}) %collective-permute-start.10) | collective-permute-done | bytes 204832 | tf_op jit(solution)/shard_map/ppermute | solution.py:388
  28.1 1.4 %collective-permute-start.5 = (bf16[2,96,384]{2,1,0:T(8,128)(2,1)S(1)}, bf16[2,96,384]{2,1,0:T(8,128)(2,1)S(1)}, u32[]{:S(2)}, u32[]{:S(2)}) collective-permute-start(bf16[2,96,384]{2,1,0:T(8,128)(2,1)S(1)} %pad_maximum_fusion.3), channel_id=1, source_target_pairs={{0,16},{8,24},{16,0},{24,8},{1,17},{9,25},{17,1},{25,9},{2,18},{10... | collective-permute-start | bytes 442376 | tf_op jit(solution)/shard_map/ppermute | solution.py:388
  29.5 0.0 collective-permute-done.13.refs_2_
  29.5 1.7 %collective-permute-start.14 = (bf16[4,64,768]{2,1,0:T(8,128)(2,1)S(1)}, bf16[4,64,768]{2,1,0:T(8,128)(2,1)S(1)}, u32[]{:S(2)}, u32[]{:S(2)}) collective-permute-start(bf16[4,64,768]{2,1,0:T(8,128)(2,1)S(1)} %collective-permute-done.13.refs_2_), channel_id=1, source_target_pairs={{0,2},{1,3},{2,6},{3,7},{6,4},{7,5},{4,0},{5,1},{8,10},{9,11},{10,... | collective-permute-start | bytes 1179656 | tf_op jit(solution)/shard_map/ppermute | solution.py:382
  31.1 0.5 %collective-permute-done.8 = bf16[800,128]{1,0:T(8,128)(2,1)S(1)} collective-permute-done((bf16[800,128]{1,0:T(8,128)(2,1)S(1)}, bf16[800,128]{1,0:T(8,128)(2,1)S(1)}, u32[]{:S(2)}, u32[]{:S(2)}) %collective-permute-start.8) | collective-permute-done | bytes 204832 | tf_op jit(solution)/shard_map/ppermute | solution.py:388
  31.6 0.1 collective-permute-done.9
  31.7 0.1 pad_maximum_fusion.1.parcel
  31.9 0.1 collective-permute-start.12
  32.0 0.6 %collective-permute-start.11 = (bf16[4,256,128]{2,1,0:T(8,128)(2,1)S(1)}, bf16[4,256,128]{2,1,0:T(8,128)(2,1)S(1)}, u32[]{:S(2)}, u32[]{:S(2)}) collective-permute-start(bf16[4,256,128]{2,1,0:T(8,128)(2,1)S(1)} %slice.8), channel_id=1, source_target_pairs={{0,1},{1,0},{2,3},{3,2},{4,5},{5,4},{6,7},{7,6},{8,9},{9,8},{10,11... | collective-permute-start | bytes 786440 | tf_op jit(solution)/shard_map/ppermute | solution.py:369
  32.5 2.3 %collective-permute-done.5 = bf16[2,96,384]{2,1,0:T(8,128)(2,1)S(1)} collective-permute-done((bf16[2,96,384]{2,1,0:T(8,128)(2,1)S(1)}, bf16[2,96,384]{2,1,0:T(8,128)(2,1)S(1)}, u32[]{:S(2)}, u32[]{:S(2)}) %collective-permute-start.5) | collective-permute-done | bytes 147488 | tf_op jit(solution)/shard_map/ppermute | solution.py:388
  34.8 0.1 collective-permute-start.6
  34.9 0.0 copy-done.7
  34.9 0.0 collective-permute-done.11.swapped
  35.0 0.0 collective-permute-done.12.swapped_value
  35.0 0.0 collective-permute-done.7.weights_other
  35.0 0.0 copy-done.3
  35.0 3.7 %early.1 = (f32[4,400,128]{2,1,0:T(8,128)S(1)}, bf16[4,128,384]{2,1,0:T(8,128)(2,1)S(1)}, bf16[768,384]{1,0:T(8,128)(2,1)S(1)}, bf16[384,768]{1,0:T(8,128)(2,1)S(1)}) custom-call(bf16[4,160,768]{2,1,0:T(8,128)(2,1)S(1)} %pad_maximum_fusion.weights_mine, bf16[4,160,768]{2,1,0:T(8,128)(2,1)S(1)} %collective-permute-done.7.weights_other, ...), custom_call_target="tpu_custom_call" | custom-call | tf_op jit(solution)/shard_map/early/pallas_call | solution.py:479
  38.7 1.9 %collective-permute-done.14.block = bf16[4,64,768]{2,1,0:T(8,128)(2,1)S(1)} collective-permute-done((bf16[4,64,768]{2,1,0:T(8,128)(2,1)S(1)}, bf16[4,64,768]{2,1,0:T(8,128)(2,1)S(1)}, u32[]{:S(2)}, u32[]{:S(2)}) %collective-permute-start.14) | collective-permute-done | bytes 393248 | tf_op jit(solution)/shard_map/ppermute | solution.py:382
  40.6 1.2 %late.3 = (f32[1,400,128]{2,1,0:T(8,128)S(1)}, f32[1,400,128]{2,1,0:T(8,128)S(1)}) custom-call(f32[4,400,128]{2,1,0:T(8,128)S(1)} %get-tuple-element.37.partial, bf16[4,128,384]{2,1,0:T(8,128)(2,1)S(1)} %get-tuple-element.38.queries, bf16[768,384]{1,0:T(8,128)(2,1)S(1)} %get-tuple-element.39.key_weight, bf16[384,768]{1,0:T(8,128)(2,1)S(1)} %get-tuple-element.40.value_weight, ...), custom_call_target="tpu_custom_call" | custom-call | tf_op jit(solution)/shard_map/late/pallas_call | solution.py:499
  41.7 0.0 copy-start
  41.8 0.0 copy-start.1
  41.8 0.1 collective-permute-start.16
  41.8 1.2 %late.2 = (f32[1,400,128]{2,1,0:T(8,128)S(1)}, f32[1,400,128]{2,1,0:T(8,128)S(1)}) custom-call(f32[4,400,128]{2,1,0:T(8,128)S(1)} %get-tuple-element.37.partial, bf16[4,128,384]{2,1,0:T(8,128)(2,1)S(1)} %get-tuple-element.38.queries, bf16[768,384]{1,0:T(8,128)(2,1)S(1)} %get-tuple-element.39.key_weight, bf16[384,768]{1,0:T(8,128)(2,1)S(1)} %get-tuple-element.40.value_weight, ...), custom_call_target="tpu_custom_call" | custom-call | tf_op jit(solution)/shard_map/late/pallas_call | solution.py:499
  43.0 0.6 %collective-permute-start.15 = (f32[1,400,128]{2,1,0:T(8,128)S(1)}, f32[1,400,128]{2,1,0:T(8,128)S(1)}, u32[]{:S(2)}, u32[]{:S(2)}) collective-permute-start(f32[1,400,128]{2,1,0:T(8,128)S(1)} %get-tuple-element.42), channel_id=1, source_target_pairs={{0,1},{1,0},{2,3},{3,2},{4,5},{5,4},{6,7},{7,6},{8,9},{9,8},{10,11... | collective-permute-start | bytes 614408 | tf_op jit(solution)/shard_map/ppermute | solution.py:369
  43.6 0.0 collective-permute-done.6.output_other
  43.6 0.0 collective-permute-done.16.got
  43.6 0.0 copy-done
  43.6 0.0 copy-done.1
  43.6 1.1 %finish.2.refs_0_ = bf16[4,64,768]{2,1,0:T(8,128)(2,1)} custom-call(bf16[4,96,384]{2,1,0:T(8,128)(2,1)S(1)} %pad_maximum_fusion.2.output_mine, bf16[4,96,384]{2,1,0:T(8,128)(2,1)S(1)} %collective-permute-done.6.output_other, bf16[4,64,768]{2,1,0:T(8,128)(2,1)S(1)} %copy-done, bf16[4,64,768]{2,1,0:T(8,128)(2,1)S(1)} %copy-done.1, ...), custom_call_target="tpu_custom_call" | custom-call | tf_op jit(solution)/shard_map/finish/pallas_call | solution.py:512
  44.7 0.0 collective-permute-done.15.got
  44.7 1.1 %finish.3 = bf16[4,64,768]{2,1,0:T(8,128)(2,1)} custom-call(bf16[4,96,384]{2,1,0:T(8,128)(2,1)S(1)} %pad_maximum_fusion.2.output_mine, bf16[4,96,384]{2,1,0:T(8,128)(2,1)S(1)} %collective-permute-done.6.output_other, bf16[4,64,768]{2,1,0:T(8,128)(2,1)S(1)} %copy-done, bf16[4,64,768]{2,1,0:T(8,128)(2,1)S(1)} %copy-done.1, ...), custom_call_target="tpu_custom_call", output_to_operand_aliasing={{}: (6, {})} | custom-call | tf_op jit(solution)/shard_map/finish/pallas_call | solution.py:512
  (5 shorter events, 0.1 us)
Async XLA Ops:
  2.9 13.5 %copy-start.2 = (bf16[4,64,768]{2,1,0:T(8,128)(2,1)S(1)}, bf16[4,64,768]{2,1,0:T(8,128)(2,1)}, u32[]{:S(2)}) copy-start(bf16[4,64,768]{2,1,0:T(8,128)(2,1)} %get-tuple-element.34.shifted) | copy-start | bytes 1179652
  2.9 13.5 %copy-start.6 = (bf16[96,768]{1,0:T(8,128)(2,1)S(1)}, bf16[96,768]{1,0:T(8,128)(2,1)}, u32[]{:S(2)}) copy-start(bf16[96,768]{1,0:T(8,128)(2,1)} %get-tuple-element.30) | copy-start | bytes 442372
  2.9 13.5 %collective-permute-start = (bf16[4,64,768]{2,1,0:T(8,128)(2,1)}, bf16[4,64,768]{2,1,0:T(8,128)(2,1)S(1)}, u32[]{:S(2)}, u32[]{:S(2)}) collective-permute-start(bf16[4,64,768]{2,1,0:T(8,128)(2,1)} %get-tuple-element.26.refs_0_), channel_id=1, source_target_pairs={{0,2},{1,3},{2,6},{3,7},{6,4},{7,5},{4,0},{5,1},{8,10},{9,11},{10,... | collective-permute-start | bytes 1179656 | tf_op jit(solution)/shard_map/ppermute | solution.py:382
  6.0 10.3 %collective-permute-start.1 = (bf16[96,768]{1,0:T(8,128)(2,1)}, bf16[96,768]{1,0:T(8,128)(2,1)S(1)}, u32[]{:S(2)}, u32[]{:S(2)}) collective-permute-start(bf16[96,768]{1,0:T(8,128)(2,1)} %get-tuple-element.30), channel_id=1, source_target_pairs={{0,8},{8,0},{16,24},{24,16},{1,9},{9,1},{17,25},{25,17},{2,10},{10... | collective-permute-start | bytes 442376 | tf_op jit(solution)/shard_map/ppermute | solution.py:388
  7.4 8.8 %collective-permute-start.2 = (bf16[96,768]{1,0:T(8,128)(2,1)}, bf16[96,768]{1,0:T(8,128)(2,1)S(1)}, u32[]{:S(2)}, u32[]{:S(2)}) collective-permute-start(bf16[96,768]{1,0:T(8,128)(2,1)} %get-tuple-element.30), channel_id=1, source_target_pairs={{0,16},{8,24},{16,0},{24,8},{1,17},{9,25},{17,1},{25,9},{2,18},{10... | collective-permute-start | bytes 442376 | tf_op jit(solution)/shard_map/ppermute | solution.py:388
  9.0 7.4 %collective-permute-start.3 = (bf16[96,768]{1,0:T(8,128)(2,1)}, bf16[96,768]{1,0:T(8,128)(2,1)S(1)}, u32[]{:S(2)}, u32[]{:S(2)}) collective-permute-start(bf16[96,768]{1,0:T(8,128)(2,1)} %get-tuple-element.30), channel_id=1, source_target_pairs={{0,24},{8,16},{16,8},{24,0},{1,25},{9,17},{17,9},{25,1},{2,26},{10... | collective-permute-start | bytes 442376 | tf_op jit(solution)/shard_map/ppermute | solution.py:388
  9.4 6.8 %collective-permute-start.4 = (bf16[96,384]{1,0:T(8,128)(2,1)}, bf16[96,384]{1,0:T(8,128)(2,1)S(1)}, u32[]{:S(2)}, u32[]{:S(2)}) collective-permute-start(bf16[96,384]{1,0:T(8,128)(2,1)} %get-tuple-element.25), channel_id=1, source_target_pairs={{0,8},{8,0},{16,24},{24,16},{1,9},{9,1},{17,25},{25,17},{2,10},{10... | collective-permute-start | bytes 221192 | tf_op jit(solution)/shard_map/ppermute | solution.py:388
  10.9 11.8 %copy-start.5 = (bf16[96,384]{1,0:T(8,128)(2,1)S(1)}, bf16[96,384]{1,0:T(8,128)(2,1)}, u32[]{:S(2)}) copy-start(bf16[96,384]{1,0:T(8,128)(2,1)} %get-tuple-element.25) | copy-start | bytes 221188
  15.5 3.7 %copy-start.4 = (bf16[800,128]{1,0:T(8,128)(2,1)S(1)}, bf16[800,128]{1,0:T(8,128)(2,1)}, u32[]{:S(2)}) copy-start(bf16[800,128]{1,0:T(8,128)(2,1)} %bias.1) | copy-start | bytes 614404
  16.5 18.5 %copy-start.7 = (bf16[384]{0:T(512)(128)(2,1)S(1)}, bf16[384]{0:T(512)(128)(2,1)}, u32[]{:S(2)}) copy-start(bf16[384]{0:T(512)(128)(2,1)} %param.19) | copy-start | bytes 2308
  16.5 18.5 %copy-start.3 = (bf16[4,64,768]{2,1,0:T(8,128)(2,1)S(1)}, bf16[4,64,768]{2,1,0:T(8,128)(2,1)}, u32[]{:S(2)}) copy-start(bf16[4,64,768]{2,1,0:T(8,128)(2,1)} %get-tuple-element.26.refs_0_) | copy-start | bytes 1179652
  16.5 18.5 %collective-permute-start.7 = (bf16[4,160,768]{2,1,0:T(8,128)(2,1)S(1)}, bf16[4,160,768]{2,1,0:T(8,128)(2,1)S(1)}, u32[]{:S(2)}, u32[]{:S(2)}) collective-permute-start(bf16[4,160,768]{2,1,0:T(8,128)(2,1)S(1)} %pad_maximum_fusion.weights_mine), channel_id=1, source_target_pairs={{0,1},{1,0},{2,3},{3,2},{4,5},{5,4},{6,7},{7,6},{8,9},{9,8},{10,11... | collective-permute-start | bytes 2949128 | tf_op jit(solution)/shard_map/ppermute | solution.py:369
  16.6 12.9 %collective-permute-start.13 = (bf16[4,64,768]{2,1,0:T(8,128)(2,1)S(1)}, bf16[4,64,768]{2,1,0:T(8,128)(2,1)S(1)}, u32[]{:S(2)}, u32[]{:S(2)}) collective-permute-start(bf16[4,64,768]{2,1,0:T(8,128)(2,1)S(1)} %collective-permute-done.refs_1_), channel_id=1, source_target_pairs={{0,2},{1,3},{2,6},{3,7},{6,4},{7,5},{4,0},{5,1},{8,10},{9,11},{10,... | collective-permute-start | bytes 1179656 | tf_op jit(solution)/shard_map/ppermute | solution.py:382
  19.2 8.9 %collective-permute-start.10 = (bf16[800,128]{1,0:T(8,128)(2,1)S(1)}, bf16[800,128]{1,0:T(8,128)(2,1)S(1)}, u32[]{:S(2)}, u32[]{:S(2)}) collective-permute-start(bf16[800,128]{1,0:T(8,128)(2,1)S(1)} %copy-done.4), channel_id=1, source_target_pairs={{0,24},{8,16},{16,8},{24,0},{1,25},{9,17},{17,9},{25,1},{2,26},{10... | collective-permute-start | bytes 614408 | tf_op jit(solution)/shard_map/ppermute | solution.py:388
  21.5 10.1 %collective-permute-start.8 = (bf16[800,128]{1,0:T(8,128)(2,1)S(1)}, bf16[800,128]{1,0:T(8,128)(2,1)S(1)}, u32[]{:S(2)}, u32[]{:S(2)}) collective-permute-start(bf16[800,128]{1,0:T(8,128)(2,1)S(1)} %copy-done.4), channel_id=1, source_target_pairs={{0,8},{8,0},{16,24},{24,16},{1,9},{9,1},{17,25},{25,17},{2,10},{10... | collective-permute-start | bytes 614408 | tf_op jit(solution)/shard_map/ppermute | solution.py:388
  22.1 9.7 %collective-permute-start.9 = (bf16[800,128]{1,0:T(8,128)(2,1)S(1)}, bf16[800,128]{1,0:T(8,128)(2,1)S(1)}, u32[]{:S(2)}, u32[]{:S(2)}) collective-permute-start(bf16[800,128]{1,0:T(8,128)(2,1)S(1)} %copy-done.4), channel_id=1, source_target_pairs={{0,16},{8,24},{16,0},{24,8},{1,17},{9,25},{17,1},{25,9},{2,18},{10... | collective-permute-start | bytes 614408 | tf_op jit(solution)/shard_map/ppermute | solution.py:388
  28.1 6.7 %collective-permute-start.5 = (bf16[2,96,384]{2,1,0:T(8,128)(2,1)S(1)}, bf16[2,96,384]{2,1,0:T(8,128)(2,1)S(1)}, u32[]{:S(2)}, u32[]{:S(2)}) collective-permute-start(bf16[2,96,384]{2,1,0:T(8,128)(2,1)S(1)} %pad_maximum_fusion.3), channel_id=1, source_target_pairs={{0,16},{8,24},{16,0},{24,8},{1,17},{9,25},{17,1},{25,9},{2,18},{10... | collective-permute-start | bytes 442376 | tf_op jit(solution)/shard_map/ppermute | solution.py:388
  29.5 11.1 %collective-permute-start.14 = (bf16[4,64,768]{2,1,0:T(8,128)(2,1)S(1)}, bf16[4,64,768]{2,1,0:T(8,128)(2,1)S(1)}, u32[]{:S(2)}, u32[]{:S(2)}) collective-permute-start(bf16[4,64,768]{2,1,0:T(8,128)(2,1)S(1)} %collective-permute-done.13.refs_2_), channel_id=1, source_target_pairs={{0,2},{1,3},{2,6},{3,7},{6,4},{7,5},{4,0},{5,1},{8,10},{9,11},{10,... | collective-permute-start | bytes 1179656 | tf_op jit(solution)/shard_map/ppermute | solution.py:382
  31.9 3.1 %collective-permute-start.12 = (bf16[4,288,128]{2,1,0:T(8,128)(2,1)S(1)}, bf16[4,288,128]{2,1,0:T(8,128)(2,1)S(1)}, u32[]{:S(2)}, u32[]{:S(2)}) collective-permute-start(bf16[4,288,128]{2,1,0:T(8,128)(2,1)S(1)} %slice.9), channel_id=1, source_target_pairs={{0,1},{1,0},{2,3},{3,2},{4,5},{5,4},{6,7},{7,6},{8,9},{9,8},{10,11... | collective-permute-start | bytes 884744 | tf_op jit(solution)/shard_map/ppermute | solution.py:369
  32.0 3.0 %collective-permute-start.11 = (bf16[4,256,128]{2,1,0:T(8,128)(2,1)S(1)}, bf16[4,256,128]{2,1,0:T(8,128)(2,1)S(1)}, u32[]{:S(2)}, u32[]{:S(2)}) collective-permute-start(bf16[4,256,128]{2,1,0:T(8,128)(2,1)S(1)} %slice.8), channel_id=1, source_target_pairs={{0,1},{1,0},{2,3},{3,2},{4,5},{5,4},{6,7},{7,6},{8,9},{9,8},{10,11... | collective-permute-start | bytes 786440 | tf_op jit(solution)/shard_map/ppermute | solution.py:369
  34.8 8.7 %collective-permute-start.6 = (bf16[4,96,384]{2,1,0:T(8,128)(2,1)S(1)}, bf16[4,96,384]{2,1,0:T(8,128)(2,1)S(1)}, u32[]{:S(2)}, u32[]{:S(2)}) collective-permute-start(bf16[4,96,384]{2,1,0:T(8,128)(2,1)S(1)} %pad_maximum_fusion.2.output_mine), channel_id=1, source_target_pairs={{0,1},{1,0},{2,3},{3,2},{4,5},{5,4},{6,7},{7,6},{8,9},{9,8},{10,11... | collective-permute-start | bytes 884744 | tf_op jit(solution)/shard_map/ppermute | solution.py:369
  41.7 1.9 %copy-start = (bf16[4,64,768]{2,1,0:T(8,128)(2,1)S(1)}, bf16[4,64,768]{2,1,0:T(8,128)(2,1)}, u32[]{:S(2)}) copy-start(bf16[4,64,768]{2,1,0:T(8,128)(2,1)} %activations.3) | copy-start | bytes 1179652
  41.8 1.9 %copy-start.1 = (bf16[4,64,768]{2,1,0:T(8,128)(2,1)S(1)}, bf16[4,64,768]{2,1,0:T(8,128)(2,1)}, u32[]{:S(2)}) copy-start(bf16[4,64,768]{2,1,0:T(8,128)(2,1)} %output_gate.3) | copy-start | bytes 1179652
  41.8 1.8 %collective-permute-start.16 = (f32[1,400,128]{2,1,0:T(8,128)S(1)}, f32[1,400,128]{2,1,0:T(8,128)S(1)}, u32[]{:S(2)}, u32[]{:S(2)}) collective-permute-start(f32[1,400,128]{2,1,0:T(8,128)S(1)} %get-tuple-element.44), channel_id=1, source_target_pairs={{0,1},{1,0},{2,3},{3,2},{4,5},{5,4},{6,7},{7,6},{8,9},{9,8},{10,11... | collective-permute-start | bytes 614408 | tf_op jit(solution)/shard_map/ppermute | solution.py:369
  43.0 1.6 %collective-permute-start.15 = (f32[1,400,128]{2,1,0:T(8,128)S(1)}, f32[1,400,128]{2,1,0:T(8,128)S(1)}, u32[]{:S(2)}, u32[]{:S(2)}) collective-permute-start(f32[1,400,128]{2,1,0:T(8,128)S(1)} %get-tuple-element.42), channel_id=1, source_target_pairs={{0,1},{1,0},{2,3},{3,2},{4,5},{5,4},{6,7},{7,6},{8,9},{9,8},{10,11... | collective-permute-start | bytes 614408 | tf_op jit(solution)/shard_map/ppermute | solution.py:369
where the time goes:
time: 45.9 us; the launch traced here: 45.7 us
  starting transfers between devices  18.6 us (41%)
  Pallas kernels  15.6 us (34%)
  waiting for transfers between devices  11 us (24%)
    ppermute x8, starting transfers between devices, from_noise(): lax.ppermute(array, 'noise', [(i, i ^ k) for i in range(lax.axis_size('no...  9.85 us
    ppermute x8, waiting for transfers between devices, from_noise(): lax.ppermute(array, 'noise', [(i, i ^ k) for i in range(lax.axis_size('no...  9.07 us
    ppermute x3, starting transfers between devices, next_chip(): return lax.ppermute(array, 'row', pairs)  7.38 us
    pallas_call x1, Pallas kernels, body(): pl.pallas_call(bias_kernel, in_specs=[in_hbm] * 3, out_shape=struct((tile...  4.57 us
    pallas_call x1, Pallas kernels, body(): pl.pallas_call(functools.partial(early_kernel, steps, heads), out_shape=[...  3.68 us
    pallas_call x1, Pallas kernels, body(): pl.pallas_call(shift_kernel, in_specs=[in_hbm] * 7, out_specs=[in_hbm] *...  2.84 us
    pallas_call x2, Pallas kernels, body(): pl.pallas_call(functools.partial(late_kernel, steps, heads, c * each), ou...  2.36 us
    pallas_call x2, Pallas kernels, body(): pl.pallas_call(functools.partial(finish_kernel, heads, c * each), in_spec...  2.1 us
  transfers between devices with their start and end apart: 17, of which 7 were waited for; matrix products, arithmetic and copies ran while one was open for 0% of the time, Pallas kernels for 26%

commit v1 on v0

--- a/solution.py
+++ b/solution.py
@@ -228,12 +228,11 @@
     return pick
 
 
-def early_kernel(steps, heads, weights_mine, weights_other, query_bias, shifted, parcel, swapped, swapped_value, *refs):
+def early_kernel(steps, heads, weights_mine, weights_other, query_bias, shifted, shifted_other, parcel, swapped, swapped_value, *refs):
     blocks = refs[: steps - 1]
     partial, queries, key_weight, value_weight, full, full_value, spread = refs[steps - 1 :]
     samples, rows, features = shifted.shape
-    noise_size = swapped_value.shape[0]
-    half = weights_mine.shape[1] - samples * rows // noise_size
+    noise_size, half, _ = weights_mine.shape
     breadth = key_weight.shape[1]
     width = breadth // heads
     core = lax.rem(lax.axis_index("row"), 2)
@@ -252,9 +251,9 @@
                 full_value[down, t * 128 : (t + 1) * 128] = value[k, at : at + half].astype(full.dtype)
     key_weight[...] = full[:, breadth : 2 * breadth].astype(jnp.bfloat16)
     value_weight[...] = full_value[...].astype(jnp.float32).T.astype(jnp.bfloat16)
-    for side, tokens in enumerate((shifted[...], weights_other[:, half:])):
+    for side, tokens in enumerate((shifted, shifted_other)):
         result = jnp.dot(
-            tokens.reshape(samples * rows, features),
+            tokens[...].reshape(samples * rows, features),
             full[:, 0:breadth].astype(jnp.bfloat16),
             preferred_element_type=jnp.float32,
         ) + query_bias[...].astype(jnp.float32)
@@ -435,7 +434,6 @@
 
     ring = [sent, next_chip(sent)]
     weights = [packed] + [from_noise(packed, k) for k in range(noise_size - 1, 0, -1)][::-1]
-    output_next = from_noise(output_columns, 1)
     head_weights, _ = after((bias_weight.T, packed))
     columns = pair_repr.shape[1]
     tile_rows = heads * rows
@@ -453,12 +451,14 @@
         compiler_params=pltpu.CompilerParams(vmem_limit_bytes=wide_bytes),
         name="bias",
     )(pair_repr, value_weight, head_weights)
-    ring[1], weights, parcel, output_next = after((ring[1], weights, parcel, output_next))
+    shifted_other = swap_cores(shifted)
+    ring[1], weights, parcel, shifted_other = after((ring[1], weights, parcel, shifted_other))
+    output_next = from_noise(output_columns, 1)
     ring.append(next_chip(ring[1]))
     output_mine = jnp.stack([output_columns, output_next])
-    tokens = shifted.reshape(noise_size, samples * rows // noise_size, features)
-    weights_mine = jnp.concatenate([jnp.stack(weights), tokens], axis=1)
+    weights_mine = jnp.stack(weights)
     weights_other = swap_cores(weights_mine)
+    parcel, _ = after((parcel, weights_mine))
     parcels = [from_noise(parcel, k) for k in range(noise_size)]
 
     for _ in range(steps - 3):
@@ -491,7 +491,7 @@
         ],
         compiler_params=params,
         name="early",
-    )(weights_mine, weights_other, bias_row, shifted, parcel_mine, swapped, swapped_value, *ring)
+    )(weights_mine, weights_other, bias_row, shifted, shifted_other, parcel_mine, swapped, swapped_value, *ring)
     keep, got = [], []
     chunks = 2
     each = samples // chunks

time: 45.9 us -> 45.6 us (level)
  other arithmetic: 0.23 us -> 1.17 us
  waiting for transfers between devices: 11 us -> 10.3 us
  starting transfers between devices: 18.6 us -> 18.1 us
    ppermute x3, waiting for transfers between devices: 1.88 us -> 0.01 us  [next_chip(): return lax.ppermute(array, 'row', pairs)]
    another operation x1, other arithmetic: 0.1 us -> 1.03 us  [body(): parcel_mine = jnp.stack(parcels)]
    ppermute x8, starting transfers between devices: 9.85 us -> 9.09 us  [from_noise(): lax.ppermute(array, 'noise', [(i, i ^ k) for i in range(lax.axis_size('no...]
    ppermute x6 -> x7, waiting for transfers between devices: 0.02 us -> 0.65 us  [swap_cores(): lax.ppermute(array, 'row', [(i, i ^ 1) for i in range(lax.axis_size('row'...]
    ppermute x8, waiting for transfers between devices: 9.07 us -> 9.65 us  [from_noise(): lax.ppermute(array, 'noise', [(i, i ^ k) for i in range(lax.axis_size('no...]
    ppermute x6 -> x7, starting transfers between devices: 1.41 us -> 1.35 us  [swap_cores(): lax.ppermute(array, 'row', [(i, i ^ 1) for i in range(lax.axis_size('row'...]
  transfers between devices with their start and end apart: 17 -> 18, of which waited for: 7 -> 6; matrix products, arithmetic and copies ran while one was open for 0% -> 3% of each run, Pallas kernels for 26% -> 26%
where the time goes in v1:
time: 45.6 us; the launch traced here: 45.4 us
  starting transfers between devices  18.1 us (40%)
  Pallas kernels  15.5 us (34%)
  waiting for transfers between devices  10.3 us (23%)
  other arithmetic  1.17 us (3%)
    ppermute x8, waiting for transfers between devices, from_noise(): lax.ppermute(array, 'noise', [(i, i ^ k) for i in range(lax.axis_size('no...  9.65 us
    ppermute x8, starting transfers between devices, from_noise(): lax.ppermute(array, 'noise', [(i, i ^ k) for i in range(lax.axis_size('no...  9.09 us
    ppermute x3, starting transfers between devices, next_chip(): return lax.ppermute(array, 'row', pairs)  7.69 us
    pallas_call x1, Pallas kernels, body(): pl.pallas_call(bias_kernel, in_specs=[in_hbm] * 3, out_shape=struct((tile...  4.54 us
    pallas_call x1, Pallas kernels, body(): pl.pallas_call(functools.partial(early_kernel, steps, heads), out_shape=[...  3.68 us
    pallas_call x1, Pallas kernels, body(): pl.pallas_call(shift_kernel, in_specs=[in_hbm] * 7, out_specs=[in_hbm] *...  2.84 us
    pallas_call x2, Pallas kernels, body(): pl.pallas_call(functools.partial(late_kernel, steps, heads, c * each), ou...  2.34 us
    pallas_call x2, Pallas kernels, body(): pl.pallas_call(functools.partial(finish_kernel, heads, c * each), in_spec...  2.08 us
  transfers between devices with their start and end apart: 18, of which 6 were waited for; matrix products, arithmetic and copies ran while one was open for 3% of the time, Pallas kernels for 26%

profile of v1, /device:TPU:0, one launch (start us, length us, event | category | flops | bytes accessed | tf_op | source)
XLA Modules:
  0.0 45.4 jit_solution(16484596636847410853)
XLA Ops:
  0.0 2.8 %shift.1 = (bf16[4,64,768]{2,1,0:T(8,128)(2,1)}, bf16[4,64,768]{2,1,0:T(8,128)(2,1)}, bf16[96,768]{1,0:T(8,128)(2,1)}, bf16[96,384]{1,0:T(8,128)(2,1)}) custom-call(bf16[4,64,768]{2,1,0:T(8,128)(2,1)} %activations.3, bf16[4,64,768]{2,1,0:T(8,128)(2,1)} %scale_hbm.1, bf16[4,64,768]{2,1,0:T(8,128)(2,1)} %shift_hbm.1, s32[4,64]{1,0:T(4,128)} %mask_hbm.1, ...), custom_call_target="tpu_custom_call" | custom-call | tf_op jit(solution)/shard_map/shift/pallas_call | solution.py:418
  2.9 0.0 copy-start.4
  2.9 0.0 copy-start.5
  2.9 3.1 %collective-permute-start.3 = (bf16[4,64,768]{2,1,0:T(8,128)(2,1)}, bf16[4,64,768]{2,1,0:T(8,128)(2,1)S(1)}, u32[]{:S(2)}, u32[]{:S(2)}) collective-permute-start(bf16[4,64,768]{2,1,0:T(8,128)(2,1)} %get-tuple-element.27.refs_0_), channel_id=1, source_target_pairs={{0,2},{1,3},{2,6},{3,7},{6,4},{7,5},{4,0},{5,1},{8,10},{9,11},{10,... | collective-permute-start | bytes 1179656 | tf_op jit(solution)/shard_map/ppermute | solution.py:381
  5.9 0.0 collective-permute-start.7
  6.0 1.5 %collective-permute-start.4 = (bf16[96,768]{1,0:T(8,128)(2,1)}, bf16[96,768]{1,0:T(8,128)(2,1)S(1)}, u32[]{:S(2)}, u32[]{:S(2)}) collective-permute-start(bf16[96,768]{1,0:T(8,128)(2,1)} %get-tuple-element.31), channel_id=1, source_target_pairs={{0,8},{8,0},{16,24},{24,16},{1,9},{9,1},{17,25},{25,17},{2,10},{10... | collective-permute-start | bytes 442376 | tf_op jit(solution)/shard_map/ppermute | solution.py:387
  7.4 1.5 %collective-permute-start.5 = (bf16[96,768]{1,0:T(8,128)(2,1)}, bf16[96,768]{1,0:T(8,128)(2,1)S(1)}, u32[]{:S(2)}, u32[]{:S(2)}) collective-permute-start(bf16[96,768]{1,0:T(8,128)(2,1)} %get-tuple-element.31), channel_id=1, source_target_pairs={{0,16},{8,24},{16,0},{24,8},{1,17},{9,25},{17,1},{25,9},{2,18},{10... | collective-permute-start | bytes 442376 | tf_op jit(solution)/shard_map/ppermute | solution.py:387
  9.0 0.5 %collective-permute-start.6 = (bf16[96,768]{1,0:T(8,128)(2,1)}, bf16[96,768]{1,0:T(8,128)(2,1)S(1)}, u32[]{:S(2)}, u32[]{:S(2)}) collective-permute-start(bf16[96,768]{1,0:T(8,128)(2,1)} %get-tuple-element.31), channel_id=1, source_target_pairs={{0,24},{8,16},{16,8},{24,0},{1,25},{9,17},{17,9},{25,1},{2,26},{10... | collective-permute-start | bytes 442376 | tf_op jit(solution)/shard_map/ppermute | solution.py:387
  9.4 4.5 %bias.1 = bf16[800,128]{1,0:T(8,128)(2,1)} custom-call(bf16[64,128,128]{2,1,0:T(8,128)(2,1)} %pair_hbm.1, bf16[192,384]{1,0:T(8,128)(2,1)} %value_hbm.1, bf16[8,128]{1,0:T(8,128)(2,1)} %bitcast.23), custom_call_target="tpu_custom_call" | custom-call | tf_op jit(solution)/shard_map/bias/pallas_call | solution.py:440
  14.0 0.0 collective-permute-done.4
  14.0 2.8 %collective-permute-done.5 = bf16[96,768]{1,0:T(8,128)(2,1)S(1)} collective-permute-done((bf16[96,768]{1,0:T(8,128)(2,1)}, bf16[96,768]{1,0:T(8,128)(2,1)S(1)}, u32[]{:S(2)}, u32[]{:S(2)}) %collective-permute-start.5) | collective-permute-done | bytes 147488 | tf_op jit(solution)/shard_map/ppermute | solution.py:387
  16.8 0.0 collective-permute-done.6
  16.8 0.0 collective-permute-done.3.refs_1_
  16.8 0.0 collective-permute-done.7.shifted_other
  16.8 2.6 %collective-permute-start.14 = (bf16[4,64,768]{2,1,0:T(8,128)(2,1)S(1)}, bf16[4,64,768]{2,1,0:T(8,128)(2,1)S(1)}, u32[]{:S(2)}, u32[]{:S(2)}) collective-permute-start(bf16[4,64,768]{2,1,0:T(8,128)(2,1)S(1)} %collective-permute-done.3.refs_1_), channel_id=1, source_target_pairs={{0,2},{1,3},{2,6},{3,7},{6,4},{7,5},{4,0},{5,1},{8,10},{9,11},{10,... | collective-permute-start | bytes 1179656 | tf_op jit(solution)/shard_map/ppermute | solution.py:381
  19.4 0.0 copy-done.4
  19.5 1.2 %collective-permute-start = (bf16[96,384]{1,0:T(8,128)(2,1)S(1)}, bf16[96,384]{1,0:T(8,128)(2,1)S(1)}, u32[]{:S(2)}, u32[]{:S(2)}) collective-permute-start(bf16[96,384]{1,0:T(8,128)(2,1)S(1)} %copy-done.4), channel_id=1, source_target_pairs={{0,8},{8,0},{16,24},{24,16},{1,9},{9,1},{17,25},{25,17},{2,10},{10... | collective-permute-start | bytes 221192 | tf_op jit(solution)/shard_map/ppermute | solution.py:387
  20.6 0.0 copy-done.5
  20.6 0.1 pad_maximum_fusion.1.weights_mine
  20.7 0.0 copy-start.6
  20.7 0.0 copy-start.2
  20.7 0.0 copy-start.3
  20.7 1.9 %collective-permute-start.11 = (bf16[800,128]{1,0:T(8,128)(2,1)}, bf16[800,128]{1,0:T(8,128)(2,1)S(1)}, u32[]{:S(2)}, u32[]{:S(2)}) collective-permute-start(bf16[800,128]{1,0:T(8,128)(2,1)} %bias.1), channel_id=1, source_target_pairs={{0,24},{8,16},{16,8},{24,0},{1,25},{9,17},{17,9},{25,1},{2,26},{10... | collective-permute-start | bytes 614408 | tf_op jit(solution)/shard_map/ppermute | solution.py:387
  22.6 0.5 %collective-permute-start.9 = (bf16[800,128]{1,0:T(8,128)(2,1)}, bf16[800,128]{1,0:T(8,128)(2,1)S(1)}, u32[]{:S(2)}, u32[]{:S(2)}) collective-permute-start(bf16[800,128]{1,0:T(8,128)(2,1)} %bias.1), channel_id=1, source_target_pairs={{0,8},{8,0},{16,24},{24,16},{1,9},{9,1},{17,25},{25,17},{2,10},{10... | collective-permute-start | bytes 614408 | tf_op jit(solution)/shard_map/ppermute | solution.py:387
  23.2 1.2 %collective-permute-start.10 = (bf16[800,128]{1,0:T(8,128)(2,1)}, bf16[800,128]{1,0:T(8,128)(2,1)S(1)}, u32[]{:S(2)}, u32[]{:S(2)}) collective-permute-start(bf16[800,128]{1,0:T(8,128)(2,1)} %bias.1), channel_id=1, source_target_pairs={{0,16},{8,24},{16,0},{24,8},{1,17},{9,25},{17,1},{25,9},{2,18},{10... | collective-permute-start | bytes 614408 | tf_op jit(solution)/shard_map/ppermute | solution.py:387
  24.3 0.3 collective-permute-done
  24.6 0.0 collective-permute-start.8
  24.6 5.4 %collective-permute-done.11 = bf16[800,128]{1,0:T(8,128)(2,1)S(1)} collective-permute-done((bf16[800,128]{1,0:T(8,128)(2,1)}, bf16[800,128]{1,0:T(8,128)(2,1)S(1)}, u32[]{:S(2)}, u32[]{:S(2)}) %collective-permute-start.11) | collective-permute-done | bytes 204832 | tf_op jit(solution)/shard_map/ppermute | solution.py:387
  30.0 0.9 %collective-permute-start.1 = (bf16[2,96,384]{2,1,0:T(8,128)(2,1)S(1)}, bf16[2,96,384]{2,1,0:T(8,128)(2,1)S(1)}, u32[]{:S(2)}, u32[]{:S(2)}) collective-permute-start(bf16[2,96,384]{2,1,0:T(8,128)(2,1)S(1)} %pad_maximum_fusion.3), channel_id=1, source_target_pairs={{0,16},{8,24},{16,0},{24,8},{1,17},{9,25},{17,1},{25,9},{2,18},{10... | collective-permute-start | bytes 442376 | tf_op jit(solution)/shard_map/ppermute | solution.py:387
  30.9 0.0 collective-permute-done.14.refs_2_
  30.9 2.0 %collective-permute-start.15 = (bf16[4,64,768]{2,1,0:T(8,128)(2,1)S(1)}, bf16[4,64,768]{2,1,0:T(8,128)(2,1)S(1)}, u32[]{:S(2)}, u32[]{:S(2)}) collective-permute-start(bf16[4,64,768]{2,1,0:T(8,128)(2,1)S(1)} %collective-permute-done.14.refs_2_), channel_id=1, source_target_pairs={{0,2},{1,3},{2,6},{3,7},{6,4},{7,5},{4,0},{5,1},{8,10},{9,11},{10,... | collective-permute-start | bytes 1179656 | tf_op jit(solution)/shard_map/ppermute | solution.py:381
  32.8 0.0 collective-permute-done.9
  32.8 0.6 %collective-permute-done.10 = bf16[800,128]{1,0:T(8,128)(2,1)S(1)} collective-permute-done((bf16[800,128]{1,0:T(8,128)(2,1)}, bf16[800,128]{1,0:T(8,128)(2,1)S(1)}, u32[]{:S(2)}, u32[]{:S(2)}) %collective-permute-start.10) | collective-permute-done | bytes 204832 | tf_op jit(solution)/shard_map/ppermute | solution.py:387
  33.4 1.0 %pad_maximum_fusion.parcel = bf16[4,800,128]{2,1,0:T(8,128)(2,1)S(1)} fusion(bf16[1,800,128]{2,1,0:T(8,128)(2,1)S(1)} %bitcast.16, bf16[1,800,128]{2,1,0:T(8,128)(2,1)S(1)} %bitcast.18, bf16[1,800,128]{2,1,0:T(8,128)(2,1)S(1)} %bitcast.17, bf16[1,800,128]{2,1,0:T(8,128)(2,1)} %bitcast.11), kind=kLoop, calls=%fused_computation | loop fusion | flops 1228800 | bytes 1638400 | tf_op jit(solution)/shard_map/stack | solution.py:467
  34.5 0.1 collective-permute-start.13
  34.6 0.6 %collective-permute-start.12 = (bf16[4,256,128]{2,1,0:T(8,128)(2,1)S(1)}, bf16[4,256,128]{2,1,0:T(8,128)(2,1)S(1)}, u32[]{:S(2)}, u32[]{:S(2)}) collective-permute-start(bf16[4,256,128]{2,1,0:T(8,128)(2,1)S(1)} %slice.8), channel_id=1, source_target_pairs={{0,1},{1,0},{2,3},{3,2},{4,5},{5,4},{6,7},{7,6},{8,9},{9,8},{10,11... | collective-permute-start | bytes 786440 | tf_op jit(solution)/shard_map/ppermute | solution.py:368
  35.1 0.6 %collective-permute-done.1 = bf16[2,96,384]{2,1,0:T(8,128)(2,1)S(1)} collective-permute-done((bf16[2,96,384]{2,1,0:T(8,128)(2,1)S(1)}, bf16[2,96,384]{2,1,0:T(8,128)(2,1)S(1)}, u32[]{:S(2)}, u32[]{:S(2)}) %collective-permute-start.1) | collective-permute-done | bytes 147488 | tf_op jit(solution)/shard_map/ppermute | solution.py:387
  35.8 0.1 collective-permute-start.2
  35.9 0.0 copy-done.6
  35.9 0.6 %collective-permute-done.12.swapped = bf16[4,256,128]{2,1,0:T(8,128)(2,1)S(1)} collective-permute-done((bf16[4,256,128]{2,1,0:T(8,128)(2,1)S(1)}, bf16[4,256,128]{2,1,0:T(8,128)(2,1)S(1)}, u32[]{:S(2)}, u32[]{:S(2)}) %collective-permute-start.12) | collective-permute-done | bytes 262176 | tf_op jit(solution)/shard_map/ppermute | solution.py:368
  36.5 0.0 collective-permute-done.13.swapped_value
  36.5 0.0 collective-permute-done.8.weights_other
  36.5 0.0 copy-done.2
  36.5 0.0 copy-done.3
  36.5 3.7 %early.1 = (f32[4,400,128]{2,1,0:T(8,128)S(1)}, bf16[4,128,384]{2,1,0:T(8,128)(2,1)S(1)}, bf16[768,384]{1,0:T(8,128)(2,1)S(1)}, bf16[384,768]{1,0:T(8,128)(2,1)S(1)}) custom-call(bf16[4,96,768]{2,1,0:T(8,128)(2,1)S(1)} %pad_maximum_fusion.1.weights_mine, bf16[4,96,768]{2,1,0:T(8,128)(2,1)S(1)} %collective-permute-done.8.weights_other, ...), custom_call_target="tpu_custom_call" | custom-call | tf_op jit(solution)/shard_map/early/pallas_call | solution.py:479
  40.2 0.0 collective-permute-done.15.block
  40.2 1.2 %late.3 = (f32[1,400,128]{2,1,0:T(8,128)S(1)}, f32[1,400,128]{2,1,0:T(8,128)S(1)}) custom-call(f32[4,400,128]{2,1,0:T(8,128)S(1)} %get-tuple-element.39.partial, bf16[4,128,384]{2,1,0:T(8,128)(2,1)S(1)} %get-tuple-element.40.queries, bf16[768,384]{1,0:T(8,128)(2,1)S(1)} %get-tuple-element.41.key_weight, bf16[384,768]{1,0:T(8,128)(2,1)S(1)} %get-tuple-element.42.value_weight, ...), custom_call_target="tpu_custom_call" | custom-call | tf_op jit(solution)/shard_map/late/pallas_call | solution.py:499
  41.4 0.0 copy-start
  41.4 0.0 copy-start.1
  41.4 0.2 collective-permute-start.17
  41.7 1.2 %late.2 = (f32[1,400,128]{2,1,0:T(8,128)S(1)}, f32[1,400,128]{2,1,0:T(8,128)S(1)}) custom-call(f32[4,400,128]{2,1,0:T(8,128)S(1)} %get-tuple-element.39.partial, bf16[4,128,384]{2,1,0:T(8,128)(2,1)S(1)} %get-tuple-element.40.queries, bf16[768,384]{1,0:T(8,128)(2,1)S(1)} %get-tuple-element.41.key_weight, bf16[384,768]{1,0:T(8,128)(2,1)S(1)} %get-tuple-element.42.value_weight, ...), custom_call_target="tpu_custom_call" | custom-call | tf_op jit(solution)/shard_map/late/pallas_call | solution.py:499
  42.8 0.4 collective-permute-start.16
  43.2 0.0 collective-permute-done.2.output_other
  43.2 0.0 collective-permute-done.17.got
  43.2 0.0 copy-done
  43.3 0.0 copy-done.1
  43.3 1.0 %finish.2.refs_0_ = bf16[4,64,768]{2,1,0:T(8,128)(2,1)} custom-call(bf16[4,96,384]{2,1,0:T(8,128)(2,1)S(1)} %pad_maximum_fusion.2.output_mine, bf16[4,96,384]{2,1,0:T(8,128)(2,1)S(1)} %collective-permute-done.2.output_other, bf16[4,64,768]{2,1,0:T(8,128)(2,1)S(1)} %copy-done, bf16[4,64,768]{2,1,0:T(8,128)(2,1)S(1)} %copy-done.1, ...), custom_call_target="tpu_custom_call" | custom-call | tf_op jit(solution)/shard_map/finish/pallas_call | solution.py:512
  44.3 0.0 collective-permute-done.16.got
  44.3 1.0 %finish.3 = bf16[4,64,768]{2,1,0:T(8,128)(2,1)} custom-call(bf16[4,96,384]{2,1,0:T(8,128)(2,1)S(1)} %pad_maximum_fusion.2.output_mine, bf16[4,96,384]{2,1,0:T(8,128)(2,1)S(1)} %collective-permute-done.2.output_other, bf16[4,64,768]{2,1,0:T(8,128)(2,1)S(1)} %copy-done, bf16[4,64,768]{2,1,0:T(8,128)(2,1)S(1)} %copy-done.1, ...), custom_call_target="tpu_custom_call", output_to_operand_aliasing={{}: (6, {})} | custom-call | tf_op jit(solution)/shard_map/finish/pallas_call | solution.py:512
  (5 shorter events, 0.1 us)
Async XLA Ops:
  2.9 16.6 %copy-start.4 = (bf16[96,384]{1,0:T(8,128)(2,1)S(1)}, bf16[96,384]{1,0:T(8,128)(2,1)}, u32[]{:S(2)}) copy-start(bf16[96,384]{1,0:T(8,128)(2,1)} %get-tuple-element.26) | copy-start | bytes 221188
  2.9 17.8 %copy-start.5 = (bf16[96,768]{1,0:T(8,128)(2,1)S(1)}, bf16[96,768]{1,0:T(8,128)(2,1)}, u32[]{:S(2)}) copy-start(bf16[96,768]{1,0:T(8,128)(2,1)} %get-tuple-element.31) | copy-start | bytes 442372
  2.9 13.9 %collective-permute-start.3 = (bf16[4,64,768]{2,1,0:T(8,128)(2,1)}, bf16[4,64,768]{2,1,0:T(8,128)(2,1)S(1)}, u32[]{:S(2)}, u32[]{:S(2)}) collective-permute-start(bf16[4,64,768]{2,1,0:T(8,128)(2,1)} %get-tuple-element.27.refs_0_), channel_id=1, source_target_pairs={{0,2},{1,3},{2,6},{3,7},{6,4},{7,5},{4,0},{5,1},{8,10},{9,11},{10,... | collective-permute-start | bytes 1179656 | tf_op jit(solution)/shard_map/ppermute | solution.py:381
  5.9 10.9 %collective-permute-start.7 = (bf16[4,64,768]{2,1,0:T(8,128)(2,1)}, bf16[4,64,768]{2,1,0:T(8,128)(2,1)S(1)}, u32[]{:S(2)}, u32[]{:S(2)}) collective-permute-start(bf16[4,64,768]{2,1,0:T(8,128)(2,1)} %get-tuple-element.30.shifted), channel_id=1, source_target_pairs={{0,1},{1,0},{2,3},{3,2},{4,5},{5,4},{6,7},{7,6},{8,9},{9,8},{10,11... | collective-permute-start | bytes 1179656 | tf_op jit(solution)/shard_map/ppermute | solution.py:368
  6.0 8.0 %collective-permute-start.4 = (bf16[96,768]{1,0:T(8,128)(2,1)}, bf16[96,768]{1,0:T(8,128)(2,1)S(1)}, u32[]{:S(2)}, u32[]{:S(2)}) collective-permute-start(bf16[96,768]{1,0:T(8,128)(2,1)} %get-tuple-element.31), channel_id=1, source_target_pairs={{0,8},{8,0},{16,24},{24,16},{1,9},{9,1},{17,25},{25,17},{2,10},{10... | collective-permute-start | bytes 442376 | tf_op jit(solution)/shard_map/ppermute | solution.py:387
  7.4 9.4 %collective-permute-start.5 = (bf16[96,768]{1,0:T(8,128)(2,1)}, bf16[96,768]{1,0:T(8,128)(2,1)S(1)}, u32[]{:S(2)}, u32[]{:S(2)}) collective-permute-start(bf16[96,768]{1,0:T(8,128)(2,1)} %get-tuple-element.31), channel_id=1, source_target_pairs={{0,16},{8,24},{16,0},{24,8},{1,17},{9,25},{17,1},{25,9},{2,18},{10... | collective-permute-start | bytes 442376 | tf_op jit(solution)/shard_map/ppermute | solution.py:387
  9.0 7.8 %collective-permute-start.6 = (bf16[96,768]{1,0:T(8,128)(2,1)}, bf16[96,768]{1,0:T(8,128)(2,1)S(1)}, u32[]{:S(2)}, u32[]{:S(2)}) collective-permute-start(bf16[96,768]{1,0:T(8,128)(2,1)} %get-tuple-element.31), channel_id=1, source_target_pairs={{0,24},{8,16},{16,8},{24,0},{1,25},{9,17},{17,9},{25,1},{2,26},{10... | collective-permute-start | bytes 442376 | tf_op jit(solution)/shard_map/ppermute | solution.py:387
  16.8 14.1 %collective-permute-start.14 = (bf16[4,64,768]{2,1,0:T(8,128)(2,1)S(1)}, bf16[4,64,768]{2,1,0:T(8,128)(2,1)S(1)}, u32[]{:S(2)}, u32[]{:S(2)}) collective-permute-start(bf16[4,64,768]{2,1,0:T(8,128)(2,1)S(1)} %collective-permute-done.3.refs_1_), channel_id=1, source_target_pairs={{0,2},{1,3},{2,6},{3,7},{6,4},{7,5},{4,0},{5,1},{8,10},{9,11},{10,... | collective-permute-start | bytes 1179656 | tf_op jit(solution)/shard_map/ppermute | solution.py:381
  19.5 5.1 %collective-permute-start = (bf16[96,384]{1,0:T(8,128)(2,1)S(1)}, bf16[96,384]{1,0:T(8,128)(2,1)S(1)}, u32[]{:S(2)}, u32[]{:S(2)}) collective-permute-start(bf16[96,384]{1,0:T(8,128)(2,1)S(1)} %copy-done.4), channel_id=1, source_target_pairs={{0,8},{8,0},{16,24},{24,16},{1,9},{9,1},{17,25},{25,17},{2,10},{10... | collective-permute-start | bytes 221192 | tf_op jit(solution)/shard_map/ppermute | solution.py:387
  20.7 15.2 %copy-start.6 = (bf16[384]{0:T(512)(128)(2,1)S(1)}, bf16[384]{0:T(512)(128)(2,1)}, u32[]{:S(2)}) copy-start(bf16[384]{0:T(512)(128)(2,1)} %param.19) | copy-start | bytes 2308
  20.7 15.8 %copy-start.2 = (bf16[4,64,768]{2,1,0:T(8,128)(2,1)S(1)}, bf16[4,64,768]{2,1,0:T(8,128)(2,1)}, u32[]{:S(2)}) copy-start(bf16[4,64,768]{2,1,0:T(8,128)(2,1)} %get-tuple-element.30.shifted) | copy-start | bytes 1179652
  20.7 15.8 %copy-start.3 = (bf16[4,64,768]{2,1,0:T(8,128)(2,1)S(1)}, bf16[4,64,768]{2,1,0:T(8,128)(2,1)}, u32[]{:S(2)}) copy-start(bf16[4,64,768]{2,1,0:T(8,128)(2,1)} %get-tuple-element.27.refs_0_) | copy-start | bytes 1179652
  20.7 9.2 %collective-permute-start.11 = (bf16[800,128]{1,0:T(8,128)(2,1)}, bf16[800,128]{1,0:T(8,128)(2,1)S(1)}, u32[]{:S(2)}, u32[]{:S(2)}) collective-permute-start(bf16[800,128]{1,0:T(8,128)(2,1)} %bias.1), channel_id=1, source_target_pairs={{0,24},{8,16},{16,8},{24,0},{1,25},{9,17},{17,9},{25,1},{2,26},{10... | collective-permute-start | bytes 614408 | tf_op jit(solution)/shard_map/ppermute | solution.py:387
  22.6 10.2 %collective-permute-start.9 = (bf16[800,128]{1,0:T(8,128)(2,1)}, bf16[800,128]{1,0:T(8,128)(2,1)S(1)}, u32[]{:S(2)}, u32[]{:S(2)}) collective-permute-start(bf16[800,128]{1,0:T(8,128)(2,1)} %bias.1), channel_id=1, source_target_pairs={{0,8},{8,0},{16,24},{24,16},{1,9},{9,1},{17,25},{25,17},{2,10},{10... | collective-permute-start | bytes 614408 | tf_op jit(solution)/shard_map/ppermute | solution.py:387
  23.2 10.3 %collective-permute-start.10 = (bf16[800,128]{1,0:T(8,128)(2,1)}, bf16[800,128]{1,0:T(8,128)(2,1)S(1)}, u32[]{:S(2)}, u32[]{:S(2)}) collective-permute-start(bf16[800,128]{1,0:T(8,128)(2,1)} %bias.1), channel_id=1, source_target_pairs={{0,16},{8,24},{16,0},{24,8},{1,17},{9,25},{17,1},{25,9},{2,18},{10... | collective-permute-start | bytes 614408 | tf_op jit(solution)/shard_map/ppermute | solution.py:387
  24.6 11.9 %collective-permute-start.8 = (bf16[4,96,768]{2,1,0:T(8,128)(2,1)S(1)}, bf16[4,96,768]{2,1,0:T(8,128)(2,1)S(1)}, u32[]{:S(2)}, u32[]{:S(2)}) collective-permute-start(bf16[4,96,768]{2,1,0:T(8,128)(2,1)S(1)} %pad_maximum_fusion.1.weights_mine), channel_id=1, source_target_pairs={{0,1},{1,0},{2,3},{3,2},{4,5},{5,4},{6,7},{7,6},{8,9},{9,8},{10,11... | collective-permute-start | bytes 1769480 | tf_op jit(solution)/shard_map/ppermute | solution.py:368
  30.0 5.8 %collective-permute-start.1 = (bf16[2,96,384]{2,1,0:T(8,128)(2,1)S(1)}, bf16[2,96,384]{2,1,0:T(8,128)(2,1)S(1)}, u32[]{:S(2)}, u32[]{:S(2)}) collective-permute-start(bf16[2,96,384]{2,1,0:T(8,128)(2,1)S(1)} %pad_maximum_fusion.3), channel_id=1, source_target_pairs={{0,16},{8,24},{16,0},{24,8},{1,17},{9,25},{17,1},{25,9},{2,18},{10... | collective-permute-start | bytes 442376 | tf_op jit(solution)/shard_map/ppermute | solution.py:387
  30.9 9.3 %collective-permute-start.15 = (bf16[4,64,768]{2,1,0:T(8,128)(2,1)S(1)}, bf16[4,64,768]{2,1,0:T(8,128)(2,1)S(1)}, u32[]{:S(2)}, u32[]{:S(2)}) collective-permute-start(bf16[4,64,768]{2,1,0:T(8,128)(2,1)S(1)} %collective-permute-done.14.refs_2_), channel_id=1, source_target_pairs={{0,2},{1,3},{2,6},{3,7},{6,4},{7,5},{4,0},{5,1},{8,10},{9,11},{10,... | collective-permute-start | bytes 1179656 | tf_op jit(solution)/shard_map/ppermute | solution.py:381
  34.5 2.0 %collective-permute-start.13 = (bf16[4,288,128]{2,1,0:T(8,128)(2,1)S(1)}, bf16[4,288,128]{2,1,0:T(8,128)(2,1)S(1)}, u32[]{:S(2)}, u32[]{:S(2)}) collective-permute-start(bf16[4,288,128]{2,1,0:T(8,128)(2,1)S(1)} %slice.9), channel_id=1, source_target_pairs={{0,1},{1,0},{2,3},{3,2},{4,5},{5,4},{6,7},{7,6},{8,9},{9,8},{10,11... | collective-permute-start | bytes 884744 | tf_op jit(solution)/shard_map/ppermute | solution.py:368
  34.6 1.9 %collective-permute-start.12 = (bf16[4,256,128]{2,1,0:T(8,128)(2,1)S(1)}, bf16[4,256,128]{2,1,0:T(8,128)(2,1)S(1)}, u32[]{:S(2)}, u32[]{:S(2)}) collective-permute-start(bf16[4,256,128]{2,1,0:T(8,128)(2,1)S(1)} %slice.8), channel_id=1, source_target_pairs={{0,1},{1,0},{2,3},{3,2},{4,5},{5,4},{6,7},{7,6},{8,9},{9,8},{10,11... | collective-permute-start | bytes 786440 | tf_op jit(solution)/shard_map/ppermute | solution.py:368
  35.8 7.4 %collective-permute-start.2 = (bf16[4,96,384]{2,1,0:T(8,128)(2,1)S(1)}, bf16[4,96,384]{2,1,0:T(8,128)(2,1)S(1)}, u32[]{:S(2)}, u32[]{:S(2)}) collective-permute-start(bf16[4,96,384]{2,1,0:T(8,128)(2,1)S(1)} %pad_maximum_fusion.2.output_mine), channel_id=1, source_target_pairs={{0,1},{1,0},{2,3},{3,2},{4,5},{5,4},{6,7},{7,6},{8,9},{9,8},{10,11... | collective-permute-start | bytes 884744 | tf_op jit(solution)/shard_map/ppermute | solution.py:368
  41.4 1.9 %copy-start = (bf16[4,64,768]{2,1,0:T(8,128)(2,1)S(1)}, bf16[4,64,768]{2,1,0:T(8,128)(2,1)}, u32[]{:S(2)}) copy-start(bf16[4,64,768]{2,1,0:T(8,128)(2,1)} %activations.3) | copy-start | bytes 1179652
  41.4 1.8 %copy-start.1 = (bf16[4,64,768]{2,1,0:T(8,128)(2,1)S(1)}, bf16[4,64,768]{2,1,0:T(8,128)(2,1)}, u32[]{:S(2)}) copy-start(bf16[4,64,768]{2,1,0:T(8,128)(2,1)} %output_gate.3) | copy-start | bytes 1179652
  41.4 1.8 %collective-permute-start.17 = (f32[1,400,128]{2,1,0:T(8,128)S(1)}, f32[1,400,128]{2,1,0:T(8,128)S(1)}, u32[]{:S(2)}, u32[]{:S(2)}) collective-permute-start(f32[1,400,128]{2,1,0:T(8,128)S(1)} %get-tuple-element.46), channel_id=1, source_target_pairs={{0,1},{1,0},{2,3},{3,2},{4,5},{5,4},{6,7},{7,6},{8,9},{9,8},{10,11... | collective-permute-start | bytes 614408 | tf_op jit(solution)/shard_map/ppermute | solution.py:368
  42.8 1.5 %collective-permute-start.16 = (f32[1,400,128]{2,1,0:T(8,128)S(1)}, f32[1,400,128]{2,1,0:T(8,128)S(1)}, u32[]{:S(2)}, u32[]{:S(2)}) collective-permute-start(f32[1,400,128]{2,1,0:T(8,128)S(1)} %get-tuple-element.44), channel_id=1, source_target_pairs={{0,1},{1,0},{2,3},{3,2},{4,5},{5,4},{6,7},{7,6},{8,9},{9,8},{10,11... | collective-permute-start | bytes 614408 | tf_op jit(solution)/shard_map/ppermute | solution.py:368

commit v2 on v1

--- a/solution.py
+++ b/solution.py
@@ -30,22 +30,18 @@
     mask_hbm,
     query_hbm,
     key_hbm,
-    output_hbm,
     shifted_hbm,
     sent_hbm,
     packed_hbm,
-    columns_hbm,
     shifted,
     sent,
     packed,
-    columns,
     activations,
     cond_scale,
     cond_shift,
     token_mask,
     query_weight,
     key_weight,
-    output_weight,
     sems,
     sems_out,
 ):
@@ -58,7 +54,6 @@
             copies.append(pltpu.make_async_copy(source.at[s], target.at[s], sems.at[1 + 3 * s + t]))
     copies.append(pltpu.make_async_copy(query_hbm, query_weight, sems.at[1 + 3 * samples]))
     copies.append(pltpu.make_async_copy(key_hbm, key_weight, sems.at[2 + 3 * samples]))
-    copies.append(pltpu.make_async_copy(output_hbm, output_weight, sems.at[3 + 3 * samples]))
     for copy in copies:
         copy.start()
     diagonal = lax.broadcasted_iota(jnp.int32, (rows, rows), 0) == lax.broadcasted_iota(
@@ -88,15 +83,13 @@
         ).astype(jnp.bfloat16)
     written.append(pltpu.make_async_copy(packed, packed_hbm, sems_out.at[2 * samples]))
     written[-1].start()
-    copies[-1].wait()
-    columns[...] = jnp.where(core == 0, output_weight[:, :breadth], output_weight[:, breadth:])
-    written.append(pltpu.make_async_copy(columns, columns_hbm, sems_out.at[2 * samples + 1]))
-    written[-1].start()
     for copy in written:
         copy.wait()
 
 
-def bias_kernel(pair_hbm, value_hbm, weights_hbm, parcel, pair, value_weight, weights, collected, sems):
+def bias_kernel(
+    pair_hbm, value_hbm, output_hbm, weights_hbm, parcel, pair, value_weight, output_weight, weights, collected, sems
+):
     rows, columns, channels = pair.shape
     heads = weights.shape[0]
     per, batches = 8, 2
@@ -106,6 +99,7 @@
         here = pl.ds(i * batch, batch)
         copies.append(pltpu.make_async_copy(pair_hbm.at[here], pair.at[here], sems.at[i]))
     copies.append(pltpu.make_async_copy(value_hbm, value_weight, sems.at[batches + 1]))
+    copies.append(pltpu.make_async_copy(output_hbm, output_weight, sems.at[batches + 2]))
     for copy in copies:
         copy.start()
     copies[0].wait()
@@ -147,13 +141,26 @@
         parcel[at : at + half, :] = jnp.concatenate(own, axis=1).astype(jnp.bfloat16)
         at += heads // 2 * half
         parcel[at : at + half, :] = jnp.concatenate(other[::-1], axis=1).astype(jnp.bfloat16)
+    copies[-2].wait()
     copies[-1].wait()
     depth, breadth = value_weight.shape
     whole = value_weight[...].astype(jnp.float32)
     kept = jnp.where(core == 0, whole[: depth // 2], whole[depth // 2 :]).astype(jnp.bfloat16)
-    for t in range(breadth // columns):
-        at = heads * half + t * (depth // 2)
-        parcel[at : at + depth // 2, :] = kept[:, t * columns : (t + 1) * columns]
+    beside = jnp.where(core == 0, output_weight[:, :breadth], output_weight[:, breadth:])
+    at = heads * half
+    for part in (kept, beside):
+        for t in range(breadth // columns):
+            parcel[at : at + depth // 2, :] = part[:, t * columns : (t + 1) * columns]
+            at += depth // 2
+
+
+def sort_kernel(*refs):
+    stacks = refs[-4:]
+    for k, parcel in enumerate(refs[:-4]):
+        at = 0
+        for stack in stacks:
+            stack[k] = parcel[at : at + stack.shape[1]]
+            at += stack.shape[1]
 
 
 def spread_queries(heads, queries, spread):
@@ -228,7 +235,7 @@
     return pick
 
 
-def early_kernel(steps, heads, weights_mine, weights_other, query_bias, shifted, shifted_other, parcel, swapped, swapped_value, *refs):
+def early_kernel(steps, heads, weights_mine, weights_other, query_bias, shifted, shifted_other, own_bias, swapped, own_value, swapped_value, *refs):
     blocks = refs[: steps - 1]
     partial, queries, key_weight, value_weight, full, full_value, spread = refs[steps - 1 :]
     samples, rows, features = shifted.shape
@@ -237,17 +244,13 @@
     width = breadth // heads
     core = lax.rem(lax.axis_index("row"), 2)
     place = lax.axis_index("noise")
-    below = parcel.shape[1] - breadth // 128 * half
-    for part, value, skipped, of_core in (
-        (weights_mine, parcel, below, core),
-        (weights_other, swapped_value, 0, 1 - core),
-    ):
+    for part, value, of_core in ((weights_mine, own_value, core), (weights_other, swapped_value, 1 - core)):
         for k in range(noise_size):
             start = ((place ^ k) * 2 + of_core) * half
             down = pl.ds(pl.multiple_of(start, math.gcd(half, 32)), half)
-            full[down, :] = part[k, 0:half].astype(full.dtype)
+            full[down, :] = part[k].astype(full.dtype)
             for t in range(breadth // 128):
-                at = skipped + t * half
+                at = t * half
                 full_value[down, t * 128 : (t + 1) * 128] = value[k, at : at + half].astype(full.dtype)
     key_weight[...] = full[:, breadth : 2 * breadth].astype(jnp.bfloat16)
     value_weight[...] = full_value[...].astype(jnp.float32).T.astype(jnp.bfloat16)
@@ -260,7 +263,7 @@
         queries[:, side * rows : (side + 1) * rows] = result.astype(jnp.bfloat16).reshape(
             samples, rows, breadth
         )
-    pick = bias_picker(parcel, swapped, steps, 0, rows)
+    pick = bias_picker(own_bias, swapped, steps, 0, rows)
     for s in range(samples):
         tokens = jnp.concatenate([block[s] for block in blocks], axis=0)
         keys = jnp.dot(tokens, key_weight[...], preferred_element_type=jnp.float32)
@@ -282,12 +285,12 @@
             partial[s, breadth + heads + h : breadth + heads + h + 1] = totals[h]
 
 
-def late_kernel(steps, heads, first, partial, queries, key_weight, value_weight, parcel, swapped, block, keep, give, merged, spread):
+def late_kernel(steps, heads, first, partial, queries, key_weight, value_weight, own_bias, swapped, block, keep, give, merged, spread):
     samples = merged.shape[0]
     rows = block.shape[1]
     breadth = key_weight.shape[1]
     width = breadth // heads
-    pick = bias_picker(parcel, swapped, steps, steps - 1, rows)
+    pick = bias_picker(own_bias, swapped, steps, steps - 1, rows)
     tokens = block[first : first + samples].reshape(samples * rows, block.shape[2])
     keys = jnp.dot(tokens, key_weight[...], preferred_element_type=jnp.float32)
     values = lax.dot_general(
@@ -322,19 +325,23 @@
         give[pair] = jnp.where(even, rights, lefts)
 
 
-def finish_kernel(heads, first, output_mine, output_other, activations, output_gate, keep, got, *refs):
+def finish_kernel(heads, first, own_output, swapped_output, activations, output_gate, keep, got, *refs):
     updated_hbm, updated, output_weight, sems = refs[-4:]
-    noise_size, part_rows, part_columns = output_mine.shape
+    noise_size, piece_rows, tile = swapped_output.shape
     breadth = output_weight.shape[0]
+    tiles = breadth // tile
+    part_rows = piece_rows // tiles
     width = breadth // heads
     samples, rows, _ = updated.shape
     core = lax.rem(lax.axis_index("row"), 2)
     place = lax.axis_index("noise")
     for k in range(noise_size):
         down = pl.ds(pl.multiple_of((place ^ k) * part_rows, math.gcd(part_rows, 32)), part_rows)
-        for part, of_core in ((output_mine, core), (output_other, 1 - core)):
-            along = pl.ds(pl.multiple_of(of_core * part_columns, 128), part_columns)
-            output_weight[down, along] = part[k].astype(output_weight.dtype)
+        for part, of_core in ((own_output, core), (swapped_output, 1 - core)):
+            for t in range(tiles):
+                along = pl.ds(pl.multiple_of((of_core * tiles + t) * tile, tile), tile)
+                at = t * part_rows
+                output_weight[down, along] = part[k, at : at + part_rows].astype(output_weight.dtype)
     writes = []
     for pair in range(samples // 2):
         own, other = keep.at[pair], got.at[pair]
@@ -414,62 +421,62 @@
     half = query_weight.shape[0] // 2
 
     in_hbm = pl.BlockSpec(memory_space=pltpu.HBM)
-    packed_shape, columns_shape = (half, 2 * head_features), (output_weight.shape[0], features // 2)
-    shifted, sent, packed, output_columns = pl.pallas_call(
+    packed_shape = (half, 2 * head_features)
+    shifted, sent, packed = pl.pallas_call(
         shift_kernel,
-        in_specs=[in_hbm] * 7,
-        out_specs=[in_hbm] * 4,
-        out_shape=[struct(activations.shape, bf16)] * 2
-        + [struct(packed_shape, bf16), struct(columns_shape, bf16)],
+        in_specs=[in_hbm] * 6,
+        out_specs=[in_hbm] * 3,
+        out_shape=[struct(activations.shape, bf16)] * 2 + [struct(packed_shape, bf16)],
         scratch_shapes=[pltpu.VMEM(activations.shape, bf16)] * 2
-        + [pltpu.VMEM(packed_shape, bf16), pltpu.VMEM(columns_shape, bf16)]
+        + [pltpu.VMEM(packed_shape, bf16)]
         + [pltpu.VMEM(activations.shape, bf16)] * 3
         + [pltpu.VMEM(token_mask.shape, jnp.int32)]
         + [pltpu.VMEM(query_weight.shape, bf16)] * 2
-        + [pltpu.VMEM(output_weight.shape, bf16)]
-        + [pltpu.SemaphoreType.DMA((3 * samples + 4,)), pltpu.SemaphoreType.DMA((2 * samples + 2,))],
+        + [pltpu.SemaphoreType.DMA((3 * samples + 3,)), pltpu.SemaphoreType.DMA((2 * samples + 1,))],
         compiler_params=pltpu.CompilerParams(vmem_limit_bytes=wide_bytes),
         name="shift",
-    )(activations, cond_scale, cond_shift, token_mask, query_weight, key_weight, output_weight)
+    )(activations, cond_scale, cond_shift, token_mask, query_weight, key_weight)
 
     ring = [sent, next_chip(sent)]
     weights = [packed] + [from_noise(packed, k) for k in range(noise_size - 1, 0, -1)][::-1]
     head_weights, _ = after((bias_weight.T, packed))
     columns = pair_repr.shape[1]
-    tile_rows = heads * rows
+    tile_rows, piece_rows = heads * rows, head_features // columns * half
+    assert output_weight.shape == (half, 2 * head_features)
     parcel = pl.pallas_call(
         bias_kernel,
-        in_specs=[in_hbm] * 3,
-        out_shape=struct((tile_rows + 3 * half, columns), bf16),
+        in_specs=[in_hbm] * 4,
+        out_shape=struct((tile_rows + 2 * piece_rows, columns), bf16),
         scratch_shapes=[
             pltpu.VMEM(pair_repr.shape, bf16),
             pltpu.VMEM(value_weight.shape, bf16),
+            pltpu.VMEM(output_weight.shape, bf16),
             pltpu.VMEM(head_weights.shape, bf16),
             pltpu.VMEM((rows * 2 * heads, columns), f32),
-            pltpu.SemaphoreType.DMA((4,)),
+            pltpu.SemaphoreType.DMA((5,)),
         ],
         compiler_params=pltpu.CompilerParams(vmem_limit_bytes=wide_bytes),
         name="bias",
-    )(pair_repr, value_weight, head_weights)
+    )(pair_repr, value_weight, output_weight, head_weights)
     shifted_other = swap_cores(shifted)
     ring[1], weights, parcel, shifted_other = after((ring[1], weights, parcel, shifted_other))
-    output_next = from_noise(output_columns, 1)
     ring.append(next_chip(ring[1]))
-    output_mine = jnp.stack([output_columns, output_next])
     weights_mine = jnp.stack(weights)
     weights_other = swap_cores(weights_mine)
-    parcel, _ = after((parcel, weights_mine))
     parcels = [from_noise(parcel, k) for k in range(noise_size)]
 
     for _ in range(steps - 3):
         ring.append(next_chip(ring[-1]))
     last = ring.pop()
-    parcel_mine = jnp.stack(parcels)
-    swapped = swap_cores(parcel_mine[:, tile_rows // 2 : tile_rows])
-    swapped_value = swap_cores(parcel_mine[:, tile_rows:])
-    for k in range(1, noise_size.bit_length() - 1):
-        output_mine = jnp.concatenate([output_mine, from_noise(output_mine, 2**k)], axis=0)
-    output_other = swap_cores(output_mine)
+    tile_shape, piece_shape = (noise_size, tile_rows // 2, columns), (noise_size, piece_rows, columns)
+    own_bias, other_bias, own_value, own_output = pl.pallas_call(
+        sort_kernel,
+        out_shape=[struct(shape, bf16) for shape in (tile_shape, tile_shape, piece_shape, piece_shape)],
+        compiler_params=params,
+        name="sort",
+    )(*parcels)
+    swapped = swap_cores(other_bias)
+    swapped_value = swap_cores(own_value)
 
     bias_row = query_bias.reshape(1, head_features)
     record = head_features + 2 * heads
@@ -491,7 +498,9 @@
         ],
         compiler_params=params,
         name="early",
-    )(weights_mine, weights_other, bias_row, shifted, shifted_other, parcel_mine, swapped, swapped_value, *ring)
+    )(weights_mine, weights_other, bias_row, shifted, shifted_other, own_bias, swapped, own_value, swapped_value, *ring)
+    then_output, _ = after((own_output, partial))
+    swapped_output = swap_cores(then_output)
     keep, got = [], []
     chunks = 2
     each = samples // chunks
@@ -502,12 +511,12 @@
             scratch_shapes=[pltpu.VMEM((each, record, 2 * rows), f32), spread],
             compiler_params=params,
             name="late",
-        )(partial, queries, key_full, value_full, parcel_mine, swapped, last)
+        )(partial, queries, key_full, value_full, own_bias, swapped, last)
         keep.append(kept)
         got.append(swap_cores(give))
     updated = []
     for c in range(chunks):
-        operands = [output_mine, output_other, activations, output_gate, keep[c], got[c], *updated]
+        operands = [own_output, swapped_output, activations, output_gate, keep[c], got[c], *updated]
         updated = [
             pl.pallas_call(
                 functools.partial(finish_kernel, heads, c * each),

time: 45.6 us -> 48.3 us (1.059)
  waiting for transfers between devices: 10.3 us -> 15.3 us
  starting transfers between devices: 18.1 us -> 15.9 us
  other arithmetic: 1.17 us -> 0.08 us
  local copies, waits for them, and re-layouts: 0.08 us -> 0.99 us
    ppermute x3, waiting for transfers between devices: 0.01 us -> 5.08 us  [next_chip(): return lax.ppermute(array, 'row', pairs)]
    ppermute x8 -> x6, starting transfers between devices: 9.09 us -> 7.04 us  [from_noise(): lax.ppermute(array, 'noise', [(i, i ^ k) for i in range(lax.axis_size('no...]
    ppermute x8 -> x6, waiting for transfers between devices: 9.65 us -> 8.56 us  [from_noise(): lax.ppermute(array, 'noise', [(i, i ^ k) for i in range(lax.axis_size('no...]
    another operation x2 -> x0, other arithmetic: 1.05 us -> none  [the longest x1 1.03 us: body(): parcel_mine = jnp.stack(parcels)]
    ppermute x7, waiting for transfers between devices: 0.65 us -> 1.66 us  [swap_cores(): lax.ppermute(array, 'row', [(i, i ^ 1) for i in range(lax.axis_size('row'...]
    unnamed x14, local copies, waits for them, and re-layouts: 0.04 us -> 0.98 us
    pallas_call x2 -> x3, Pallas kernels: 7.38 us -> 7.52 us  [the longest x1 4.66 us: body(): pl.pallas_call(bias_kernel, in_specs=[in_hbm] * 4, out_shape=struct((tile...]
  transfers between devices with their start and end apart: 18 -> 16, of which waited for: 6 -> 6; matrix products, arithmetic and copies ran while one was open for 3% -> 0% of each run, Pallas kernels for 26% -> 25%
where the time goes in v2:
time: 48.3 us; the launch traced here: 48.1 us
  starting transfers between devices  15.9 us (33%)
  Pallas kernels  15.7 us (33%)
  waiting for transfers between devices  15.3 us (32%)
  local copies, waits for them, and re-layouts  0.99 us (2%)
    ppermute x6, waiting for transfers between devices, from_noise(): lax.ppermute(array, 'noise', [(i, i ^ k) for i in range(lax.axis_size('no...  8.56 us
    ppermute x3, starting transfers between devices, next_chip(): return lax.ppermute(array, 'row', pairs)  7.41 us
    ppermute x6, starting transfers between devices, from_noise(): lax.ppermute(array, 'noise', [(i, i ^ k) for i in range(lax.axis_size('no...  7.04 us
    ppermute x3, waiting for transfers between devices, next_chip(): return lax.ppermute(array, 'row', pairs)  5.08 us
    pallas_call x1, Pallas kernels, body(): pl.pallas_call(bias_kernel, in_specs=[in_hbm] * 4, out_shape=struct((tile...  4.66 us
    pallas_call x1, Pallas kernels, body(): pl.pallas_call(functools.partial(early_kernel, steps, heads), out_shape=[...  3.67 us
    pallas_call x1, Pallas kernels, body(): pl.pallas_call(shift_kernel, in_specs=[in_hbm] * 6, out_specs=[in_hbm] *...  2.79 us
    pallas_call x2, Pallas kernels, body(): pl.pallas_call(functools.partial(late_kernel, steps, heads, c * each), ou...  2.34 us
  transfers between devices with their start and end apart: 16, of which 6 were waited for; matrix products, arithmetic and copies ran while one was open for 0% of the time, Pallas kernels for 25%

profile of v2, /device:TPU:0, one launch (start us, length us, event | category | flops | bytes accessed | tf_op | source)
XLA Modules:
  0.0 48.1 jit_solution(14153869583801198027)
XLA Ops:
  0.0 2.8 %shift.1 = (bf16[4,64,768]{2,1,0:T(8,128)(2,1)}, bf16[4,64,768]{2,1,0:T(8,128)(2,1)}, bf16[96,768]{1,0:T(8,128)(2,1)}) custom-call(bf16[4,64,768]{2,1,0:T(8,128)(2,1)} %activations.3, bf16[4,64,768]{2,1,0:T(8,128)(2,1)} %scale_hbm.1, bf16[4,64,768]{2,1,0:T(8,128)(2,1)} %shift_hbm.1, s32[4,64]{1,0:T(4,128)} %mask_hbm.1, bf16[192,384]{1,0:T(8,128)(2,1)} %query_hbm.1, ...), custom_call_target="tpu_custom_call" | custom-call | tf_op jit(solution)/shard_map/shift/pallas_call | solution.py:425
  2.8 0.0 copy-start.5
  2.8 3.1 %collective-permute-start = (bf16[4,64,768]{2,1,0:T(8,128)(2,1)}, bf16[4,64,768]{2,1,0:T(8,128)(2,1)S(1)}, u32[]{:S(2)}, u32[]{:S(2)}) collective-permute-start(bf16[4,64,768]{2,1,0:T(8,128)(2,1)} %get-tuple-element.29.refs_0_), channel_id=1, source_target_pairs={{0,2},{1,3},{2,6},{3,7},{6,4},{7,5},{4,0},{5,1},{8,10},{9,11},{10,... | collective-permute-start | bytes 1179656 | tf_op jit(solution)/shard_map/ppermute | solution.py:388
  5.9 0.0 collective-permute-start.4
  5.9 1.5 %collective-permute-start.1 = (bf16[96,768]{1,0:T(8,128)(2,1)}, bf16[96,768]{1,0:T(8,128)(2,1)S(1)}, u32[]{:S(2)}, u32[]{:S(2)}) collective-permute-start(bf16[96,768]{1,0:T(8,128)(2,1)} %get-tuple-element.35), channel_id=1, source_target_pairs={{0,8},{8,0},{16,24},{24,16},{1,9},{9,1},{17,25},{25,17},{2,10},{10... | collective-permute-start | bytes 442376 | tf_op jit(solution)/shard_map/ppermute | solution.py:394
  7.4 1.5 %collective-permute-start.2 = (bf16[96,768]{1,0:T(8,128)(2,1)}, bf16[96,768]{1,0:T(8,128)(2,1)S(1)}, u32[]{:S(2)}, u32[]{:S(2)}) collective-permute-start(bf16[96,768]{1,0:T(8,128)(2,1)} %get-tuple-element.35), channel_id=1, source_target_pairs={{0,16},{8,24},{16,0},{24,8},{1,17},{9,25},{17,1},{25,9},{2,18},{10... | collective-permute-start | bytes 442376 | tf_op jit(solution)/shard_map/ppermute | solution.py:394
  8.9 0.5 collective-permute-start.3
  9.4 0.0 copy-start.6
  9.4 0.0 copy-start.3
  9.4 0.0 copy-start.4
  9.4 4.7 %bias.1.refs_0_ = bf16[1088,128]{1,0:T(8,128)(2,1)} custom-call(bf16[64,128,128]{2,1,0:T(8,128)(2,1)} %pair_hbm.1, bf16[192,384]{1,0:T(8,128)(2,1)} %value_hbm.1, bf16[96,768]{1,0:T(8,128)(2,1)} %output_hbm.1, bf16[8,128]{1,0:T(8,128)(2,1)} %bitcast.9), custom_call_target="tpu_custom_call" | custom-call | tf_op jit(solution)/shard_map/bias/pallas_call | solution.py:446
  14.1 0.0 collective-permute-done.1
  14.1 2.7 %collective-permute-done.2 = bf16[96,768]{1,0:T(8,128)(2,1)S(1)} collective-permute-done((bf16[96,768]{1,0:T(8,128)(2,1)}, bf16[96,768]{1,0:T(8,128)(2,1)S(1)}, u32[]{:S(2)}, u32[]{:S(2)}) %collective-permute-start.2) | collective-permute-done | bytes 147488 | tf_op jit(solution)/shard_map/ppermute | solution.py:394
  16.7 0.0 collective-permute-done.3
  16.7 0.0 collective-permute-done.refs_1_
  16.7 0.0 collective-permute-done.4.shifted_other
  16.7 2.6 %collective-permute-start.11 = (bf16[4,64,768]{2,1,0:T(8,128)(2,1)S(1)}, bf16[4,64,768]{2,1,0:T(8,128)(2,1)S(1)}, u32[]{:S(2)}, u32[]{:S(2)}) collective-permute-start(bf16[4,64,768]{2,1,0:T(8,128)(2,1)S(1)} %collective-permute-done.refs_1_), channel_id=1, source_target_pairs={{0,2},{1,3},{2,6},{3,7},{6,4},{7,5},{4,0},{5,1},{8,10},{9,11},{10,... | collective-permute-start | bytes 1179656 | tf_op jit(solution)/shard_map/ppermute | solution.py:388
  19.4 0.0 copy-done.5
  19.4 0.1 pad_maximum_fusion.weights_mine
  19.5 0.1 collective-permute-start.8
  19.5 1.2 %collective-permute-start.5 = (bf16[1088,128]{1,0:T(8,128)(2,1)}, bf16[1088,128]{1,0:T(8,128)(2,1)S(1)}, u32[]{:S(2)}, u32[]{:S(2)}) collective-permute-start(bf16[1088,128]{1,0:T(8,128)(2,1)} %bias.1.refs_0_), channel_id=1, source_target_pairs={{0,8},{8,0},{16,24},{24,16},{1,9},{9,1},{17,25},{25,17},{2,10},{10... | collective-permute-start | bytes 835592 | tf_op jit(solution)/shard_map/ppermute | solution.py:394
  20.8 0.9 %collective-permute-start.6 = (bf16[1088,128]{1,0:T(8,128)(2,1)}, bf16[1088,128]{1,0:T(8,128)(2,1)S(1)}, u32[]{:S(2)}, u32[]{:S(2)}) collective-permute-start(bf16[1088,128]{1,0:T(8,128)(2,1)} %bias.1.refs_0_), channel_id=1, source_target_pairs={{0,16},{8,24},{16,0},{24,8},{1,17},{9,25},{17,1},{25,9},{2,18},{10... | collective-permute-start | bytes 835592 | tf_op jit(solution)/shard_map/ppermute | solution.py:394
  21.7 1.4 %collective-permute-start.7 = (bf16[1088,128]{1,0:T(8,128)(2,1)}, bf16[1088,128]{1,0:T(8,128)(2,1)S(1)}, u32[]{:S(2)}, u32[]{:S(2)}) collective-permute-start(bf16[1088,128]{1,0:T(8,128)(2,1)} %bias.1.refs_0_), channel_id=1, source_target_pairs={{0,24},{8,16},{16,8},{24,0},{1,25},{9,17},{17,9},{25,1},{2,26},{10... | collective-permute-start | bytes 835592 | tf_op jit(solution)/shard_map/ppermute | solution.py:394
  23.1 5.1 %collective-permute-done.11.refs_2_ = bf16[4,64,768]{2,1,0:T(8,128)(2,1)S(1)} collective-permute-done((bf16[4,64,768]{2,1,0:T(8,128)(2,1)S(1)}, bf16[4,64,768]{2,1,0:T(8,128)(2,1)S(1)}, u32[]{:S(2)}, u32[]{:S(2)}) %collective-permute-start.11) | collective-permute-done | bytes 393248 | tf_op jit(solution)/shard_map/ppermute | solution.py:388
  28.2 1.7 %collective-permute-start.13 = (bf16[4,64,768]{2,1,0:T(8,128)(2,1)S(1)}, bf16[4,64,768]{2,1,0:T(8,128)(2,1)S(1)}, u32[]{:S(2)}, u32[]{:S(2)}) collective-permute-start(bf16[4,64,768]{2,1,0:T(8,128)(2,1)S(1)} %collective-permute-done.11.refs_2_), channel_id=1, source_target_pairs={{0,2},{1,3},{2,6},{3,7},{6,4},{7,5},{4,0},{5,1},{8,10},{9,11},{10,... | collective-permute-start | bytes 1179656 | tf_op jit(solution)/shard_map/ppermute | solution.py:388
  29.9 0.0 collective-permute-done.5.refs_1_
  29.9 4.4 %collective-permute-done.6.refs_2_ = bf16[1088,128]{1,0:T(8,128)(2,1)S(1)} collective-permute-done((bf16[1088,128]{1,0:T(8,128)(2,1)}, bf16[1088,128]{1,0:T(8,128)(2,1)S(1)}, u32[]{:S(2)}, u32[]{:S(2)}) %collective-permute-start.6) | collective-permute-done | bytes 278560 | tf_op jit(solution)/shard_map/ppermute | solution.py:394
  34.2 1.5 %collective-permute-done.7.refs_3_ = bf16[1088,128]{1,0:T(8,128)(2,1)S(1)} collective-permute-done((bf16[1088,128]{1,0:T(8,128)(2,1)}, bf16[1088,128]{1,0:T(8,128)(2,1)S(1)}, u32[]{:S(2)}, u32[]{:S(2)}) %collective-permute-start.7) | collective-permute-done | bytes 278560 | tf_op jit(solution)/shard_map/ppermute | solution.py:394
  35.8 0.0 copy-start.2
  35.8 1.0 %copy-done.2 = bf16[1088,128]{1,0:T(8,128)(2,1)S(1)} copy-done((bf16[1088,128]{1,0:T(8,128)(2,1)S(1)}, bf16[1088,128]{1,0:T(8,128)(2,1)}, u32[]{:S(2)}) %copy-start.2) | copy-done | bytes 278552
  36.7 0.1 sort.1
  36.8 0.1 collective-permute-start.10
  36.9 0.5 %collective-permute-start.9 = (bf16[4,256,128]{2,1,0:T(8,128)(2,1)S(1)}, bf16[4,256,128]{2,1,0:T(8,128)(2,1)S(1)}, u32[]{:S(2)}, u32[]{:S(2)}) collective-permute-start(bf16[4,256,128]{2,1,0:T(8,128)(2,1)S(1)} %get-tuple-element.41), channel_id=1, source_target_pairs={{0,1},{1,0},{2,3},{3,2},{4,5},{5,4},{6,7},{7,6},{8,9},{9,8},{10,11... | collective-permute-start | bytes 786440 | tf_op jit(solution)/shard_map/ppermute | solution.py:375
  37.4 0.0 copy-done.6
  37.4 1.4 %collective-permute-done.9.swapped = bf16[4,256,128]{2,1,0:T(8,128)(2,1)S(1)} collective-permute-done((bf16[4,256,128]{2,1,0:T(8,128)(2,1)S(1)}, bf16[4,256,128]{2,1,0:T(8,128)(2,1)S(1)}, u32[]{:S(2)}, u32[]{:S(2)}) %collective-permute-start.9) | collective-permute-done | bytes 262176 | tf_op jit(solution)/shard_map/ppermute | solution.py:375
  38.8 0.0 collective-permute-done.10.swapped_value
  38.8 0.0 collective-permute-done.8.weights_other
  38.8 0.0 copy-done.3
  38.8 0.0 copy-done.4
  38.8 3.7 %early.1 = (f32[4,400,128]{2,1,0:T(8,128)S(1)}, bf16[4,128,384]{2,1,0:T(8,128)(2,1)S(1)}, bf16[768,384]{1,0:T(8,128)(2,1)S(1)}, bf16[384,768]{1,0:T(8,128)(2,1)S(1)}) custom-call(bf16[4,96,768]{2,1,0:T(8,128)(2,1)S(1)} %pad_maximum_fusion.weights_mine, bf16[4,96,768]{2,1,0:T(8,128)(2,1)S(1)} %collective-permute-done.8.weights_other, ...), custom_call_target="tpu_custom_call" | custom-call | tf_op jit(solution)/shard_map/early/pallas_call | solution.py:486
  42.5 0.2 collective-permute-start.12
  42.7 0.0 collective-permute-done.13.block
  42.7 1.2 %late.3 = (f32[1,400,128]{2,1,0:T(8,128)S(1)}, f32[1,400,128]{2,1,0:T(8,128)S(1)}) custom-call(f32[4,400,128]{2,1,0:T(8,128)S(1)} %get-tuple-element.44.partial, bf16[4,128,384]{2,1,0:T(8,128)(2,1)S(1)} %get-tuple-element.46.queries, bf16[768,384]{1,0:T(8,128)(2,1)S(1)} %get-tuple-element.47.key_weight, bf16[384,768]{1,0:T(8,128)(2,1)S(1)} %get-tuple-element.48.value_weight, ...), custom_call_target="tpu_custom_call" | custom-call | tf_op jit(solution)/shard_map/late/pallas_call | solution.py:508
  43.9 0.0 copy-start
  43.9 0.0 copy-start.1
  43.9 0.4 collective-permute-start.15
  44.4 1.2 %late.2 = (f32[1,400,128]{2,1,0:T(8,128)S(1)}, f32[1,400,128]{2,1,0:T(8,128)S(1)}) custom-call(f32[4,400,128]{2,1,0:T(8,128)S(1)} %get-tuple-element.44.partial, bf16[4,128,384]{2,1,0:T(8,128)(2,1)S(1)} %get-tuple-element.46.queries, bf16[768,384]{1,0:T(8,128)(2,1)S(1)} %get-tuple-element.47.key_weight, bf16[384,768]{1,0:T(8,128)(2,1)S(1)} %get-tuple-element.48.value_weight, ...), custom_call_target="tpu_custom_call" | custom-call | tf_op jit(solution)/shard_map/late/pallas_call | solution.py:508
  45.5 0.2 collective-permute-start.14
  45.7 0.0 collective-permute-done.12.swapped_output
  45.7 0.0 collective-permute-done.15.got
  45.7 0.0 copy-done
  45.7 0.0 copy-done.1
  45.8 1.1 %finish.2.refs_0_ = bf16[4,64,768]{2,1,0:T(8,128)(2,1)} custom-call(bf16[4,288,128]{2,1,0:T(8,128)(2,1)S(1)} %get-tuple-element.45.own_output, bf16[4,288,128]{2,1,0:T(8,128)(2,1)S(1)} %collective-permute-done.12.swapped_output, bf16[4,64,768]{2,1,0:T(8,128)(2,1)S(1)} %copy-done, bf16[4,64,768]{2,1,0:T(8,128)(2,1)S(1)} %copy-done.1, ...), custom_call_target="tpu_custom_call" | custom-call | tf_op jit(solution)/shard_map/finish/pallas_call | solution.py:521
  46.8 0.2 collective-permute-done.14.got
  47.1 1.1 %finish.3 = bf16[4,64,768]{2,1,0:T(8,128)(2,1)} custom-call(bf16[4,288,128]{2,1,0:T(8,128)(2,1)S(1)} %get-tuple-element.45.own_output, bf16[4,288,128]{2,1,0:T(8,128)(2,1)S(1)} %collective-permute-done.12.swapped_output, bf16[4,64,768]{2,1,0:T(8,128)(2,1)S(1)} %copy-done, bf16[4,64,768]{2,1,0:T(8,128)(2,1)S(1)} %copy-done.1, ...), custom_call_target="tpu_custom_call", output_to_operand_aliasing={{}: (6, {})} | custom-call | tf_op jit(solution)/shard_map/finish/pallas_call | solution.py:521
  (1 shorter events, 0.0 us)
Async XLA Ops:
  2.8 16.6 %copy-start.5 = (bf16[96,768]{1,0:T(8,128)(2,1)S(1)}, bf16[96,768]{1,0:T(8,128)(2,1)}, u32[]{:S(2)}) copy-start(bf16[96,768]{1,0:T(8,128)(2,1)} %get-tuple-element.35) | copy-start | bytes 442372
  2.8 13.9 %collective-permute-start = (bf16[4,64,768]{2,1,0:T(8,128)(2,1)}, bf16[4,64,768]{2,1,0:T(8,128)(2,1)S(1)}, u32[]{:S(2)}, u32[]{:S(2)}) collective-permute-start(bf16[4,64,768]{2,1,0:T(8,128)(2,1)} %get-tuple-element.29.refs_0_), channel_id=1, source_target_pairs={{0,2},{1,3},{2,6},{3,7},{6,4},{7,5},{4,0},{5,1},{8,10},{9,11},{10,... | collective-permute-start | bytes 1179656 | tf_op jit(solution)/shard_map/ppermute | solution.py:388
  5.9 10.9 %collective-permute-start.4 = (bf16[4,64,768]{2,1,0:T(8,128)(2,1)}, bf16[4,64,768]{2,1,0:T(8,128)(2,1)S(1)}, u32[]{:S(2)}, u32[]{:S(2)}) collective-permute-start(bf16[4,64,768]{2,1,0:T(8,128)(2,1)} %get-tuple-element.32.shifted), channel_id=1, source_target_pairs={{0,1},{1,0},{2,3},{3,2},{4,5},{5,4},{6,7},{7,6},{8,9},{9,8},{10,11... | collective-permute-start | bytes 1179656 | tf_op jit(solution)/shard_map/ppermute | solution.py:375
  5.9 8.2 %collective-permute-start.1 = (bf16[96,768]{1,0:T(8,128)(2,1)}, bf16[96,768]{1,0:T(8,128)(2,1)S(1)}, u32[]{:S(2)}, u32[]{:S(2)}) collective-permute-start(bf16[96,768]{1,0:T(8,128)(2,1)} %get-tuple-element.35), channel_id=1, source_target_pairs={{0,8},{8,0},{16,24},{24,16},{1,9},{9,1},{17,25},{25,17},{2,10},{10... | collective-permute-start | bytes 442376 | tf_op jit(solution)/shard_map/ppermute | solution.py:394
  7.4 9.4 %collective-permute-start.2 = (bf16[96,768]{1,0:T(8,128)(2,1)}, bf16[96,768]{1,0:T(8,128)(2,1)S(1)}, u32[]{:S(2)}, u32[]{:S(2)}) collective-permute-start(bf16[96,768]{1,0:T(8,128)(2,1)} %get-tuple-element.35), channel_id=1, source_target_pairs={{0,16},{8,24},{16,0},{24,8},{1,17},{9,25},{17,1},{25,9},{2,18},{10... | collective-permute-start | bytes 442376 | tf_op jit(solution)/shard_map/ppermute | solution.py:394
  8.9 7.8 %collective-permute-start.3 = (bf16[96,768]{1,0:T(8,128)(2,1)}, bf16[96,768]{1,0:T(8,128)(2,1)S(1)}, u32[]{:S(2)}, u32[]{:S(2)}) collective-permute-start(bf16[96,768]{1,0:T(8,128)(2,1)} %get-tuple-element.35), channel_id=1, source_target_pairs={{0,24},{8,16},{16,8},{24,0},{1,25},{9,17},{17,9},{25,1},{2,26},{10... | collective-permute-start | bytes 442376 | tf_op jit(solution)/shard_map/ppermute | solution.py:394
  9.4 28.0 %copy-start.6 = (bf16[384]{0:T(512)(128)(2,1)S(1)}, bf16[384]{0:T(512)(128)(2,1)}, u32[]{:S(2)}) copy-start(bf16[384]{0:T(512)(128)(2,1)} %param.19) | copy-start | bytes 2308
  9.4 29.4 %copy-start.3 = (bf16[4,64,768]{2,1,0:T(8,128)(2,1)S(1)}, bf16[4,64,768]{2,1,0:T(8,128)(2,1)}, u32[]{:S(2)}) copy-start(bf16[4,64,768]{2,1,0:T(8,128)(2,1)} %get-tuple-element.32.shifted) | copy-start | bytes 1179652
  9.4 29.4 %copy-start.4 = (bf16[4,64,768]{2,1,0:T(8,128)(2,1)S(1)}, bf16[4,64,768]{2,1,0:T(8,128)(2,1)}, u32[]{:S(2)}) copy-start(bf16[4,64,768]{2,1,0:T(8,128)(2,1)} %get-tuple-element.29.refs_0_) | copy-start | bytes 1179652
  16.7 11.4 %collective-permute-start.11 = (bf16[4,64,768]{2,1,0:T(8,128)(2,1)S(1)}, bf16[4,64,768]{2,1,0:T(8,128)(2,1)S(1)}, u32[]{:S(2)}, u32[]{:S(2)}) collective-permute-start(bf16[4,64,768]{2,1,0:T(8,128)(2,1)S(1)} %collective-permute-done.refs_1_), channel_id=1, source_target_pairs={{0,2},{1,3},{2,6},{3,7},{6,4},{7,5},{4,0},{5,1},{8,10},{9,11},{10,... | collective-permute-start | bytes 1179656 | tf_op jit(solution)/shard_map/ppermute | solution.py:388
  19.5 19.3 %collective-permute-start.8 = (bf16[4,96,768]{2,1,0:T(8,128)(2,1)S(1)}, bf16[4,96,768]{2,1,0:T(8,128)(2,1)S(1)}, u32[]{:S(2)}, u32[]{:S(2)}) collective-permute-start(bf16[4,96,768]{2,1,0:T(8,128)(2,1)S(1)} %pad_maximum_fusion.weights_mine), channel_id=1, source_target_pairs={{0,1},{1,0},{2,3},{3,2},{4,5},{5,4},{6,7},{7,6},{8,9},{9,8},{10,11... | collective-permute-start | bytes 1769480 | tf_op jit(solution)/shard_map/ppermute | solution.py:375
  19.5 10.3 %collective-permute-start.5 = (bf16[1088,128]{1,0:T(8,128)(2,1)}, bf16[1088,128]{1,0:T(8,128)(2,1)S(1)}, u32[]{:S(2)}, u32[]{:S(2)}) collective-permute-start(bf16[1088,128]{1,0:T(8,128)(2,1)} %bias.1.refs_0_), channel_id=1, source_target_pairs={{0,8},{8,0},{16,24},{24,16},{1,9},{9,1},{17,25},{25,17},{2,10},{10... | collective-permute-start | bytes 835592 | tf_op jit(solution)/shard_map/ppermute | solution.py:394
  20.8 13.4 %collective-permute-start.6 = (bf16[1088,128]{1,0:T(8,128)(2,1)}, bf16[1088,128]{1,0:T(8,128)(2,1)S(1)}, u32[]{:S(2)}, u32[]{:S(2)}) collective-permute-start(bf16[1088,128]{1,0:T(8,128)(2,1)} %bias.1.refs_0_), channel_id=1, source_target_pairs={{0,16},{8,24},{16,0},{24,8},{1,17},{9,25},{17,1},{25,9},{2,18},{10... | collective-permute-start | bytes 835592 | tf_op jit(solution)/shard_map/ppermute | solution.py:394
  21.7 14.1 %collective-permute-start.7 = (bf16[1088,128]{1,0:T(8,128)(2,1)}, bf16[1088,128]{1,0:T(8,128)(2,1)S(1)}, u32[]{:S(2)}, u32[]{:S(2)}) collective-permute-start(bf16[1088,128]{1,0:T(8,128)(2,1)} %bias.1.refs_0_), channel_id=1, source_target_pairs={{0,24},{8,16},{16,8},{24,0},{1,25},{9,17},{17,9},{25,1},{2,26},{10... | collective-permute-start | bytes 835592 | tf_op jit(solution)/shard_map/ppermute | solution.py:394
  28.2 14.5 %collective-permute-start.13 = (bf16[4,64,768]{2,1,0:T(8,128)(2,1)S(1)}, bf16[4,64,768]{2,1,0:T(8,128)(2,1)S(1)}, u32[]{:S(2)}, u32[]{:S(2)}) collective-permute-start(bf16[4,64,768]{2,1,0:T(8,128)(2,1)S(1)} %collective-permute-done.11.refs_2_), channel_id=1, source_target_pairs={{0,2},{1,3},{2,6},{3,7},{6,4},{7,5},{4,0},{5,1},{8,10},{9,11},{10,... | collective-permute-start | bytes 1179656 | tf_op jit(solution)/shard_map/ppermute | solution.py:388
  35.8 1.0 %copy-start.2 = (bf16[1088,128]{1,0:T(8,128)(2,1)S(1)}, bf16[1088,128]{1,0:T(8,128)(2,1)}, u32[]{:S(2)}) copy-start(bf16[1088,128]{1,0:T(8,128)(2,1)} %bias.1.refs_0_) | copy-start | bytes 835588
  36.8 2.0 %collective-permute-start.10 = (bf16[4,288,128]{2,1,0:T(8,128)(2,1)S(1)}, bf16[4,288,128]{2,1,0:T(8,128)(2,1)S(1)}, u32[]{:S(2)}, u32[]{:S(2)}) collective-permute-start(bf16[4,288,128]{2,1,0:T(8,128)(2,1)S(1)} %get-tuple-element.42.own_value), channel_id=1, source_target_pairs={{0,1},{1,0},{2,3},{3,2},{4,5},{5,4},{6,7},{7,6},{8,9},{9,8},{10,11... | collective-permute-start | bytes 884744 | tf_op jit(solution)/shard_map/ppermute | solution.py:375
  36.9 1.9 %collective-permute-start.9 = (bf16[4,256,128]{2,1,0:T(8,128)(2,1)S(1)}, bf16[4,256,128]{2,1,0:T(8,128)(2,1)S(1)}, u32[]{:S(2)}, u32[]{:S(2)}) collective-permute-start(bf16[4,256,128]{2,1,0:T(8,128)(2,1)S(1)} %get-tuple-element.41), channel_id=1, source_target_pairs={{0,1},{1,0},{2,3},{3,2},{4,5},{5,4},{6,7},{7,6},{8,9},{9,8},{10,11... | collective-permute-start | bytes 786440 | tf_op jit(solution)/shard_map/ppermute | solution.py:375
  42.5 3.2 %collective-permute-start.12 = (bf16[4,288,128]{2,1,0:T(8,128)(2,1)S(1)}, bf16[4,288,128]{2,1,0:T(8,128)(2,1)S(1)}, u32[]{:S(2)}, u32[]{:S(2)}) collective-permute-start(bf16[4,288,128]{2,1,0:T(8,128)(2,1)S(1)} %get-tuple-element.45.own_output), channel_id=1, source_target_pairs={{0,1},{1,0},{2,3},{3,2},{4,5},{5,4},{6,7},{7,6},{8,9},{9,8},{10,11... | collective-permute-start | bytes 884744 | tf_op jit(solution)/shard_map/ppermute | solution.py:375
  43.9 1.9 %copy-start = (bf16[4,64,768]{2,1,0:T(8,128)(2,1)S(1)}, bf16[4,64,768]{2,1,0:T(8,128)(2,1)}, u32[]{:S(2)}) copy-start(bf16[4,64,768]{2,1,0:T(8,128)(2,1)} %activations.3) | copy-start | bytes 1179652
  43.9 1.8 %copy-start.1 = (bf16[4,64,768]{2,1,0:T(8,128)(2,1)S(1)}, bf16[4,64,768]{2,1,0:T(8,128)(2,1)}, u32[]{:S(2)}) copy-start(bf16[4,64,768]{2,1,0:T(8,128)(2,1)} %output_gate.3) | copy-start | bytes 1179652
  43.9 1.8 %collective-permute-start.15 = (f32[1,400,128]{2,1,0:T(8,128)S(1)}, f32[1,400,128]{2,1,0:T(8,128)S(1)}, u32[]{:S(2)}, u32[]{:S(2)}) collective-permute-start(f32[1,400,128]{2,1,0:T(8,128)S(1)} %get-tuple-element.52), channel_id=1, source_target_pairs={{0,1},{1,0},{2,3},{3,2},{4,5},{5,4},{6,7},{7,6},{8,9},{9,8},{10,11... | collective-permute-start | bytes 614408 | tf_op jit(solution)/shard_map/ppermute | solution.py:375
  45.5 1.5 %collective-permute-start.14 = (f32[1,400,128]{2,1,0:T(8,128)S(1)}, f32[1,400,128]{2,1,0:T(8,128)S(1)}, u32[]{:S(2)}, u32[]{:S(2)}) collective-permute-start(f32[1,400,128]{2,1,0:T(8,128)S(1)} %get-tuple-element.50), channel_id=1, source_target_pairs={{0,1},{1,0},{2,3},{3,2},{4,5},{5,4},{6,7},{7,6},{8,9},{9,8},{10,11... | collective-permute-start | bytes 614408 | tf_op jit(solution)/shard_map/ppermute | solution.py:375

commit v3 on v2

--- a/solution.py
+++ b/solution.py
@@ -30,18 +30,21 @@
     mask_hbm,
     query_hbm,
     key_hbm,
+    output_hbm,
     shifted_hbm,
     sent_hbm,
     packed_hbm,
+    extended_hbm,
     shifted,
     sent,
-    packed,
+    extended,
     activations,
     cond_scale,
     cond_shift,
     token_mask,
     query_weight,
     key_weight,
+    output_weight,
     sems,
     sems_out,
 ):
@@ -54,6 +57,7 @@
             copies.append(pltpu.make_async_copy(source.at[s], target.at[s], sems.at[1 + 3 * s + t]))
     copies.append(pltpu.make_async_copy(query_hbm, query_weight, sems.at[1 + 3 * samples]))
     copies.append(pltpu.make_async_copy(key_hbm, key_weight, sems.at[2 + 3 * samples]))
+    copies.append(pltpu.make_async_copy(output_hbm, output_weight, sems.at[3 + 3 * samples]))
     for copy in copies:
         copy.start()
     diagonal = lax.broadcasted_iota(jnp.int32, (rows, rows), 0) == lax.broadcasted_iota(
@@ -74,21 +78,31 @@
             written.append(pltpu.make_async_copy(source.at[s], target.at[s], sems_out.at[2 * s + t]))
             written[-1].start()
     core = lax.rem(lax.axis_index("row"), 2)
-    half, breadth = packed.shape[0], query_weight.shape[1]
+    half, breadth = packed_hbm.shape[0], query_weight.shape[1]
     for w, weight in enumerate((query_weight, key_weight)):
         copies[1 + 3 * samples + w].wait()
         whole = weight[...].astype(jnp.float32)
-        packed[:, w * breadth : (w + 1) * breadth] = jnp.where(
+        extended[0:half, w * breadth : (w + 1) * breadth] = jnp.where(
             core == 0, whole[:half], whole[half:]
         ).astype(jnp.bfloat16)
-    written.append(pltpu.make_async_copy(packed, packed_hbm, sems_out.at[2 * samples]))
+    written.append(
+        pltpu.make_async_copy(
+            extended.at[0:half, 0 : 2 * breadth], packed_hbm, sems_out.at[2 * samples]
+        )
+    )
+    written[-1].start()
+    copies[-1].wait()
+    extended[:, 2 * breadth :] = jnp.where(
+        core == 0, output_weight[:, :breadth], output_weight[:, breadth:]
+    )
+    written.append(pltpu.make_async_copy(extended, extended_hbm, sems_out.at[2 * samples + 1]))
     written[-1].start()
     for copy in written:
         copy.wait()
 
 
 def bias_kernel(
-    pair_hbm, value_hbm, output_hbm, weights_hbm, parcel, pair, value_weight, output_weight, weights, collected, sems
+    pair_hbm, value_hbm, weights_hbm, parcel, pair, value_weight, weights, collected, sems
 ):
     rows, columns, channels = pair.shape
     heads = weights.shape[0]
@@ -99,7 +113,6 @@
         here = pl.ds(i * batch, batch)
         copies.append(pltpu.make_async_copy(pair_hbm.at[here], pair.at[here], sems.at[i]))
     copies.append(pltpu.make_async_copy(value_hbm, value_weight, sems.at[batches + 1]))
-    copies.append(pltpu.make_async_copy(output_hbm, output_weight, sems.at[batches + 2]))
     for copy in copies:
         copy.start()
     copies[0].wait()
@@ -141,26 +154,31 @@
         parcel[at : at + half, :] = jnp.concatenate(own, axis=1).astype(jnp.bfloat16)
         at += heads // 2 * half
         parcel[at : at + half, :] = jnp.concatenate(other[::-1], axis=1).astype(jnp.bfloat16)
-    copies[-2].wait()
     copies[-1].wait()
     depth, breadth = value_weight.shape
     whole = value_weight[...].astype(jnp.float32)
     kept = jnp.where(core == 0, whole[: depth // 2], whole[depth // 2 :]).astype(jnp.bfloat16)
-    beside = jnp.where(core == 0, output_weight[:, :breadth], output_weight[:, breadth:])
     at = heads * half
-    for part in (kept, beside):
-        for t in range(breadth // columns):
-            parcel[at : at + depth // 2, :] = part[:, t * columns : (t + 1) * columns]
-            at += depth // 2
+    for t in range(breadth // columns):
+        parcel[at : at + depth // 2, :] = kept[:, t * columns : (t + 1) * columns]
+        at += depth // 2
 
 
 def sort_kernel(*refs):
-    stacks = refs[-4:]
-    for k, parcel in enumerate(refs[:-4]):
+    stacks = refs[-3:]
+    for k, parcel in enumerate(refs[:-3]):
         at = 0
         for stack in stacks:
             stack[k] = parcel[at : at + stack.shape[1]]
             at += stack.shape[1]
+
+
+def stack_kernel(first, *refs):
+    stacks = [ref for ref in refs if len(ref.shape) == 3]
+    for k, part in enumerate(refs[: -len(stacks)]):
+        for t, stack in enumerate(stacks):
+            breadth = stack.shape[2]
+            stack[k] = part[:, (first + t) * breadth : (first + t + 1) * breadth]
 
 
 def spread_queries(heads, queries, spread):
@@ -235,20 +253,24 @@
     return pick
 
 
-def early_kernel(steps, heads, weights_mine, weights_other, query_bias, shifted, shifted_other, own_bias, swapped, own_value, swapped_value, *refs):
+def early_kernel(steps, heads, query_mine, key_mine, query_other, key_other, query_bias, shifted, shifted_other, own_bias, swapped, own_value, swapped_value, *refs):
     blocks = refs[: steps - 1]
     partial, queries, key_weight, value_weight, full, full_value, spread = refs[steps - 1 :]
     samples, rows, features = shifted.shape
-    noise_size, half, _ = weights_mine.shape
+    noise_size, half, _ = query_mine.shape
     breadth = key_weight.shape[1]
     width = breadth // heads
     core = lax.rem(lax.axis_index("row"), 2)
     place = lax.axis_index("noise")
-    for part, value, of_core in ((weights_mine, own_value, core), (weights_other, swapped_value, 1 - core)):
+    for query, key, value, of_core in (
+        (query_mine, key_mine, own_value, core),
+        (query_other, key_other, swapped_value, 1 - core),
+    ):
         for k in range(noise_size):
             start = ((place ^ k) * 2 + of_core) * half
             down = pl.ds(pl.multiple_of(start, math.gcd(half, 32)), half)
-            full[down, :] = part[k].astype(full.dtype)
+            full[down, 0:breadth] = query[k].astype(full.dtype)
+            full[down, breadth:] = key[k].astype(full.dtype)
             for t in range(breadth // 128):
                 at = t * half
                 full_value[down, t * 128 : (t + 1) * 128] = value[k, at : at + half].astype(full.dtype)
@@ -325,23 +347,22 @@
         give[pair] = jnp.where(even, rights, lefts)
 
 
-def finish_kernel(heads, first, own_output, swapped_output, activations, output_gate, keep, got, *refs):
+def finish_kernel(heads, first, groups, *refs):
+    own_output, swapped_output = refs[:groups], refs[groups : 2 * groups]
+    activations, output_gate, keep, got = refs[2 * groups : 2 * groups + 4]
     updated_hbm, updated, output_weight, sems = refs[-4:]
-    noise_size, piece_rows, tile = swapped_output.shape
+    _, part_rows, part_columns = own_output[0].shape
     breadth = output_weight.shape[0]
-    tiles = breadth // tile
-    part_rows = piece_rows // tiles
     width = breadth // heads
     samples, rows, _ = updated.shape
     core = lax.rem(lax.axis_index("row"), 2)
     place = lax.axis_index("noise")
-    for k in range(noise_size):
-        down = pl.ds(pl.multiple_of((place ^ k) * part_rows, math.gcd(part_rows, 32)), part_rows)
-        for part, of_core in ((own_output, core), (swapped_output, 1 - core)):
-            for t in range(tiles):
-                along = pl.ds(pl.multiple_of((of_core * tiles + t) * tile, tile), tile)
-                at = t * part_rows
-                output_weight[down, along] = part[k, at : at + part_rows].astype(output_weight.dtype)
+    for parts, of_core in ((own_output, core), (swapped_output, 1 - core)):
+        along = pl.ds(pl.multiple_of(of_core * part_columns, 128), part_columns)
+        ordered = [part.at[k] for part in parts for k in range(part.shape[0])]
+        for k, part in enumerate(ordered):
+            down = pl.ds(pl.multiple_of((place ^ k) * part_rows, math.gcd(part_rows, 32)), part_rows)
+            output_weight[down, along] = part[...].astype(output_weight.dtype)
     writes = []
     for pair in range(samples // 2):
         own, other = keep.at[pair], got.at[pair]
@@ -392,6 +413,17 @@
     if k == 0:
         return array
     return lax.ppermute(array, "noise", [(i, i ^ k) for i in range(lax.axis_size("noise"))])
+
+
+def from_all_noise(own, direct, breadth):
+    parts = [own] + [None] * (2 ** len(direct) - 1)
+    for k in range(1, len(parts)):
+        low = k & -k
+        if low == k:
+            parts[k] = direct[low.bit_length() - 1]
+        else:
+            parts[k] = from_noise(parts[k ^ low][:, :breadth], low)
+    return parts
 
 
 def body(
@@ -421,57 +453,73 @@
     half = query_weight.shape[0] // 2
 
     in_hbm = pl.BlockSpec(memory_space=pltpu.HBM)
-    packed_shape = (half, 2 * head_features)
-    shifted, sent, packed = pl.pallas_call(
+    packed_shape, extended_shape = (half, 2 * head_features), (half, 3 * head_features)
+    assert output_weight.shape == (half, 2 * head_features)
+    shifted, sent, packed, extended = pl.pallas_call(
         shift_kernel,
-        in_specs=[in_hbm] * 6,
-        out_specs=[in_hbm] * 3,
-        out_shape=[struct(activations.shape, bf16)] * 2 + [struct(packed_shape, bf16)],
+        in_specs=[in_hbm] * 7,
+        out_specs=[in_hbm] * 4,
+        out_shape=[struct(activations.shape, bf16)] * 2
+        + [struct(packed_shape, bf16), struct(extended_shape, bf16)],
         scratch_shapes=[pltpu.VMEM(activations.shape, bf16)] * 2
-        + [pltpu.VMEM(packed_shape, bf16)]
+        + [pltpu.VMEM(extended_shape, bf16)]
         + [pltpu.VMEM(activations.shape, bf16)] * 3
         + [pltpu.VMEM(token_mask.shape, jnp.int32)]
         + [pltpu.VMEM(query_weight.shape, bf16)] * 2
-        + [pltpu.SemaphoreType.DMA((3 * samples + 3,)), pltpu.SemaphoreType.DMA((2 * samples + 1,))],
+        + [pltpu.VMEM(output_weight.shape, bf16)]
+        + [pltpu.SemaphoreType.DMA((3 * samples + 4,)), pltpu.SemaphoreType.DMA((2 * samples + 2,))],
         compiler_params=pltpu.CompilerParams(vmem_limit_bytes=wide_bytes),
         name="shift",
-    )(activations, cond_scale, cond_shift, token_mask, query_weight, key_weight)
+    )(activations, cond_scale, cond_shift, token_mask, query_weight, key_weight, output_weight)
 
     ring = [sent, next_chip(sent)]
-    weights = [packed] + [from_noise(packed, k) for k in range(noise_size - 1, 0, -1)][::-1]
+    direct = [from_noise(extended, 1)] + [from_noise(packed, 2**k) for k in range(1, noise_size.bit_length() - 1)]
     head_weights, _ = after((bias_weight.T, packed))
     columns = pair_repr.shape[1]
     tile_rows, piece_rows = heads * rows, head_features // columns * half
     assert output_weight.shape == (half, 2 * head_features)
     parcel = pl.pallas_call(
         bias_kernel,
-        in_specs=[in_hbm] * 4,
-        out_shape=struct((tile_rows + 2 * piece_rows, columns), bf16),
+        in_specs=[in_hbm] * 3,
+        out_shape=struct((tile_rows + piece_rows, columns), bf16),
         scratch_shapes=[
             pltpu.VMEM(pair_repr.shape, bf16),
             pltpu.VMEM(value_weight.shape, bf16),
-            pltpu.VMEM(output_weight.shape, bf16),
             pltpu.VMEM(head_weights.shape, bf16),
             pltpu.VMEM((rows * 2 * heads, columns), f32),
-            pltpu.SemaphoreType.DMA((5,)),
+            pltpu.SemaphoreType.DMA((4,)),
         ],
         compiler_params=pltpu.CompilerParams(vmem_limit_bytes=wide_bytes),
         name="bias",
-    )(pair_repr, value_weight, output_weight, head_weights)
+    )(pair_repr, value_weight, head_weights)
     shifted_other = swap_cores(shifted)
-    ring[1], weights, parcel, shifted_other = after((ring[1], weights, parcel, shifted_other))
+    ring[1], direct, parcel, shifted_other = after((ring[1], direct, parcel, shifted_other))
     ring.append(next_chip(ring[1]))
-    weights_mine = jnp.stack(weights)
-    weights_other = swap_cores(weights_mine)
     parcels = [from_noise(parcel, k) for k in range(noise_size)]
+    weights = from_all_noise(extended, direct, 2 * head_features)
+    part_shape = (noise_size, half, head_features)
+    query_mine, key_mine = pl.pallas_call(
+        functools.partial(stack_kernel, 0),
+        out_shape=[struct(part_shape, bf16)] * 2,
+        compiler_params=params,
+        name="stack",
+    )(*weights)
+    query_other, key_other = swap_cores(query_mine), swap_cores(key_mine)
+    output_mine = pl.pallas_call(
+        functools.partial(stack_kernel, 2),
+        out_shape=struct((2, half, head_features), bf16),
+        compiler_params=params,
+        name="stack_output",
+    )(extended, direct[0])
+    output_mine, _ = after((output_mine, ring[2]))
 
     for _ in range(steps - 3):
         ring.append(next_chip(ring[-1]))
     last = ring.pop()
     tile_shape, piece_shape = (noise_size, tile_rows // 2, columns), (noise_size, piece_rows, columns)
-    own_bias, other_bias, own_value, own_output = pl.pallas_call(
+    own_bias, other_bias, own_value = pl.pallas_call(
         sort_kernel,
-        out_shape=[struct(shape, bf16) for shape in (tile_shape, tile_shape, piece_shape, piece_shape)],
+        out_shape=[struct(shape, bf16) for shape in (tile_shape, tile_shape, piece_shape)],
         compiler_params=params,
         name="sort",
     )(*parcels)
@@ -498,9 +546,13 @@
         ],
         compiler_params=params,
         name="early",
-    )(weights_mine, weights_other, bias_row, shifted, shifted_other, own_bias, swapped, own_value, swapped_value, *ring)
-    then_output, _ = after((own_output, partial))
-    swapped_output = swap_cores(then_output)
+    )(query_mine, key_mine, query_other, key_other, bias_row, shifted, shifted_other, own_bias, swapped, own_value, swapped_value, *ring)
+    own_output = [output_mine]
+    for k in range(1, noise_size.bit_length() - 1):
+        arrived = from_noise(own_output[0] if k == 1 else jnp.concatenate(own_output, axis=0), 2**k)
+        own_output.append(arrived)
+    own_output, _ = after((own_output, partial))
+    swapped_output = [swap_cores(part) for part in own_output]
     keep, got = [], []
     chunks = 2
     each = samples // chunks
@@ -516,14 +568,14 @@
         got.append(swap_cores(give))
     updated = []
     for c in range(chunks):
-        operands = [own_output, swapped_output, activations, output_gate, keep[c], got[c], *updated]
+        operands = [*own_output, *swapped_output, activations, output_gate, keep[c], got[c], *updated]
         updated = [
             pl.pallas_call(
-                functools.partial(finish_kernel, heads, c * each),
-                in_specs=[pl.BlockSpec(memory_space=pltpu.VMEM)] * 6 + [in_hbm] * len(updated),
+                functools.partial(finish_kernel, heads, c * each, len(own_output)),
+                in_specs=[pl.BlockSpec(memory_space=pltpu.VMEM)] * (2 * len(own_output) + 4) + [in_hbm] * len(updated),
                 out_specs=in_hbm,
                 out_shape=struct(activations.shape, bf16),
-                input_output_aliases={6: 0} if updated else {},
+                input_output_aliases={2 * len(own_output) + 4: 0} if updated else {},
                 scratch_shapes=[
                     pltpu.VMEM((each, rows, features), bf16),
                     pltpu.VMEM((head_features, features), output_type),

time: 48.3 us -> 45.6 us (0.944); the launches traced: 48.1 us -> 44.7 us
  waiting for transfers between devices: 15.3 us -> 12.5 us
  starting transfers between devices: 15.9 us -> 15.3 us
    ppermute x6 -> x7, waiting for transfers between devices: 8.56 us -> 3.45 us  [from_noise(): lax.ppermute(array, 'noise', [(i, i ^ k) for i in range(lax.axis_size('no...]
    ppermute x3, starting transfers between devices: 7.41 us -> 4.54 us  [next_chip(): return lax.ppermute(array, 'row', pairs)]
    ppermute x3, waiting for transfers between devices: 5.08 us -> 7.56 us  [next_chip(): return lax.ppermute(array, 'row', pairs)]
    ppermute x6 -> x7, starting transfers between devices: 7.04 us -> 8.96 us  [from_noise(): lax.ppermute(array, 'noise', [(i, i ^ k) for i in range(lax.axis_size('no...]
    ppermute x7 -> x9, starting transfers between devices: 1.48 us -> 1.79 us  [swap_cores(): lax.ppermute(array, 'row', [(i, i ^ 1) for i in range(lax.axis_size('row'...]
    ppermute x7 -> x9, waiting for transfers between devices: 1.66 us -> 1.53 us  [swap_cores(): lax.ppermute(array, 'row', [(i, i ^ 1) for i in range(lax.axis_size('row'...]
    pallas_call x4 -> x6, Pallas kernels: 9.62 us -> 9.69 us  [the longest x1 4.62 us: body(): pl.pallas_call(bias_kernel, in_specs=[in_hbm] * 3, out_shape=struct((tile...]
  transfers between devices with their start and end apart: 16 -> 19, of which waited for: 6 -> 9; matrix products, arithmetic and copies ran while one was open for 0% -> 0% of each run, Pallas kernels for 25% -> 26%
where the time goes in v3:
time: 45.6 us; the launch traced here: 44.7 us
  Pallas kernels  15.8 us (35%)
  starting transfers between devices  15.3 us (34%)
  waiting for transfers between devices  12.5 us (27%)
  local copies, waits for them, and re-layouts  0.96 us (2%)
    ppermute x7, starting transfers between devices, from_noise(): lax.ppermute(array, 'noise', [(i, i ^ k) for i in range(lax.axis_size('no...  8.96 us
    ppermute x3, waiting for transfers between devices, next_chip(): return lax.ppermute(array, 'row', pairs)  7.56 us
    pallas_call x1, Pallas kernels, body(): pl.pallas_call(bias_kernel, in_specs=[in_hbm] * 3, out_shape=struct((tile...  4.62 us
    ppermute x3, starting transfers between devices, next_chip(): return lax.ppermute(array, 'row', pairs)  4.54 us
    pallas_call x1, Pallas kernels, body(): pl.pallas_call(functools.partial(early_kernel, steps, heads), out_shape=[...  3.7 us
    ppermute x7, waiting for transfers between devices, from_noise(): lax.ppermute(array, 'noise', [(i, i ^ k) for i in range(lax.axis_size('no...  3.45 us
    pallas_call x1, Pallas kernels, body(): pl.pallas_call(shift_kernel, in_specs=[in_hbm] * 7, out_specs=[in_hbm] *...  2.9 us
    pallas_call x2, Pallas kernels, body(): pl.pallas_call(functools.partial(late_kernel, steps, heads, c * each), ou...  2.35 us
  transfers between devices with their start and end apart: 19, of which 9 were waited for; matrix products, arithmetic and copies ran while one was open for 0% of the time, Pallas kernels for 26%

profile of v3, /device:TPU:0, one launch (start us, length us, event | category | flops | bytes accessed | tf_op | source)
XLA Modules:
  0.0 44.7 jit_solution(4716220395506848538)
XLA Ops:
  0.0 2.9 %shift.1 = (bf16[4,64,768]{2,1,0:T(8,128)(2,1)}, bf16[4,64,768]{2,1,0:T(8,128)(2,1)}, bf16[96,768]{1,0:T(8,128)(2,1)}, bf16[96,1152]{1,0:T(8,128)(2,1)}) custom-call(bf16[4,64,768]{2,1,0:T(8,128)(2,1)} %refs_4_.3, bf16[4,64,768]{2,1,0:T(8,128)(2,1)} %scale_hbm.1, bf16[4,64,768]{2,1,0:T(8,128)(2,1)} %shift_hbm.1, s32[4,64]{1,0:T(4,128)} %mask_hbm.1, ...), custom_call_target="tpu_custom_call" | custom-call | tf_op jit(solution)/shard_map/shift/pallas_call | solution.py:458
  2.9 0.0 copy-start.2
  2.9 3.1 %collective-permute-start = (bf16[4,64,768]{2,1,0:T(8,128)(2,1)}, bf16[4,64,768]{2,1,0:T(8,128)(2,1)S(1)}, u32[]{:S(2)}, u32[]{:S(2)}) collective-permute-start(bf16[4,64,768]{2,1,0:T(8,128)(2,1)} %get-tuple-element.32.refs_0_), channel_id=1, source_target_pairs={{0,2},{1,3},{2,6},{3,7},{6,4},{7,5},{4,0},{5,1},{8,10},{9,11},{10,... | collective-permute-start | bytes 1179656 | tf_op jit(solution)/shard_map/ppermute | solution.py:409
  6.0 0.0 collective-permute-start.3
  6.0 1.5 %collective-permute-start.1 = (bf16[96,1152]{1,0:T(8,128)(2,1)}, bf16[96,1152]{1,0:T(8,128)(2,1)S(1)}, u32[]{:S(2)}, u32[]{:S(2)}) collective-permute-start(bf16[96,1152]{1,0:T(8,128)(2,1)} %get-tuple-element.31.refs_0_), channel_id=1, source_target_pairs={{0,8},{8,0},{16,24},{24,16},{1,9},{9,1},{17,25},{25,17},{2,10},{10... | collective-permute-start | bytes 663560 | tf_op jit(solution)/shard_map/ppermute | solution.py:415
  7.5 1.5 %collective-permute-start.2 = (bf16[96,768]{1,0:T(8,128)(2,1)}, bf16[96,768]{1,0:T(8,128)(2,1)S(1)}, u32[]{:S(2)}, u32[]{:S(2)}) collective-permute-start(bf16[96,768]{1,0:T(8,128)(2,1)} %get-tuple-element.33), channel_id=1, source_target_pairs={{0,16},{8,24},{16,0},{24,8},{1,17},{9,25},{17,1},{25,9},{2,18},{10... | collective-permute-start | bytes 442376 | tf_op jit(solution)/shard_map/ppermute | solution.py:415
  9.0 0.0 copy-start.6
  9.0 0.0 copy-start.4
  9.0 0.0 copy-start.5
  9.0 4.6 %bias.1.refs_0_ = bf16[800,128]{1,0:T(8,128)(2,1)} custom-call(bf16[64,128,128]{2,1,0:T(8,128)(2,1)} %pair_hbm.1, bf16[192,384]{1,0:T(8,128)(2,1)} %value_hbm.1, bf16[8,128]{1,0:T(8,128)(2,1)} %bitcast.1), custom_call_target="tpu_custom_call" | custom-call | tf_op jit(solution)/shard_map/bias/pallas_call | solution.py:481
  13.6 0.0 collective-permute-done.2.refs_2_
  13.7 0.4 collective-permute-done.1.refs_1_
  14.1 2.3 %collective-permute-done.refs_1_ = bf16[4,64,768]{2,1,0:T(8,128)(2,1)S(1)} collective-permute-done((bf16[4,64,768]{2,1,0:T(8,128)(2,1)}, bf16[4,64,768]{2,1,0:T(8,128)(2,1)S(1)}, u32[]{:S(2)}, u32[]{:S(2)}) %collective-permute-start) | collective-permute-done | bytes 393248 | tf_op jit(solution)/shard_map/ppermute | solution.py:409
  16.3 0.0 collective-permute-done.3.shifted_other
  16.3 0.9 %collective-permute-start.4 = (bf16[4,64,768]{2,1,0:T(8,128)(2,1)S(1)}, bf16[4,64,768]{2,1,0:T(8,128)(2,1)S(1)}, u32[]{:S(2)}, u32[]{:S(2)}) collective-permute-start(bf16[4,64,768]{2,1,0:T(8,128)(2,1)S(1)} %collective-permute-done.refs_1_), channel_id=1, source_target_pairs={{0,2},{1,3},{2,6},{3,7},{6,4},{7,5},{4,0},{5,1},{8,10},{9,11},{10,... | collective-permute-start | bytes 1179656 | tf_op jit(solution)/shard_map/ppermute | solution.py:409
  17.3 1.5 %collective-permute-start.6 = (bf16[96,768]{1,0:T(8,128)(2,1)S(1)}, bf16[96,768]{1,0:T(8,128)(2,1)S(1)}, u32[]{:S(2)}, u32[]{:S(2)}) collective-permute-start(bf16[96,768]{1,0:T(8,128)(2,1)S(1)} %collective-permute-done.2.refs_2_), channel_id=1, source_target_pairs={{0,8},{8,0},{16,24},{24,16},{1,9},{9,1},{17,25},{25,17},{2,10},{10... | collective-permute-start | bytes 442376 | tf_op jit(solution)/shard_map/ppermute | solution.py:415
  18.8 1.5 %collective-permute-start.11 = (bf16[800,128]{1,0:T(8,128)(2,1)}, bf16[800,128]{1,0:T(8,128)(2,1)S(1)}, u32[]{:S(2)}, u32[]{:S(2)}) collective-permute-start(bf16[800,128]{1,0:T(8,128)(2,1)} %bias.1.refs_0_), channel_id=1, source_target_pairs={{0,24},{8,16},{16,8},{24,0},{1,25},{9,17},{17,9},{25,1},{2,26},{10... | collective-permute-start | bytes 614408 | tf_op jit(solution)/shard_map/ppermute | solution.py:415
  20.3 0.5 %collective-permute-start.10 = (bf16[800,128]{1,0:T(8,128)(2,1)}, bf16[800,128]{1,0:T(8,128)(2,1)S(1)}, u32[]{:S(2)}, u32[]{:S(2)}) collective-permute-start(bf16[800,128]{1,0:T(8,128)(2,1)} %bias.1.refs_0_), channel_id=1, source_target_pairs={{0,16},{8,24},{16,0},{24,8},{1,17},{9,25},{17,1},{25,9},{2,18},{10... | collective-permute-start | bytes 614408 | tf_op jit(solution)/shard_map/ppermute | solution.py:415
  20.8 1.5 %collective-permute-start.9 = (bf16[800,128]{1,0:T(8,128)(2,1)}, bf16[800,128]{1,0:T(8,128)(2,1)S(1)}, u32[]{:S(2)}, u32[]{:S(2)}) collective-permute-start(bf16[800,128]{1,0:T(8,128)(2,1)} %bias.1.refs_0_), channel_id=1, source_target_pairs={{0,8},{8,0},{16,24},{24,16},{1,9},{9,1},{17,25},{25,17},{2,10},{10... | collective-permute-start | bytes 614408 | tf_op jit(solution)/shard_map/ppermute | solution.py:415
  22.3 5.3 %collective-permute-done.4.refs_2_ = bf16[4,64,768]{2,1,0:T(8,128)(2,1)S(1)} collective-permute-done((bf16[4,64,768]{2,1,0:T(8,128)(2,1)S(1)}, bf16[4,64,768]{2,1,0:T(8,128)(2,1)S(1)}, u32[]{:S(2)}, u32[]{:S(2)}) %collective-permute-start.4) | collective-permute-done | bytes 393248 | tf_op jit(solution)/shard_map/ppermute | solution.py:409
  27.5 0.5 %collective-permute-start.16 = (bf16[4,64,768]{2,1,0:T(8,128)(2,1)S(1)}, bf16[4,64,768]{2,1,0:T(8,128)(2,1)S(1)}, u32[]{:S(2)}, u32[]{:S(2)}) collective-permute-start(bf16[4,64,768]{2,1,0:T(8,128)(2,1)S(1)} %collective-permute-done.4.refs_2_), channel_id=1, source_target_pairs={{0,2},{1,3},{2,6},{3,7},{6,4},{7,5},{4,0},{5,1},{8,10},{9,11},{10,... | collective-permute-start | bytes 1179656 | tf_op jit(solution)/shard_map/ppermute | solution.py:409
  28.1 0.0 collective-permute-done.6.refs_3_
  28.1 0.0 copy-done.2
  28.1 0.1 stack.1
  28.1 0.1 collective-permute-start.7
  28.2 1.2 %collective-permute-done.11.refs_3_ = bf16[800,128]{1,0:T(8,128)(2,1)S(1)} collective-permute-done((bf16[800,128]{1,0:T(8,128)(2,1)}, bf16[800,128]{1,0:T(8,128)(2,1)S(1)}, u32[]{:S(2)}, u32[]{:S(2)}) %collective-permute-start.11) | collective-permute-done | bytes 204832 | tf_op jit(solution)/shard_map/ppermute | solution.py:415
  29.4 0.0 collective-permute-start.8
  29.4 0.6 %collective-permute-done.10.refs_2_ = bf16[800,128]{1,0:T(8,128)(2,1)S(1)} collective-permute-done((bf16[800,128]{1,0:T(8,128)(2,1)}, bf16[800,128]{1,0:T(8,128)(2,1)S(1)}, u32[]{:S(2)}, u32[]{:S(2)}) %collective-permute-start.10) | collective-permute-done | bytes 204832 | tf_op jit(solution)/shard_map/ppermute | solution.py:415
  30.0 1.2 %collective-permute-done.9.refs_1_ = bf16[800,128]{1,0:T(8,128)(2,1)S(1)} collective-permute-done((bf16[800,128]{1,0:T(8,128)(2,1)}, bf16[800,128]{1,0:T(8,128)(2,1)S(1)}, u32[]{:S(2)}, u32[]{:S(2)}) %collective-permute-start.9) | collective-permute-done | bytes 204832 | tf_op jit(solution)/shard_map/ppermute | solution.py:415
  31.2 0.0 copy-start.3
  31.2 0.9 %copy-done.3 = bf16[800,128]{1,0:T(8,128)(2,1)S(1)} copy-done((bf16[800,128]{1,0:T(8,128)(2,1)S(1)}, bf16[800,128]{1,0:T(8,128)(2,1)}, u32[]{:S(2)}) %copy-start.3) | copy-done | bytes 204824
  32.2 0.1 sort.1
  32.2 0.1 collective-permute-start.13
  32.3 0.5 %collective-permute-start.12 = (bf16[4,256,128]{2,1,0:T(8,128)(2,1)S(1)}, bf16[4,256,128]{2,1,0:T(8,128)(2,1)S(1)}, u32[]{:S(2)}, u32[]{:S(2)}) collective-permute-start(bf16[4,256,128]{2,1,0:T(8,128)(2,1)S(1)} %get-tuple-element.45), channel_id=1, source_target_pairs={{0,1},{1,0},{2,3},{3,2},{4,5},{5,4},{6,7},{7,6},{8,9},{9,8},{10,11... | collective-permute-start | bytes 786440 | tf_op jit(solution)/shard_map/ppermute | solution.py:396
  32.8 0.0 collective-permute-done.7.query_other
  32.8 1.0 %collective-permute-start.5 = (bf16[2,96,384]{2,1,0:T(8,128)(2,1)S(1)}, bf16[2,96,384]{2,1,0:T(8,128)(2,1)S(1)}, u32[]{:S(2)}, u32[]{:S(2)}) collective-permute-start(bf16[2,96,384]{2,1,0:T(8,128)(2,1)S(1)} %stack_output.1.refs_0_), channel_id=1, source_target_pairs={{0,16},{8,24},{16,0},{24,8},{1,17},{9,25},{17,1},{25,9},{2,18},{10... | collective-permute-start | bytes 442376 | tf_op jit(solution)/shard_map/ppermute | solution.py:415
  33.8 0.0 copy-done.6
  33.8 0.0 collective-permute-done.8.key_other
  33.8 0.4 collective-permute-done.12.swapped
  34.3 0.0 collective-permute-done.13.swapped_value
  34.3 0.0 copy-done.4
  34.3 0.0 copy-done.5
  34.3 3.7 %early.1 = (f32[4,400,128]{2,1,0:T(8,128)S(1)}, bf16[4,128,384]{2,1,0:T(8,128)(2,1)S(1)}, bf16[768,384]{1,0:T(8,128)(2,1)S(1)}, bf16[384,768]{1,0:T(8,128)(2,1)S(1)}) custom-call(bf16[4,96,384]{2,1,0:T(8,128)(2,1)S(1)} %get-tuple-element.40.query_mine, bf16[4,96,384]{2,1,0:T(8,128)(2,1)S(1)} %get-tuple-element.41.key_mine, ...), custom_call_target="tpu_custom_call" | custom-call | tf_op jit(solution)/shard_map/early/pallas_call | solution.py:534
  38.0 0.0 collective-permute-done.16.block
  38.0 1.2 %late.3 = (f32[1,400,128]{2,1,0:T(8,128)S(1)}, f32[1,400,128]{2,1,0:T(8,128)S(1)}) custom-call(f32[4,400,128]{2,1,0:T(8,128)S(1)} %get-tuple-element.47.partial, bf16[4,128,384]{2,1,0:T(8,128)(2,1)S(1)} %get-tuple-element.50.queries, bf16[768,384]{1,0:T(8,128)(2,1)S(1)} %get-tuple-element.51.key_weight, bf16[384,768]{1,0:T(8,128)(2,1)S(1)} %get-tuple-element.52.value_weight, ...), custom_call_target="tpu_custom_call" | custom-call | tf_op jit(solution)/shard_map/late/pallas_call | solution.py:560
  39.2 0.0 copy-start
  39.2 0.0 copy-start.1
  39.2 0.2 collective-permute-start.18
  39.4 1.2 %late.2 = (f32[1,400,128]{2,1,0:T(8,128)S(1)}, f32[1,400,128]{2,1,0:T(8,128)S(1)}) custom-call(f32[4,400,128]{2,1,0:T(8,128)S(1)} %get-tuple-element.47.partial, bf16[4,128,384]{2,1,0:T(8,128)(2,1)S(1)} %get-tuple-element.50.queries, bf16[768,384]{1,0:T(8,128)(2,1)S(1)} %get-tuple-element.51.key_weight, bf16[384,768]{1,0:T(8,128)(2,1)S(1)} %get-tuple-element.52.value_weight, ...), custom_call_target="tpu_custom_call" | custom-call | tf_op jit(solution)/shard_map/late/pallas_call | solution.py:560
  40.6 0.4 collective-permute-start.17
  41.0 0.0 collective-permute-done.5.refs_1_
  41.0 0.1 collective-permute-start.14
  41.1 0.4 collective-permute-start.15
  41.5 0.9 %collective-permute-done.14.refs_2_ = bf16[2,96,384]{2,1,0:T(8,128)(2,1)S(1)} collective-permute-done((bf16[2,96,384]{2,1,0:T(8,128)(2,1)S(1)}, bf16[2,96,384]{2,1,0:T(8,128)(2,1)S(1)}, u32[]{:S(2)}, u32[]{:S(2)}) %collective-permute-start.14) | collective-permute-done | bytes 147488 | tf_op jit(solution)/shard_map/ppermute | solution.py:396
  42.4 0.2 collective-permute-done.15.refs_3_
  42.6 0.0 collective-permute-done.18.refs_7_
  42.6 0.0 copy-done
  42.6 0.0 copy-done.1
  42.6 1.0 %finish.2.refs_8_ = bf16[4,64,768]{2,1,0:T(8,128)(2,1)} custom-call(bf16[2,96,384]{2,1,0:T(8,128)(2,1)S(1)} %stack_output.1.refs_0_, bf16[2,96,384]{2,1,0:T(8,128)(2,1)S(1)} %collective-permute-done.5.refs_1_, bf16[2,96,384]{2,1,0:T(8,128)(2,1)S(1)} %collective-permute-done.14.refs_2_, bf16[2,96,384]{2,1,0:T(8,128)(2,1)S(1)} %collective-permute-done.15.refs_3_, ...), custom_call_target="tpu_custom_call" | custom-call | tf_op jit(solution)/shard_map/finish/pallas_call | solution.py:573
  43.7 0.0 collective-permute-done.17.refs_7_
  43.7 1.1 %finish.3 = bf16[4,64,768]{2,1,0:T(8,128)(2,1)} custom-call(bf16[2,96,384]{2,1,0:T(8,128)(2,1)S(1)} %stack_output.1.refs_0_, bf16[2,96,384]{2,1,0:T(8,128)(2,1)S(1)} %collective-permute-done.5.refs_1_, bf16[2,96,384]{2,1,0:T(8,128)(2,1)S(1)} %collective-permute-done.14.refs_2_, ...), custom_call_target="tpu_custom_call", output_to_operand_aliasing={{}: (8, {})} | custom-call | tf_op jit(solution)/shard_map/finish/pallas_call | solution.py:573
  (2 shorter events, 0.0 us)
Async XLA Ops:
  2.9 25.2 %copy-start.2 = (bf16[96,1152]{1,0:T(8,128)(2,1)S(1)}, bf16[96,1152]{1,0:T(8,128)(2,1)}, u32[]{:S(2)}) copy-start(bf16[96,1152]{1,0:T(8,128)(2,1)} %get-tuple-element.31.refs_0_) | copy-start | bytes 663556
  2.9 13.4 %collective-permute-start = (bf16[4,64,768]{2,1,0:T(8,128)(2,1)}, bf16[4,64,768]{2,1,0:T(8,128)(2,1)S(1)}, u32[]{:S(2)}, u32[]{:S(2)}) collective-permute-start(bf16[4,64,768]{2,1,0:T(8,128)(2,1)} %get-tuple-element.32.refs_0_), channel_id=1, source_target_pairs={{0,2},{1,3},{2,6},{3,7},{6,4},{7,5},{4,0},{5,1},{8,10},{9,11},{10,... | collective-permute-start | bytes 1179656 | tf_op jit(solution)/shard_map/ppermute | solution.py:409
  6.0 10.3 %collective-permute-start.3 = (bf16[4,64,768]{2,1,0:T(8,128)(2,1)}, bf16[4,64,768]{2,1,0:T(8,128)(2,1)S(1)}, u32[]{:S(2)}, u32[]{:S(2)}) collective-permute-start(bf16[4,64,768]{2,1,0:T(8,128)(2,1)} %get-tuple-element.35.shifted), channel_id=1, source_target_pairs={{0,1},{1,0},{2,3},{3,2},{4,5},{5,4},{6,7},{7,6},{8,9},{9,8},{10,11... | collective-permute-start | bytes 1179656 | tf_op jit(solution)/shard_map/ppermute | solution.py:396
  6.0 8.1 %collective-permute-start.1 = (bf16[96,1152]{1,0:T(8,128)(2,1)}, bf16[96,1152]{1,0:T(8,128)(2,1)S(1)}, u32[]{:S(2)}, u32[]{:S(2)}) collective-permute-start(bf16[96,1152]{1,0:T(8,128)(2,1)} %get-tuple-element.31.refs_0_), channel_id=1, source_target_pairs={{0,8},{8,0},{16,24},{24,16},{1,9},{9,1},{17,25},{25,17},{2,10},{10... | collective-permute-start | bytes 663560 | tf_op jit(solution)/shard_map/ppermute | solution.py:415
  7.5 6.2 %collective-permute-start.2 = (bf16[96,768]{1,0:T(8,128)(2,1)}, bf16[96,768]{1,0:T(8,128)(2,1)S(1)}, u32[]{:S(2)}, u32[]{:S(2)}) collective-permute-start(bf16[96,768]{1,0:T(8,128)(2,1)} %get-tuple-element.33), channel_id=1, source_target_pairs={{0,16},{8,24},{16,0},{24,8},{1,17},{9,25},{17,1},{25,9},{2,18},{10... | collective-permute-start | bytes 442376 | tf_op jit(solution)/shard_map/ppermute | solution.py:415
  9.0 24.8 %copy-start.6 = (bf16[384]{0:T(512)(128)(2,1)S(1)}, bf16[384]{0:T(512)(128)(2,1)}, u32[]{:S(2)}) copy-start(bf16[384]{0:T(512)(128)(2,1)} %param.19) | copy-start | bytes 2308
  9.0 25.2 %copy-start.4 = (bf16[4,64,768]{2,1,0:T(8,128)(2,1)S(1)}, bf16[4,64,768]{2,1,0:T(8,128)(2,1)}, u32[]{:S(2)}) copy-start(bf16[4,64,768]{2,1,0:T(8,128)(2,1)} %get-tuple-element.35.shifted) | copy-start | bytes 1179652
  9.0 25.2 %copy-start.5 = (bf16[4,64,768]{2,1,0:T(8,128)(2,1)S(1)}, bf16[4,64,768]{2,1,0:T(8,128)(2,1)}, u32[]{:S(2)}) copy-start(bf16[4,64,768]{2,1,0:T(8,128)(2,1)} %get-tuple-element.32.refs_0_) | copy-start | bytes 1179652
  16.3 11.2 %collective-permute-start.4 = (bf16[4,64,768]{2,1,0:T(8,128)(2,1)S(1)}, bf16[4,64,768]{2,1,0:T(8,128)(2,1)S(1)}, u32[]{:S(2)}, u32[]{:S(2)}) collective-permute-start(bf16[4,64,768]{2,1,0:T(8,128)(2,1)S(1)} %collective-permute-done.refs_1_), channel_id=1, source_target_pairs={{0,2},{1,3},{2,6},{3,7},{6,4},{7,5},{4,0},{5,1},{8,10},{9,11},{10,... | collective-permute-start | bytes 1179656 | tf_op jit(solution)/shard_map/ppermute | solution.py:409
  17.3 10.8 %collective-permute-start.6 = (bf16[96,768]{1,0:T(8,128)(2,1)S(1)}, bf16[96,768]{1,0:T(8,128)(2,1)S(1)}, u32[]{:S(2)}, u32[]{:S(2)}) collective-permute-start(bf16[96,768]{1,0:T(8,128)(2,1)S(1)} %collective-permute-done.2.refs_2_), channel_id=1, source_target_pairs={{0,8},{8,0},{16,24},{24,16},{1,9},{9,1},{17,25},{25,17},{2,10},{10... | collective-permute-start | bytes 442376 | tf_op jit(solution)/shard_map/ppermute | solution.py:415
  18.8 10.6 %collective-permute-start.11 = (bf16[800,128]{1,0:T(8,128)(2,1)}, bf16[800,128]{1,0:T(8,128)(2,1)S(1)}, u32[]{:S(2)}, u32[]{:S(2)}) collective-permute-start(bf16[800,128]{1,0:T(8,128)(2,1)} %bias.1.refs_0_), channel_id=1, source_target_pairs={{0,24},{8,16},{16,8},{24,0},{1,25},{9,17},{17,9},{25,1},{2,26},{10... | collective-permute-start | bytes 614408 | tf_op jit(solution)/shard_map/ppermute | solution.py:415
  20.3 9.7 %collective-permute-start.10 = (bf16[800,128]{1,0:T(8,128)(2,1)}, bf16[800,128]{1,0:T(8,128)(2,1)S(1)}, u32[]{:S(2)}, u32[]{:S(2)}) collective-permute-start(bf16[800,128]{1,0:T(8,128)(2,1)} %bias.1.refs_0_), channel_id=1, source_target_pairs={{0,16},{8,24},{16,0},{24,8},{1,17},{9,25},{17,1},{25,9},{2,18},{10... | collective-permute-start | bytes 614408 | tf_op jit(solution)/shard_map/ppermute | solution.py:415
  20.8 10.5 %collective-permute-start.9 = (bf16[800,128]{1,0:T(8,128)(2,1)}, bf16[800,128]{1,0:T(8,128)(2,1)S(1)}, u32[]{:S(2)}, u32[]{:S(2)}) collective-permute-start(bf16[800,128]{1,0:T(8,128)(2,1)} %bias.1.refs_0_), channel_id=1, source_target_pairs={{0,8},{8,0},{16,24},{24,16},{1,9},{9,1},{17,25},{25,17},{2,10},{10... | collective-permute-start | bytes 614408 | tf_op jit(solution)/shard_map/ppermute | solution.py:415
  27.5 10.4 %collective-permute-start.16 = (bf16[4,64,768]{2,1,0:T(8,128)(2,1)S(1)}, bf16[4,64,768]{2,1,0:T(8,128)(2,1)S(1)}, u32[]{:S(2)}, u32[]{:S(2)}) collective-permute-start(bf16[4,64,768]{2,1,0:T(8,128)(2,1)S(1)} %collective-permute-done.4.refs_2_), channel_id=1, source_target_pairs={{0,2},{1,3},{2,6},{3,7},{6,4},{7,5},{4,0},{5,1},{8,10},{9,11},{10,... | collective-permute-start | bytes 1179656 | tf_op jit(solution)/shard_map/ppermute | solution.py:409
  28.1 4.7 %collective-permute-start.7 = (bf16[4,96,384]{2,1,0:T(8,128)(2,1)S(1)}, bf16[4,96,384]{2,1,0:T(8,128)(2,1)S(1)}, u32[]{:S(2)}, u32[]{:S(2)}) collective-permute-start(bf16[4,96,384]{2,1,0:T(8,128)(2,1)S(1)} %get-tuple-element.40.query_mine), channel_id=1, source_target_pairs={{0,1},{1,0},{2,3},{3,2},{4,5},{5,4},{6,7},{7,6},{8,9},{9,8},{10,11... | collective-permute-start | bytes 884744 | tf_op jit(solution)/shard_map/ppermute | solution.py:396
  29.4 4.4 %collective-permute-start.8 = (bf16[4,96,384]{2,1,0:T(8,128)(2,1)S(1)}, bf16[4,96,384]{2,1,0:T(8,128)(2,1)S(1)}, u32[]{:S(2)}, u32[]{:S(2)}) collective-permute-start(bf16[4,96,384]{2,1,0:T(8,128)(2,1)S(1)} %get-tuple-element.41.key_mine), channel_id=1, source_target_pairs={{0,1},{1,0},{2,3},{3,2},{4,5},{5,4},{6,7},{7,6},{8,9},{9,8},{10,11... | collective-permute-start | bytes 884744 | tf_op jit(solution)/shard_map/ppermute | solution.py:396
  31.2 0.9 %copy-start.3 = (bf16[800,128]{1,0:T(8,128)(2,1)S(1)}, bf16[800,128]{1,0:T(8,128)(2,1)}, u32[]{:S(2)}) copy-start(bf16[800,128]{1,0:T(8,128)(2,1)} %bias.1.refs_0_) | copy-start | bytes 614404
  32.2 2.0 %collective-permute-start.13 = (bf16[4,288,128]{2,1,0:T(8,128)(2,1)S(1)}, bf16[4,288,128]{2,1,0:T(8,128)(2,1)S(1)}, u32[]{:S(2)}, u32[]{:S(2)}) collective-permute-start(bf16[4,288,128]{2,1,0:T(8,128)(2,1)S(1)} %get-tuple-element.46.own_value), channel_id=1, source_target_pairs={{0,1},{1,0},{2,3},{3,2},{4,5},{5,4},{6,7},{7,6},{8,9},{9,8},{10,11... | collective-permute-start | bytes 884744 | tf_op jit(solution)/shard_map/ppermute | solution.py:396
  32.3 1.9 %collective-permute-start.12 = (bf16[4,256,128]{2,1,0:T(8,128)(2,1)S(1)}, bf16[4,256,128]{2,1,0:T(8,128)(2,1)S(1)}, u32[]{:S(2)}, u32[]{:S(2)}) collective-permute-start(bf16[4,256,128]{2,1,0:T(8,128)(2,1)S(1)} %get-tuple-element.45), channel_id=1, source_target_pairs={{0,1},{1,0},{2,3},{3,2},{4,5},{5,4},{6,7},{7,6},{8,9},{9,8},{10,11... | collective-permute-start | bytes 786440 | tf_op jit(solution)/shard_map/ppermute | solution.py:396
  32.8 8.2 %collective-permute-start.5 = (bf16[2,96,384]{2,1,0:T(8,128)(2,1)S(1)}, bf16[2,96,384]{2,1,0:T(8,128)(2,1)S(1)}, u32[]{:S(2)}, u32[]{:S(2)}) collective-permute-start(bf16[2,96,384]{2,1,0:T(8,128)(2,1)S(1)} %stack_output.1.refs_0_), channel_id=1, source_target_pairs={{0,16},{8,24},{16,0},{24,8},{1,17},{9,25},{17,1},{25,9},{2,18},{10... | collective-permute-start | bytes 442376 | tf_op jit(solution)/shard_map/ppermute | solution.py:415
  39.2 3.4 %copy-start = (bf16[4,64,768]{2,1,0:T(8,128)(2,1)S(1)}, bf16[4,64,768]{2,1,0:T(8,128)(2,1)}, u32[]{:S(2)}) copy-start(bf16[4,64,768]{2,1,0:T(8,128)(2,1)} %refs_4_.3) | copy-start | bytes 1179652
  39.2 3.4 %copy-start.1 = (bf16[4,64,768]{2,1,0:T(8,128)(2,1)S(1)}, bf16[4,64,768]{2,1,0:T(8,128)(2,1)}, u32[]{:S(2)}) copy-start(bf16[4,64,768]{2,1,0:T(8,128)(2,1)} %refs_5_.3) | copy-start | bytes 1179652
  39.2 3.4 %collective-permute-start.18 = (f32[1,400,128]{2,1,0:T(8,128)S(1)}, f32[1,400,128]{2,1,0:T(8,128)S(1)}, u32[]{:S(2)}, u32[]{:S(2)}) collective-permute-start(f32[1,400,128]{2,1,0:T(8,128)S(1)} %get-tuple-element.56), channel_id=1, source_target_pairs={{0,1},{1,0},{2,3},{3,2},{4,5},{5,4},{6,7},{7,6},{8,9},{9,8},{10,11... | collective-permute-start | bytes 614408 | tf_op jit(solution)/shard_map/ppermute | solution.py:396
  40.6 3.1 %collective-permute-start.17 = (f32[1,400,128]{2,1,0:T(8,128)S(1)}, f32[1,400,128]{2,1,0:T(8,128)S(1)}, u32[]{:S(2)}, u32[]{:S(2)}) collective-permute-start(f32[1,400,128]{2,1,0:T(8,128)S(1)} %get-tuple-element.54), channel_id=1, source_target_pairs={{0,1},{1,0},{2,3},{3,2},{4,5},{5,4},{6,7},{7,6},{8,9},{9,8},{10,11... | collective-permute-start | bytes 614408 | tf_op jit(solution)/shard_map/ppermute | solution.py:396
  41.0 1.4 %collective-permute-start.14 = (bf16[2,96,384]{2,1,0:T(8,128)(2,1)S(1)}, bf16[2,96,384]{2,1,0:T(8,128)(2,1)S(1)}, u32[]{:S(2)}, u32[]{:S(2)}) collective-permute-start(bf16[2,96,384]{2,1,0:T(8,128)(2,1)S(1)} %stack_output.1.refs_0_), channel_id=1, source_target_pairs={{0,1},{1,0},{2,3},{3,2},{4,5},{5,4},{6,7},{7,6},{8,9},{9,8},{10,11... | collective-permute-start | bytes 442376 | tf_op jit(solution)/shard_map/ppermute | solution.py:396
  41.1 1.5 %collective-permute-start.15 = (bf16[2,96,384]{2,1,0:T(8,128)(2,1)S(1)}, bf16[2,96,384]{2,1,0:T(8,128)(2,1)S(1)}, u32[]{:S(2)}, u32[]{:S(2)}) collective-permute-start(bf16[2,96,384]{2,1,0:T(8,128)(2,1)S(1)} %collective-permute-done.5.refs_1_), channel_id=1, source_target_pairs={{0,1},{1,0},{2,3},{3,2},{4,5},{5,4},{6,7},{7,6},{8,9},{9,8},{10,11... | collective-permute-start | bytes 442376 | tf_op jit(solution)/shard_map/ppermute | solution.py:396

commit v4 on v3

--- a/solution.py
+++ b/solution.py
@@ -92,30 +92,17 @@
     )
     written[-1].start()
     copies[-1].wait()
-    extended[:, 2 * breadth :] = jnp.where(
-        core == 0, output_weight[:, :breadth], output_weight[:, breadth:]
-    )
+    extended[:, 2 * breadth :] = output_weight[...]
     written.append(pltpu.make_async_copy(extended, extended_hbm, sems_out.at[2 * samples + 1]))
     written[-1].start()
     for copy in written:
         copy.wait()
 
 
-def bias_kernel(
-    pair_hbm, value_hbm, weights_hbm, parcel, pair, value_weight, weights, collected, sems
-):
+def bias_kernel(pair, value_weight, weights, parcel, collected):
     rows, columns, channels = pair.shape
     heads = weights.shape[0]
-    per, batches = 8, 2
-    batch = rows // batches
-    copies = [pltpu.make_async_copy(weights_hbm, weights, sems.at[batches])]
-    for i in range(batches):
-        here = pl.ds(i * batch, batch)
-        copies.append(pltpu.make_async_copy(pair_hbm.at[here], pair.at[here], sems.at[i]))
-    copies.append(pltpu.make_async_copy(value_hbm, value_weight, sems.at[batches + 1]))
-    for copy in copies:
-        copy.start()
-    copies[0].wait()
+    per = 8
     record = 2 * heads
     extended = jnp.concatenate(
         [weights[...], jnp.full((heads, channels), 1.0 / channels, jnp.bfloat16)], axis=0
@@ -126,8 +113,6 @@
     lane = lax.broadcasted_iota(jnp.int32, (1, rows), 1)
     squares = jnp.zeros((columns, rows), jnp.float32)
     for i in range(rows // per):
-        if i * per % batch == 0:
-            copies[1 + i * per // batch].wait()
         block = pair[i * per : (i + 1) * per].reshape(per * columns, channels)
         centred = jnp.dot(block, centring, preferred_element_type=jnp.float32)
         summed = jnp.sum(centred * centred, axis=1, keepdims=True)
@@ -154,7 +139,6 @@
         parcel[at : at + half, :] = jnp.concatenate(own, axis=1).astype(jnp.bfloat16)
         at += heads // 2 * half
         parcel[at : at + half, :] = jnp.concatenate(other[::-1], axis=1).astype(jnp.bfloat16)
-    copies[-1].wait()
     depth, breadth = value_weight.shape
     whole = value_weight[...].astype(jnp.float32)
     kept = jnp.where(core == 0, whole[: depth // 2], whole[depth // 2 :]).astype(jnp.bfloat16)
@@ -347,22 +331,17 @@
         give[pair] = jnp.where(even, rights, lefts)
 
 
-def finish_kernel(heads, first, groups, *refs):
-    own_output, swapped_output = refs[:groups], refs[groups : 2 * groups]
-    activations, output_gate, keep, got = refs[2 * groups : 2 * groups + 4]
+def finish_kernel(heads, first, groups, activations, output_gate, keep, got, *refs):
+    output_parts = [group.at[k] for group in refs[:groups] for k in range(group.shape[0])]
     updated_hbm, updated, output_weight, sems = refs[-4:]
-    _, part_rows, part_columns = own_output[0].shape
+    part_rows = output_parts[0].shape[0]
     breadth = output_weight.shape[0]
     width = breadth // heads
     samples, rows, _ = updated.shape
-    core = lax.rem(lax.axis_index("row"), 2)
     place = lax.axis_index("noise")
-    for parts, of_core in ((own_output, core), (swapped_output, 1 - core)):
-        along = pl.ds(pl.multiple_of(of_core * part_columns, 128), part_columns)
-        ordered = [part.at[k] for part in parts for k in range(part.shape[0])]
-        for k, part in enumerate(ordered):
-            down = pl.ds(pl.multiple_of((place ^ k) * part_rows, math.gcd(part_rows, 32)), part_rows)
-            output_weight[down, along] = part[...].astype(output_weight.dtype)
+    for k, part in enumerate(output_parts):
+        down = pl.ds(pl.multiple_of((place ^ k) * part_rows, math.gcd(part_rows, 32)), part_rows)
+        output_weight[down, :] = part[...].astype(output_weight.dtype)
     writes = []
     for pair in range(samples // 2):
         own, other = keep.at[pair], got.at[pair]
@@ -453,7 +432,7 @@
     half = query_weight.shape[0] // 2
 
     in_hbm = pl.BlockSpec(memory_space=pltpu.HBM)
-    packed_shape, extended_shape = (half, 2 * head_features), (half, 3 * head_features)
+    packed_shape, extended_shape = (half, 2 * head_features), (half, 2 * head_features + features)
     assert output_weight.shape == (half, 2 * head_features)
     shifted, sent, packed, extended = pl.pallas_call(
         shift_kernel,
@@ -480,16 +459,9 @@
     assert output_weight.shape == (half, 2 * head_features)
     parcel = pl.pallas_call(
         bias_kernel,
-        in_specs=[in_hbm] * 3,
         out_shape=struct((tile_rows + piece_rows, columns), bf16),
-        scratch_shapes=[
-            pltpu.VMEM(pair_repr.shape, bf16),
-            pltpu.VMEM(value_weight.shape, bf16),
-            pltpu.VMEM(head_weights.shape, bf16),
-            pltpu.VMEM((rows * 2 * heads, columns), f32),
-            pltpu.SemaphoreType.DMA((4,)),
-        ],
-        compiler_params=pltpu.CompilerParams(vmem_limit_bytes=wide_bytes),
+        scratch_shapes=[pltpu.VMEM((rows * 2 * heads, columns), f32)],
+        compiler_params=params,
         name="bias",
     )(pair_repr, value_weight, head_weights)
     shifted_other = swap_cores(shifted)
@@ -506,8 +478,8 @@
     )(*weights)
     query_other, key_other = swap_cores(query_mine), swap_cores(key_mine)
     output_mine = pl.pallas_call(
-        functools.partial(stack_kernel, 2),
-        out_shape=struct((2, half, head_features), bf16),
+        functools.partial(stack_kernel, 1),
+        out_shape=struct((2, half, features), bf16),
         compiler_params=params,
         name="stack_output",
     )(extended, direct[0])
@@ -547,12 +519,10 @@
         compiler_params=params,
         name="early",
     )(query_mine, key_mine, query_other, key_other, bias_row, shifted, shifted_other, own_bias, swapped, own_value, swapped_value, *ring)
-    own_output = [output_mine]
+    output_parts = [output_mine]
     for k in range(1, noise_size.bit_length() - 1):
-        arrived = from_noise(own_output[0] if k == 1 else jnp.concatenate(own_output, axis=0), 2**k)
-        own_output.append(arrived)
-    own_output, _ = after((own_output, partial))
-    swapped_output = [swap_cores(part) for part in own_output]
+        held = jnp.concatenate(output_parts, axis=0) if k > 1 else output_mine
+        output_parts.append(from_noise(held, 2**k))
     keep, got = [], []
     chunks = 2
     each = samples // chunks
@@ -568,14 +538,14 @@
         got.append(swap_cores(give))
     updated = []
     for c in range(chunks):
-        operands = [*own_output, *swapped_output, activations, output_gate, keep[c], got[c], *updated]
+        operands = [activations, output_gate, keep[c], got[c], *output_parts, *updated]
         updated = [
             pl.pallas_call(
-                functools.partial(finish_kernel, heads, c * each, len(own_output)),
-                in_specs=[pl.BlockSpec(memory_space=pltpu.VMEM)] * (2 * len(own_output) + 4) + [in_hbm] * len(updated),
+                functools.partial(finish_kernel, heads, c * each, len(output_parts)),
+                in_specs=[pl.BlockSpec(memory_space=pltpu.VMEM)] * (4 + len(output_parts)) + [in_hbm] * len(updated),
                 out_specs=in_hbm,
                 out_shape=struct(activations.shape, bf16),
-                input_output_aliases={2 * len(own_output) + 4: 0} if updated else {},
+                input_output_aliases={4 + len(output_parts): 0} if updated else {},
                 scratch_shapes=[
                     pltpu.VMEM((each, rows, features), bf16),
                     pltpu.VMEM((head_features, features), output_type),

time: 45.6 us -> 44.3 us (0.971); the launches traced: 44.7 us -> 44.1 us
  Pallas kernels: 15.8 us -> 13.1 us
  local copies, waits for them, and re-layouts: 0.96 us -> 3.21 us
  waiting for transfers between devices: 12.5 us -> 10.3 us
  starting transfers between devices: 15.3 us -> 17.3 us
    pallas_call x4, Pallas kernels: 6.73 us -> 3.98 us  [the longest x2 2.1 us: body(): pl.pallas_call(functools.partial(finish_kernel, heads, c * each, len(outp...]
    ppermute x3, waiting for transfers between devices: 7.56 us -> 5.03 us  [next_chip(): return lax.ppermute(array, 'row', pairs)]
    unnamed x14 -> x18, local copies, waits for them, and re-layouts: 0.96 us -> 3.21 us
    ppermute x3, starting transfers between devices: 4.54 us -> 6.4 us  [next_chip(): return lax.ppermute(array, 'row', pairs)]
    ppermute x7, waiting for transfers between devices: 3.45 us -> 5.29 us  [from_noise(): lax.ppermute(array, 'noise', [(i, i ^ k) for i in range(lax.axis_size('no...]
    ppermute x9 -> x7, waiting for transfers between devices: 1.53 us -> 0.02 us  [swap_cores(): lax.ppermute(array, 'row', [(i, i ^ 1) for i in range(lax.axis_size('row'...]
    ppermute x7, starting transfers between devices: 8.96 us -> 9.57 us  [from_noise(): lax.ppermute(array, 'noise', [(i, i ^ k) for i in range(lax.axis_size('no...]
    ppermute x9 -> x7, starting transfers between devices: 1.79 us -> 1.27 us  [swap_cores(): lax.ppermute(array, 'row', [(i, i ^ 1) for i in range(lax.axis_size('row'...]
  transfers between devices with their start and end apart: 19 -> 17, of which waited for: 9 -> 7; matrix products, arithmetic and copies ran while one was open for 0% -> 0% of each run, Pallas kernels for 26% -> 21%
where the time goes in v4:
time: 44.3 us; the launch traced here: 44.1 us
  starting transfers between devices  17.3 us (39%)
  Pallas kernels  13.1 us (30%)
  waiting for transfers between devices  10.3 us (23%)
  local copies, waits for them, and re-layouts  3.21 us (7%)
    ppermute x7, starting transfers between devices, from_noise(): lax.ppermute(array, 'noise', [(i, i ^ k) for i in range(lax.axis_size('no...  9.57 us
    ppermute x3, starting transfers between devices, next_chip(): return lax.ppermute(array, 'row', pairs)  6.4 us
    ppermute x7, waiting for transfers between devices, from_noise(): lax.ppermute(array, 'noise', [(i, i ^ k) for i in range(lax.axis_size('no...  5.29 us
    ppermute x3, waiting for transfers between devices, next_chip(): return lax.ppermute(array, 'row', pairs)  5.03 us
    pallas_call x1, Pallas kernels, body(): pl.pallas_call(functools.partial(early_kernel, steps, heads), out_shape=[...  3.72 us
    unnamed x18, local copies, waits for them, and re-layouts  3.21 us
    pallas_call x1, Pallas kernels, body(): pl.pallas_call(shift_kernel, in_specs=[in_hbm] * 7, out_specs=[in_hbm] *...  2.91 us
    pallas_call x2, Pallas kernels, body(): pl.pallas_call(functools.partial(late_kernel, steps, heads, c * each), ou...  2.35 us
  transfers between devices with their start and end apart: 17, of which 7 were waited for; matrix products, arithmetic and copies ran while one was open for 0% of the time, Pallas kernels for 21%

profile of v4, /device:TPU:0, one launch (start us, length us, event | category | flops | bytes accessed | tf_op | source)
XLA Modules:
  0.0 44.1 jit_solution(2557990523046064844)
XLA Ops:
  0.0 2.9 %shift.1 = (bf16[4,64,768]{2,1,0:T(8,128)(2,1)}, bf16[4,64,768]{2,1,0:T(8,128)(2,1)}, bf16[96,768]{1,0:T(8,128)(2,1)}, bf16[96,1536]{1,0:T(8,128)(2,1)}) custom-call(bf16[4,64,768]{2,1,0:T(8,128)(2,1)} %activations.3, bf16[4,64,768]{2,1,0:T(8,128)(2,1)} %scale_hbm.1, bf16[4,64,768]{2,1,0:T(8,128)(2,1)} %shift_hbm.1, s32[4,64]{1,0:T(4,128)} %mask_hbm.1, ...), custom_call_target="tpu_custom_call" | custom-call | tf_op jit(solution)/shard_map/shift/pallas_call | solution.py:437
  2.9 3.1 %collective-permute-start = (bf16[4,64,768]{2,1,0:T(8,128)(2,1)}, bf16[4,64,768]{2,1,0:T(8,128)(2,1)S(1)}, u32[]{:S(2)}, u32[]{:S(2)}) collective-permute-start(bf16[4,64,768]{2,1,0:T(8,128)(2,1)} %get-tuple-element.30.refs_0_), channel_id=1, source_target_pairs={{0,2},{1,3},{2,6},{3,7},{6,4},{7,5},{4,0},{5,1},{8,10},{9,11},{10,... | collective-permute-start | bytes 1179656 | tf_op jit(solution)/shard_map/ppermute | solution.py:388
  6.0 0.0 collective-permute-start.3
  6.0 1.5 %collective-permute-start.1 = (bf16[96,1536]{1,0:T(8,128)(2,1)}, bf16[96,1536]{1,0:T(8,128)(2,1)S(1)}, u32[]{:S(2)}, u32[]{:S(2)}) collective-permute-start(bf16[96,1536]{1,0:T(8,128)(2,1)} %get-tuple-element.29.refs_0_), channel_id=1, source_target_pairs={{0,8},{8,0},{16,24},{24,16},{1,9},{9,1},{17,25},{25,17},{2,10},{10... | collective-permute-start | bytes 884744 | tf_op jit(solution)/shard_map/ppermute | solution.py:394
  7.5 1.5 %collective-permute-start.2 = (bf16[96,768]{1,0:T(8,128)(2,1)}, bf16[96,768]{1,0:T(8,128)(2,1)S(1)}, u32[]{:S(2)}, u32[]{:S(2)}) collective-permute-start(bf16[96,768]{1,0:T(8,128)(2,1)} %get-tuple-element.31), channel_id=1, source_target_pairs={{0,16},{8,24},{16,0},{24,8},{1,17},{9,25},{17,1},{25,9},{2,18},{10... | collective-permute-start | bytes 442376 | tf_op jit(solution)/shard_map/ppermute | solution.py:394
  9.0 0.0 copy-start.1
  9.0 1.6 %copy-done.1 = bf16[64,128,128]{2,1,0:T(8,128)(2,1)S(1)} copy-done((bf16[64,128,128]{2,1,0:T(8,128)(2,1)S(1)}, bf16[64,128,128]{2,1,0:T(8,128)(2,1)}, u32[]{:S(2)}) %copy-start.1) | copy-done | bytes 2097176
  10.6 0.0 copy-start.6
  10.6 0.9 %copy-done.6 = bf16[192,384]{1,0:T(8,128)(2,1)S(1)} copy-done((bf16[192,384]{1,0:T(8,128)(2,1)S(1)}, bf16[192,384]{1,0:T(8,128)(2,1)}, u32[]{:S(2)}) %copy-start.6) | copy-done | bytes 147480
  11.5 0.0 copy-start.7
  11.5 0.7 %copy-done.7 = bf16[128,8]{0,1:T(8,128)(2,1)S(1)} copy-done((bf16[128,8]{0,1:T(8,128)(2,1)S(1)}, bf16[128,8]{0,1:T(8,128)(2,1)}, u32[]{:S(2)}) %copy-start.7) | copy-done | bytes 2072
  12.2 0.0 copy-start.3
  12.2 0.0 copy-start.8
  12.2 0.0 copy-start.4
  12.2 0.0 copy-start.5
  12.2 1.9 %bias.1.refs_0_ = bf16[800,128]{1,0:T(8,128)(2,1)S(1)} custom-call(bf16[64,128,128]{2,1,0:T(8,128)(2,1)S(1)} %copy-done.1, bf16[192,384]{1,0:T(8,128)(2,1)S(1)} %copy-done.6, bf16[8,128]{1,0:T(8,128)(2,1)S(1)} %bitcast.1), custom_call_target="tpu_custom_call" | custom-call | tf_op jit(solution)/shard_map/bias/pallas_call | solution.py:460
  14.1 0.0 collective-permute-done.2.refs_2_
  14.1 1.5 %collective-permute-done.1.refs_1_ = bf16[96,1536]{1,0:T(8,128)(2,1)S(1)} collective-permute-done((bf16[96,1536]{1,0:T(8,128)(2,1)}, bf16[96,1536]{1,0:T(8,128)(2,1)S(1)}, u32[]{:S(2)}, u32[]{:S(2)}) %collective-permute-start.1) | collective-permute-done | bytes 294944 | tf_op jit(solution)/shard_map/ppermute | solution.py:394
  15.6 0.7 %collective-permute-done.refs_1_ = bf16[4,64,768]{2,1,0:T(8,128)(2,1)S(1)} collective-permute-done((bf16[4,64,768]{2,1,0:T(8,128)(2,1)}, bf16[4,64,768]{2,1,0:T(8,128)(2,1)S(1)}, u32[]{:S(2)}, u32[]{:S(2)}) %collective-permute-start) | collective-permute-done | bytes 393248 | tf_op jit(solution)/shard_map/ppermute | solution.py:388
  16.3 0.0 collective-permute-done.3.shifted_other
  16.3 1.9 %collective-permute-start.12 = (bf16[4,64,768]{2,1,0:T(8,128)(2,1)S(1)}, bf16[4,64,768]{2,1,0:T(8,128)(2,1)S(1)}, u32[]{:S(2)}, u32[]{:S(2)}) collective-permute-start(bf16[4,64,768]{2,1,0:T(8,128)(2,1)S(1)} %collective-permute-done.refs_1_), channel_id=1, source_target_pairs={{0,2},{1,3},{2,6},{3,7},{6,4},{7,5},{4,0},{5,1},{8,10},{9,11},{10,... | collective-permute-start | bytes 1179656 | tf_op jit(solution)/shard_map/ppermute | solution.py:388
  18.2 1.5 %collective-permute-start.4 = (bf16[96,768]{1,0:T(8,128)(2,1)S(1)}, bf16[96,768]{1,0:T(8,128)(2,1)S(1)}, u32[]{:S(2)}, u32[]{:S(2)}) collective-permute-start(bf16[96,768]{1,0:T(8,128)(2,1)S(1)} %collective-permute-done.2.refs_2_), channel_id=1, source_target_pairs={{0,8},{8,0},{16,24},{24,16},{1,9},{9,1},{17,25},{25,17},{2,10},{10... | collective-permute-start | bytes 442376 | tf_op jit(solution)/shard_map/ppermute | solution.py:394
  19.7 1.5 %collective-permute-start.9 = (bf16[800,128]{1,0:T(8,128)(2,1)S(1)}, bf16[800,128]{1,0:T(8,128)(2,1)S(1)}, u32[]{:S(2)}, u32[]{:S(2)}) collective-permute-start(bf16[800,128]{1,0:T(8,128)(2,1)S(1)} %bias.1.refs_0_), channel_id=1, source_target_pairs={{0,24},{8,16},{16,8},{24,0},{1,25},{9,17},{17,9},{25,1},{2,26},{10... | collective-permute-start | bytes 614408 | tf_op jit(solution)/shard_map/ppermute | solution.py:394
  21.2 0.5 %collective-permute-start.8 = (bf16[800,128]{1,0:T(8,128)(2,1)S(1)}, bf16[800,128]{1,0:T(8,128)(2,1)S(1)}, u32[]{:S(2)}, u32[]{:S(2)}) collective-permute-start(bf16[800,128]{1,0:T(8,128)(2,1)S(1)} %bias.1.refs_0_), channel_id=1, source_target_pairs={{0,16},{8,24},{16,0},{24,8},{1,17},{9,25},{17,1},{25,9},{2,18},{10... | collective-permute-start | bytes 614408 | tf_op jit(solution)/shard_map/ppermute | solution.py:394
  21.7 1.5 %collective-permute-start.7 = (bf16[800,128]{1,0:T(8,128)(2,1)S(1)}, bf16[800,128]{1,0:T(8,128)(2,1)S(1)}, u32[]{:S(2)}, u32[]{:S(2)}) collective-permute-start(bf16[800,128]{1,0:T(8,128)(2,1)S(1)} %bias.1.refs_0_), channel_id=1, source_target_pairs={{0,8},{8,0},{16,24},{24,16},{1,9},{9,1},{17,25},{25,17},{2,10},{10... | collective-permute-start | bytes 614408 | tf_op jit(solution)/shard_map/ppermute | solution.py:394
  23.2 4.3 %collective-permute-done.12.refs_2_ = bf16[4,64,768]{2,1,0:T(8,128)(2,1)S(1)} collective-permute-done((bf16[4,64,768]{2,1,0:T(8,128)(2,1)S(1)}, bf16[4,64,768]{2,1,0:T(8,128)(2,1)S(1)}, u32[]{:S(2)}, u32[]{:S(2)}) %collective-permute-start.12) | collective-permute-done | bytes 393248 | tf_op jit(solution)/shard_map/ppermute | solution.py:388
  27.5 1.4 %collective-permute-start.13 = (bf16[4,64,768]{2,1,0:T(8,128)(2,1)S(1)}, bf16[4,64,768]{2,1,0:T(8,128)(2,1)S(1)}, u32[]{:S(2)}, u32[]{:S(2)}) collective-permute-start(bf16[4,64,768]{2,1,0:T(8,128)(2,1)S(1)} %collective-permute-done.12.refs_2_), channel_id=1, source_target_pairs={{0,2},{1,3},{2,6},{3,7},{6,4},{7,5},{4,0},{5,1},{8,10},{9,11},{10,... | collective-permute-start | bytes 1179656 | tf_op jit(solution)/shard_map/ppermute | solution.py:388
  29.0 0.0 collective-permute-done.4.refs_3_
  29.0 0.0 copy-done.3
  29.0 0.1 stack.1
  29.0 0.1 collective-permute-start.5
  29.1 1.2 %collective-permute-done.9.refs_3_ = bf16[800,128]{1,0:T(8,128)(2,1)S(1)} collective-permute-done((bf16[800,128]{1,0:T(8,128)(2,1)S(1)}, bf16[800,128]{1,0:T(8,128)(2,1)S(1)}, u32[]{:S(2)}, u32[]{:S(2)}) %collective-permute-start.9) | collective-permute-done | bytes 204832 | tf_op jit(solution)/shard_map/ppermute | solution.py:394
  30.4 0.0 collective-permute-start.6
  30.4 1.1 %collective-permute-done.8.refs_2_ = bf16[800,128]{1,0:T(8,128)(2,1)S(1)} collective-permute-done((bf16[800,128]{1,0:T(8,128)(2,1)S(1)}, bf16[800,128]{1,0:T(8,128)(2,1)S(1)}, u32[]{:S(2)}, u32[]{:S(2)}) %collective-permute-start.8) | collective-permute-done | bytes 204832 | tf_op jit(solution)/shard_map/ppermute | solution.py:394
  31.5 0.7 %collective-permute-done.7.refs_1_ = bf16[800,128]{1,0:T(8,128)(2,1)S(1)} collective-permute-done((bf16[800,128]{1,0:T(8,128)(2,1)S(1)}, bf16[800,128]{1,0:T(8,128)(2,1)S(1)}, u32[]{:S(2)}, u32[]{:S(2)}) %collective-permute-start.7) | collective-permute-done | bytes 204832 | tf_op jit(solution)/shard_map/ppermute | solution.py:394
  32.2 0.1 sort.1
  32.3 0.1 collective-permute-start.11
  32.3 0.5 %collective-permute-start.10 = (bf16[4,256,128]{2,1,0:T(8,128)(2,1)S(1)}, bf16[4,256,128]{2,1,0:T(8,128)(2,1)S(1)}, u32[]{:S(2)}, u32[]{:S(2)}) collective-permute-start(bf16[4,256,128]{2,1,0:T(8,128)(2,1)S(1)} %get-tuple-element.41), channel_id=1, source_target_pairs={{0,1},{1,0},{2,3},{3,2},{4,5},{5,4},{6,7},{7,6},{8,9},{9,8},{10,11... | collective-permute-start | bytes 786440 | tf_op jit(solution)/shard_map/ppermute | solution.py:375
  32.9 0.0 collective-permute-done.5.query_other
  32.9 1.6 %collective-permute-start.15 = (bf16[2,96,768]{2,1,0:T(8,128)(2,1)S(1)}, bf16[2,96,768]{2,1,0:T(8,128)(2,1)S(1)}, u32[]{:S(2)}, u32[]{:S(2)}) collective-permute-start(bf16[2,96,768]{2,1,0:T(8,128)(2,1)S(1)} %stack_output.1.refs_0_), channel_id=1, source_target_pairs={{0,16},{8,24},{16,0},{24,8},{1,17},{9,25},{17,1},{25,9},{2,18},{10... | collective-permute-start | bytes 884744 | tf_op jit(solution)/shard_map/ppermute | solution.py:394
  34.5 0.0 copy-done.8
  34.5 0.0 collective-permute-done.6.key_other
  34.5 0.0 collective-permute-done.10.swapped
  34.5 0.0 collective-permute-done.11.swapped_value
  34.5 0.0 copy-done.4
  34.5 0.0 copy-done.5
  34.5 3.7 %early.1 = (f32[4,400,128]{2,1,0:T(8,128)S(1)}, bf16[4,128,384]{2,1,0:T(8,128)(2,1)S(1)}, bf16[768,384]{1,0:T(8,128)(2,1)S(1)}, bf16[384,768]{1,0:T(8,128)(2,1)S(1)}) custom-call(bf16[4,96,384]{2,1,0:T(8,128)(2,1)S(1)} %get-tuple-element.36.query_mine, bf16[4,96,384]{2,1,0:T(8,128)(2,1)S(1)} %get-tuple-element.37.key_mine, ...), custom_call_target="tpu_custom_call" | custom-call | tf_op jit(solution)/shard_map/early/pallas_call | solution.py:506
  38.2 0.0 collective-permute-done.13.block
  38.2 1.2 %late.3 = (f32[1,400,128]{2,1,0:T(8,128)S(1)}, f32[1,400,128]{2,1,0:T(8,128)S(1)}) custom-call(f32[4,400,128]{2,1,0:T(8,128)S(1)} %get-tuple-element.44.partial, bf16[4,128,384]{2,1,0:T(8,128)(2,1)S(1)} %get-tuple-element.45.queries, bf16[768,384]{1,0:T(8,128)(2,1)S(1)} %get-tuple-element.46.key_weight, bf16[384,768]{1,0:T(8,128)(2,1)S(1)} %get-tuple-element.47.value_weight, ...), custom_call_target="tpu_custom_call" | custom-call | tf_op jit(solution)/shard_map/late/pallas_call | solution.py:530
  39.4 0.0 copy-start
  39.4 0.0 copy-start.2
  39.5 0.1 collective-permute-start.16
  39.5 1.2 %late.2 = (f32[1,400,128]{2,1,0:T(8,128)S(1)}, f32[1,400,128]{2,1,0:T(8,128)S(1)}) custom-call(f32[4,400,128]{2,1,0:T(8,128)S(1)} %get-tuple-element.44.partial, bf16[4,128,384]{2,1,0:T(8,128)(2,1)S(1)} %get-tuple-element.45.queries, bf16[768,384]{1,0:T(8,128)(2,1)S(1)} %get-tuple-element.46.key_weight, bf16[384,768]{1,0:T(8,128)(2,1)S(1)} %get-tuple-element.47.value_weight, ...), custom_call_target="tpu_custom_call" | custom-call | tf_op jit(solution)/shard_map/late/pallas_call | solution.py:530
  40.7 0.6 %collective-permute-start.14 = (f32[1,400,128]{2,1,0:T(8,128)S(1)}, f32[1,400,128]{2,1,0:T(8,128)S(1)}, u32[]{:S(2)}, u32[]{:S(2)}) collective-permute-start(f32[1,400,128]{2,1,0:T(8,128)S(1)} %get-tuple-element.49), channel_id=1, source_target_pairs={{0,1},{1,0},{2,3},{3,2},{4,5},{5,4},{6,7},{7,6},{8,9},{9,8},{10,11... | collective-permute-start | bytes 614408 | tf_op jit(solution)/shard_map/ppermute | solution.py:375
  41.3 0.7 %collective-permute-done.15.refs_1_ = bf16[2,96,768]{2,1,0:T(8,128)(2,1)S(1)} collective-permute-done((bf16[2,96,768]{2,1,0:T(8,128)(2,1)S(1)}, bf16[2,96,768]{2,1,0:T(8,128)(2,1)S(1)}, u32[]{:S(2)}, u32[]{:S(2)}) %collective-permute-start.15) | collective-permute-done | bytes 294944 | tf_op jit(solution)/shard_map/ppermute | solution.py:394
  41.9 0.0 collective-permute-done.16.got
  41.9 0.0 copy-done
  41.9 0.0 copy-done.2
  41.9 1.1 %finish.2.refs_2_ = bf16[4,64,768]{2,1,0:T(8,128)(2,1)} custom-call(bf16[4,64,768]{2,1,0:T(8,128)(2,1)S(1)} %copy-done, bf16[4,64,768]{2,1,0:T(8,128)(2,1)S(1)} %copy-done.2, f32[1,400,128]{2,1,0:T(8,128)S(1)} %get-tuple-element.51.keep, f32[1,400,128]{2,1,0:T(8,128)S(1)} %collective-permute-done.16.got, bf16[2,96,768]{2,1,0:T(8,128)(2,1)S(1)} %stack_output.1.refs_0_, ...), custom_call_target="tpu_custom_call" | custom-call | tf_op jit(solution)/shard_map/finish/pallas_call | solution.py:543
  43.0 0.0 collective-permute-done.14.got
  43.0 1.0 %finish.3 = bf16[4,64,768]{2,1,0:T(8,128)(2,1)} custom-call(bf16[4,64,768]{2,1,0:T(8,128)(2,1)S(1)} %copy-done, bf16[4,64,768]{2,1,0:T(8,128)(2,1)S(1)} %copy-done.2, f32[1,400,128]{2,1,0:T(8,128)S(1)} %get-tuple-element.48.keep, f32[1,400,128]{2,1,0:T(8,128)S(1)} %collective-permute-done.14.got, ...), custom_call_target="tpu_custom_call", output_to_operand_aliasing={{}: (6, {})} | custom-call | tf_op jit(solution)/shard_map/finish/pallas_call | solution.py:543
  (2 shorter events, 0.0 us)
Async XLA Ops:
  2.9 13.4 %collective-permute-start = (bf16[4,64,768]{2,1,0:T(8,128)(2,1)}, bf16[4,64,768]{2,1,0:T(8,128)(2,1)S(1)}, u32[]{:S(2)}, u32[]{:S(2)}) collective-permute-start(bf16[4,64,768]{2,1,0:T(8,128)(2,1)} %get-tuple-element.30.refs_0_), channel_id=1, source_target_pairs={{0,2},{1,3},{2,6},{3,7},{6,4},{7,5},{4,0},{5,1},{8,10},{9,11},{10,... | collective-permute-start | bytes 1179656 | tf_op jit(solution)/shard_map/ppermute | solution.py:388
  6.0 10.3 %collective-permute-start.3 = (bf16[4,64,768]{2,1,0:T(8,128)(2,1)}, bf16[4,64,768]{2,1,0:T(8,128)(2,1)S(1)}, u32[]{:S(2)}, u32[]{:S(2)}) collective-permute-start(bf16[4,64,768]{2,1,0:T(8,128)(2,1)} %get-tuple-element.33.shifted), channel_id=1, source_target_pairs={{0,1},{1,0},{2,3},{3,2},{4,5},{5,4},{6,7},{7,6},{8,9},{9,8},{10,11... | collective-permute-start | bytes 1179656 | tf_op jit(solution)/shard_map/ppermute | solution.py:375
  6.0 9.6 %collective-permute-start.1 = (bf16[96,1536]{1,0:T(8,128)(2,1)}, bf16[96,1536]{1,0:T(8,128)(2,1)S(1)}, u32[]{:S(2)}, u32[]{:S(2)}) collective-permute-start(bf16[96,1536]{1,0:T(8,128)(2,1)} %get-tuple-element.29.refs_0_), channel_id=1, source_target_pairs={{0,8},{8,0},{16,24},{24,16},{1,9},{9,1},{17,25},{25,17},{2,10},{10... | collective-permute-start | bytes 884744 | tf_op jit(solution)/shard_map/ppermute | solution.py:394
  7.5 6.6 %collective-permute-start.2 = (bf16[96,768]{1,0:T(8,128)(2,1)}, bf16[96,768]{1,0:T(8,128)(2,1)S(1)}, u32[]{:S(2)}, u32[]{:S(2)}) collective-permute-start(bf16[96,768]{1,0:T(8,128)(2,1)} %get-tuple-element.31), channel_id=1, source_target_pairs={{0,16},{8,24},{16,0},{24,8},{1,17},{9,25},{17,1},{25,9},{2,18},{10... | collective-permute-start | bytes 442376 | tf_op jit(solution)/shard_map/ppermute | solution.py:394
  9.0 1.6 %copy-start.1 = (bf16[64,128,128]{2,1,0:T(8,128)(2,1)S(1)}, bf16[64,128,128]{2,1,0:T(8,128)(2,1)}, u32[]{:S(2)}) copy-start(bf16[64,128,128]{2,1,0:T(8,128)(2,1)} %pair.1) | copy-start | bytes 6291460
  10.6 0.9 %copy-start.6 = (bf16[192,384]{1,0:T(8,128)(2,1)S(1)}, bf16[192,384]{1,0:T(8,128)(2,1)}, u32[]{:S(2)}) copy-start(bf16[192,384]{1,0:T(8,128)(2,1)} %value_weight.1) | copy-start | bytes 442372
  11.5 0.7 %copy-start.7 = (bf16[128,8]{0,1:T(8,128)(2,1)S(1)}, bf16[128,8]{0,1:T(8,128)(2,1)}, u32[]{:S(2)}) copy-start(bf16[128,8]{0,1:T(8,128)(2,1)} %param.17) | copy-start | bytes 6148
  12.2 16.8 %copy-start.3 = (bf16[96,1536]{1,0:T(8,128)(2,1)S(1)}, bf16[96,1536]{1,0:T(8,128)(2,1)}, u32[]{:S(2)}) copy-start(bf16[96,1536]{1,0:T(8,128)(2,1)} %get-tuple-element.29.refs_0_) | copy-start | bytes 884740
  12.2 22.3 %copy-start.8 = (bf16[384]{0:T(512)(128)(2,1)S(1)}, bf16[384]{0:T(512)(128)(2,1)}, u32[]{:S(2)}) copy-start(bf16[384]{0:T(512)(128)(2,1)} %param.19) | copy-start | bytes 2308
  12.2 22.3 %copy-start.4 = (bf16[4,64,768]{2,1,0:T(8,128)(2,1)S(1)}, bf16[4,64,768]{2,1,0:T(8,128)(2,1)}, u32[]{:S(2)}) copy-start(bf16[4,64,768]{2,1,0:T(8,128)(2,1)} %get-tuple-element.33.shifted) | copy-start | bytes 1179652
  12.2 22.3 %copy-start.5 = (bf16[4,64,768]{2,1,0:T(8,128)(2,1)S(1)}, bf16[4,64,768]{2,1,0:T(8,128)(2,1)}, u32[]{:S(2)}) copy-start(bf16[4,64,768]{2,1,0:T(8,128)(2,1)} %get-tuple-element.30.refs_0_) | copy-start | bytes 1179652
  16.3 11.2 %collective-permute-start.12 = (bf16[4,64,768]{2,1,0:T(8,128)(2,1)S(1)}, bf16[4,64,768]{2,1,0:T(8,128)(2,1)S(1)}, u32[]{:S(2)}, u32[]{:S(2)}) collective-permute-start(bf16[4,64,768]{2,1,0:T(8,128)(2,1)S(1)} %collective-permute-done.refs_1_), channel_id=1, source_target_pairs={{0,2},{1,3},{2,6},{3,7},{6,4},{7,5},{4,0},{5,1},{8,10},{9,11},{10,... | collective-permute-start | bytes 1179656 | tf_op jit(solution)/shard_map/ppermute | solution.py:388
  18.2 10.7 %collective-permute-start.4 = (bf16[96,768]{1,0:T(8,128)(2,1)S(1)}, bf16[96,768]{1,0:T(8,128)(2,1)S(1)}, u32[]{:S(2)}, u32[]{:S(2)}) collective-permute-start(bf16[96,768]{1,0:T(8,128)(2,1)S(1)} %collective-permute-done.2.refs_2_), channel_id=1, source_target_pairs={{0,8},{8,0},{16,24},{24,16},{1,9},{9,1},{17,25},{25,17},{2,10},{10... | collective-permute-start | bytes 442376 | tf_op jit(solution)/shard_map/ppermute | solution.py:394
  19.7 10.6 %collective-permute-start.9 = (bf16[800,128]{1,0:T(8,128)(2,1)S(1)}, bf16[800,128]{1,0:T(8,128)(2,1)S(1)}, u32[]{:S(2)}, u32[]{:S(2)}) collective-permute-start(bf16[800,128]{1,0:T(8,128)(2,1)S(1)} %bias.1.refs_0_), channel_id=1, source_target_pairs={{0,24},{8,16},{16,8},{24,0},{1,25},{9,17},{17,9},{25,1},{2,26},{10... | collective-permute-start | bytes 614408 | tf_op jit(solution)/shard_map/ppermute | solution.py:394
  21.2 10.3 %collective-permute-start.8 = (bf16[800,128]{1,0:T(8,128)(2,1)S(1)}, bf16[800,128]{1,0:T(8,128)(2,1)S(1)}, u32[]{:S(2)}, u32[]{:S(2)}) collective-permute-start(bf16[800,128]{1,0:T(8,128)(2,1)S(1)} %bias.1.refs_0_), channel_id=1, source_target_pairs={{0,16},{8,24},{16,0},{24,8},{1,17},{9,25},{17,1},{25,9},{2,18},{10... | collective-permute-start | bytes 614408 | tf_op jit(solution)/shard_map/ppermute | solution.py:394
  21.7 10.5 %collective-permute-start.7 = (bf16[800,128]{1,0:T(8,128)(2,1)S(1)}, bf16[800,128]{1,0:T(8,128)(2,1)S(1)}, u32[]{:S(2)}, u32[]{:S(2)}) collective-permute-start(bf16[800,128]{1,0:T(8,128)(2,1)S(1)} %bias.1.refs_0_), channel_id=1, source_target_pairs={{0,8},{8,0},{16,24},{24,16},{1,9},{9,1},{17,25},{25,17},{2,10},{10... | collective-permute-start | bytes 614408 | tf_op jit(solution)/shard_map/ppermute | solution.py:394
  27.5 10.7 %collective-permute-start.13 = (bf16[4,64,768]{2,1,0:T(8,128)(2,1)S(1)}, bf16[4,64,768]{2,1,0:T(8,128)(2,1)S(1)}, u32[]{:S(2)}, u32[]{:S(2)}) collective-permute-start(bf16[4,64,768]{2,1,0:T(8,128)(2,1)S(1)} %collective-permute-done.12.refs_2_), channel_id=1, source_target_pairs={{0,2},{1,3},{2,6},{3,7},{6,4},{7,5},{4,0},{5,1},{8,10},{9,11},{10,... | collective-permute-start | bytes 1179656 | tf_op jit(solution)/shard_map/ppermute | solution.py:388
  29.0 3.8 %collective-permute-start.5 = (bf16[4,96,384]{2,1,0:T(8,128)(2,1)S(1)}, bf16[4,96,384]{2,1,0:T(8,128)(2,1)S(1)}, u32[]{:S(2)}, u32[]{:S(2)}) collective-permute-start(bf16[4,96,384]{2,1,0:T(8,128)(2,1)S(1)} %get-tuple-element.36.query_mine), channel_id=1, source_target_pairs={{0,1},{1,0},{2,3},{3,2},{4,5},{5,4},{6,7},{7,6},{8,9},{9,8},{10,11... | collective-permute-start | bytes 884744 | tf_op jit(solution)/shard_map/ppermute | solution.py:375
  30.4 4.1 %collective-permute-start.6 = (bf16[4,96,384]{2,1,0:T(8,128)(2,1)S(1)}, bf16[4,96,384]{2,1,0:T(8,128)(2,1)S(1)}, u32[]{:S(2)}, u32[]{:S(2)}) collective-permute-start(bf16[4,96,384]{2,1,0:T(8,128)(2,1)S(1)} %get-tuple-element.37.key_mine), channel_id=1, source_target_pairs={{0,1},{1,0},{2,3},{3,2},{4,5},{5,4},{6,7},{7,6},{8,9},{9,8},{10,11... | collective-permute-start | bytes 884744 | tf_op jit(solution)/shard_map/ppermute | solution.py:375
  32.3 2.2 %collective-permute-start.11 = (bf16[4,288,128]{2,1,0:T(8,128)(2,1)S(1)}, bf16[4,288,128]{2,1,0:T(8,128)(2,1)S(1)}, u32[]{:S(2)}, u32[]{:S(2)}) collective-permute-start(bf16[4,288,128]{2,1,0:T(8,128)(2,1)S(1)} %get-tuple-element.42.own_value), channel_id=1, source_target_pairs={{0,1},{1,0},{2,3},{3,2},{4,5},{5,4},{6,7},{7,6},{8,9},{9,8},{10,11... | collective-permute-start | bytes 884744 | tf_op jit(solution)/shard_map/ppermute | solution.py:375
  32.3 2.1 %collective-permute-start.10 = (bf16[4,256,128]{2,1,0:T(8,128)(2,1)S(1)}, bf16[4,256,128]{2,1,0:T(8,128)(2,1)S(1)}, u32[]{:S(2)}, u32[]{:S(2)}) collective-permute-start(bf16[4,256,128]{2,1,0:T(8,128)(2,1)S(1)} %get-tuple-element.41), channel_id=1, source_target_pairs={{0,1},{1,0},{2,3},{3,2},{4,5},{5,4},{6,7},{7,6},{8,9},{9,8},{10,11... | collective-permute-start | bytes 786440 | tf_op jit(solution)/shard_map/ppermute | solution.py:375
  32.9 9.1 %collective-permute-start.15 = (bf16[2,96,768]{2,1,0:T(8,128)(2,1)S(1)}, bf16[2,96,768]{2,1,0:T(8,128)(2,1)S(1)}, u32[]{:S(2)}, u32[]{:S(2)}) collective-permute-start(bf16[2,96,768]{2,1,0:T(8,128)(2,1)S(1)} %stack_output.1.refs_0_), channel_id=1, source_target_pairs={{0,16},{8,24},{16,0},{24,8},{1,17},{9,25},{17,1},{25,9},{2,18},{10... | collective-permute-start | bytes 884744 | tf_op jit(solution)/shard_map/ppermute | solution.py:394
  39.4 2.5 %copy-start = (bf16[4,64,768]{2,1,0:T(8,128)(2,1)S(1)}, bf16[4,64,768]{2,1,0:T(8,128)(2,1)}, u32[]{:S(2)}) copy-start(bf16[4,64,768]{2,1,0:T(8,128)(2,1)} %activations.3) | copy-start | bytes 1179652
  39.4 2.5 %copy-start.2 = (bf16[4,64,768]{2,1,0:T(8,128)(2,1)S(1)}, bf16[4,64,768]{2,1,0:T(8,128)(2,1)}, u32[]{:S(2)}) copy-start(bf16[4,64,768]{2,1,0:T(8,128)(2,1)} %output_gate.3) | copy-start | bytes 1179652
  39.5 2.5 %collective-permute-start.16 = (f32[1,400,128]{2,1,0:T(8,128)S(1)}, f32[1,400,128]{2,1,0:T(8,128)S(1)}, u32[]{:S(2)}, u32[]{:S(2)}) collective-permute-start(f32[1,400,128]{2,1,0:T(8,128)S(1)} %get-tuple-element.52), channel_id=1, source_target_pairs={{0,1},{1,0},{2,3},{3,2},{4,5},{5,4},{6,7},{7,6},{8,9},{9,8},{10,11... | collective-permute-start | bytes 614408 | tf_op jit(solution)/shard_map/ppermute | solution.py:375
  40.7 2.3 %collective-permute-start.14 = (f32[1,400,128]{2,1,0:T(8,128)S(1)}, f32[1,400,128]{2,1,0:T(8,128)S(1)}, u32[]{:S(2)}, u32[]{:S(2)}) collective-permute-start(f32[1,400,128]{2,1,0:T(8,128)S(1)} %get-tuple-element.49), channel_id=1, source_target_pairs={{0,1},{1,0},{2,3},{3,2},{4,5},{5,4},{6,7},{7,6},{8,9},{9,8},{10,11... | collective-permute-start | bytes 614408 | tf_op jit(solution)/shard_map/ppermute | solution.py:375

commit v5 on v4

--- a/solution.py
+++ b/solution.py
@@ -160,9 +160,25 @@
 def stack_kernel(first, *refs):
     stacks = [ref for ref in refs if len(ref.shape) == 3]
     for k, part in enumerate(refs[: -len(stacks)]):
+        rows, breadth = stacks[0].shape[1:]
+        tile = part.shape[1]
         for t, stack in enumerate(stacks):
-            breadth = stack.shape[2]
-            stack[k] = part[:, (first + t) * breadth : (first + t + 1) * breadth]
+            if tile >= breadth:
+                stack[k] = part[:, (first + t) * breadth : (first + t + 1) * breadth]
+                continue
+            tiles = breadth // tile
+            for i in range(tiles):
+                at = part.shape[0] - ((len(stacks) - t) * tiles - i) * rows
+                stack[k, :, i * tile : (i + 1) * tile] = part[at : at + rows]
+
+
+def join_kernel(parcel, part, joined):
+    rows, breadth = part.shape
+    below, tile = parcel.shape
+    joined[0:below] = parcel[...]
+    for t in range(breadth // tile):
+        at = below + t * rows
+        joined[at : at + rows] = part[:, t * tile : (t + 1) * tile]
 
 
 def spread_queries(heads, queries, spread):
@@ -394,11 +410,13 @@
     return lax.ppermute(array, "noise", [(i, i ^ k) for i in range(lax.axis_size("noise"))])
 
 
-def from_all_noise(own, direct, breadth):
+def from_all_noise(own, direct, third, breadth):
     parts = [own] + [None] * (2 ** len(direct) - 1)
     for k in range(1, len(parts)):
         low = k & -k
-        if low == k:
+        if k == 3:
+            parts[k] = third
+        elif low == k:
             parts[k] = direct[low.bit_length() - 1]
         else:
             parts[k] = from_noise(parts[k ^ low][:, :breadth], low)
@@ -467,8 +485,14 @@
     shifted_other = swap_cores(shifted)
     ring[1], direct, parcel, shifted_other = after((ring[1], direct, parcel, shifted_other))
     ring.append(next_chip(ring[1]))
-    parcels = [from_noise(parcel, k) for k in range(noise_size)]
-    weights = from_all_noise(extended, direct, 2 * head_features)
+    joined = pl.pallas_call(
+        join_kernel,
+        out_shape=struct((parcel.shape[0] + 2 * piece_rows, columns), bf16),
+        compiler_params=params,
+        name="join",
+    )(parcel, direct[1])
+    parcels = [parcel, from_noise(joined, 1)] + [from_noise(parcel, k) for k in range(2, noise_size)]
+    weights = from_all_noise(extended, direct, parcels[1], 2 * head_features)
     part_shape = (noise_size, half, head_features)
     query_mine, key_mine = pl.pallas_call(
         functools.partial(stack_kernel, 0),

time: 44.3 us -> 46.3 us (1.045)
  waiting for transfers between devices: 10.3 us -> 14.4 us
  starting transfers between devices: 17.3 us -> 15.2 us
    ppermute x7 -> x6, starting transfers between devices: 9.57 us -> 7.07 us  [from_noise(): lax.ppermute(array, 'noise', [(i, i ^ k) for i in range(lax.axis_size('no...]
    ppermute x7 -> x6, waiting for transfers between devices: 5.29 us -> 6.86 us  [from_noise(): lax.ppermute(array, 'noise', [(i, i ^ k) for i in range(lax.axis_size('no...]
    ppermute x3, waiting for transfers between devices: 5.03 us -> 6.42 us  [next_chip(): return lax.ppermute(array, 'row', pairs)]
    ppermute x7, waiting for transfers between devices: 0.02 us -> 1.11 us  [swap_cores(): lax.ppermute(array, 'row', [(i, i ^ 1) for i in range(lax.axis_size('row'...]
    ppermute x7, starting transfers between devices: 1.27 us -> 1.77 us  [swap_cores(): lax.ppermute(array, 'row', [(i, i ^ 1) for i in range(lax.axis_size('row'...]
  transfers between devices with their start and end apart: 17 -> 16, of which waited for: 7 -> 8; matrix products, arithmetic and copies ran while one was open for 0% -> 0% of each run, Pallas kernels for 21% -> 20%
where the time goes in v5:
time: 46.3 us; the launch traced here: 46.1 us
  starting transfers between devices  15.2 us (33%)
  waiting for transfers between devices  14.4 us (31%)
  Pallas kernels  13.1 us (28%)
  local copies, waits for them, and re-layouts  3.22 us (7%)
    ppermute x6, starting transfers between devices, from_noise(): lax.ppermute(array, 'noise', [(i, i ^ k) for i in range(lax.axis_size('no...  7.07 us
    ppermute x6, waiting for transfers between devices, from_noise(): lax.ppermute(array, 'noise', [(i, i ^ k) for i in range(lax.axis_size('no...  6.86 us
    ppermute x3, waiting for transfers between devices, next_chip(): return lax.ppermute(array, 'row', pairs)  6.42 us
    ppermute x3, starting transfers between devices, next_chip(): return lax.ppermute(array, 'row', pairs)  6.4 us
    pallas_call x1, Pallas kernels, body(): pl.pallas_call(functools.partial(early_kernel, steps, heads), out_shape=[...  3.7 us
    unnamed x18, local copies, waits for them, and re-layouts  3.21 us
    pallas_call x1, Pallas kernels, body(): pl.pallas_call(shift_kernel, in_specs=[in_hbm] * 7, out_specs=[in_hbm] *...  2.92 us
    pallas_call x2, Pallas kernels, body(): pl.pallas_call(functools.partial(late_kernel, steps, heads, c * each), ou...  2.35 us
  transfers between devices with their start and end apart: 16, of which 8 were waited for; matrix products, arithmetic and copies ran while one was open for 0% of the time, Pallas kernels for 20%

profile of v5, /device:TPU:0, one launch (start us, length us, event | category | flops | bytes accessed | tf_op | source)
XLA Modules:
  0.0 46.1 jit_solution(1713508966640993962)
XLA Ops:
  0.0 2.9 %shift.1 = (bf16[4,64,768]{2,1,0:T(8,128)(2,1)}, bf16[4,64,768]{2,1,0:T(8,128)(2,1)}, bf16[96,768]{1,0:T(8,128)(2,1)}, bf16[96,1536]{1,0:T(8,128)(2,1)}) custom-call(bf16[4,64,768]{2,1,0:T(8,128)(2,1)} %activations.3, bf16[4,64,768]{2,1,0:T(8,128)(2,1)} %scale_hbm.1, bf16[4,64,768]{2,1,0:T(8,128)(2,1)} %shift_hbm.1, s32[4,64]{1,0:T(4,128)} %mask_hbm.1, ...), custom_call_target="tpu_custom_call" | custom-call | tf_op jit(solution)/shard_map/shift/pallas_call | solution.py:455
  2.9 3.1 %collective-permute-start = (bf16[4,64,768]{2,1,0:T(8,128)(2,1)}, bf16[4,64,768]{2,1,0:T(8,128)(2,1)S(1)}, u32[]{:S(2)}, u32[]{:S(2)}) collective-permute-start(bf16[4,64,768]{2,1,0:T(8,128)(2,1)} %get-tuple-element.30.refs_0_), channel_id=1, source_target_pairs={{0,2},{1,3},{2,6},{3,7},{6,4},{7,5},{4,0},{5,1},{8,10},{9,11},{10,... | collective-permute-start | bytes 1179656 | tf_op jit(solution)/shard_map/ppermute | solution.py:404
  6.0 0.0 collective-permute-start.3
  6.0 1.5 %collective-permute-start.1 = (bf16[96,1536]{1,0:T(8,128)(2,1)}, bf16[96,1536]{1,0:T(8,128)(2,1)S(1)}, u32[]{:S(2)}, u32[]{:S(2)}) collective-permute-start(bf16[96,1536]{1,0:T(8,128)(2,1)} %get-tuple-element.29.refs_0_), channel_id=1, source_target_pairs={{0,8},{8,0},{16,24},{24,16},{1,9},{9,1},{17,25},{25,17},{2,10},{10... | collective-permute-start | bytes 884744 | tf_op jit(solution)/shard_map/ppermute | solution.py:410
  7.5 1.5 %collective-permute-start.2 = (bf16[96,768]{1,0:T(8,128)(2,1)}, bf16[96,768]{1,0:T(8,128)(2,1)S(1)}, u32[]{:S(2)}, u32[]{:S(2)}) collective-permute-start(bf16[96,768]{1,0:T(8,128)(2,1)} %get-tuple-element.31), channel_id=1, source_target_pairs={{0,16},{8,24},{16,0},{24,8},{1,17},{9,25},{17,1},{25,9},{2,18},{10... | collective-permute-start | bytes 442376 | tf_op jit(solution)/shard_map/ppermute | solution.py:410
  9.0 0.0 copy-start.1
  9.0 1.6 %copy-done.1 = bf16[64,128,128]{2,1,0:T(8,128)(2,1)S(1)} copy-done((bf16[64,128,128]{2,1,0:T(8,128)(2,1)S(1)}, bf16[64,128,128]{2,1,0:T(8,128)(2,1)}, u32[]{:S(2)}) %copy-start.1) | copy-done | bytes 2097176
  10.6 0.0 copy-start.6
  10.6 0.9 %copy-done.6 = bf16[192,384]{1,0:T(8,128)(2,1)S(1)} copy-done((bf16[192,384]{1,0:T(8,128)(2,1)S(1)}, bf16[192,384]{1,0:T(8,128)(2,1)}, u32[]{:S(2)}) %copy-start.6) | copy-done | bytes 147480
  11.5 0.0 copy-start.7
  11.5 0.7 %copy-done.7 = bf16[128,8]{0,1:T(8,128)(2,1)S(1)} copy-done((bf16[128,8]{0,1:T(8,128)(2,1)S(1)}, bf16[128,8]{0,1:T(8,128)(2,1)}, u32[]{:S(2)}) %copy-start.7) | copy-done | bytes 2072
  12.2 0.0 copy-start.3
  12.2 1.9 %bias.1.parcel.refs_0_ = bf16[800,128]{1,0:T(8,128)(2,1)S(1)} custom-call(bf16[64,128,128]{2,1,0:T(8,128)(2,1)S(1)} %copy-done.1, bf16[192,384]{1,0:T(8,128)(2,1)S(1)} %copy-done.6, bf16[8,128]{1,0:T(8,128)(2,1)S(1)} %bitcast.1), custom_call_target="tpu_custom_call" | custom-call | tf_op jit(solution)/shard_map/bias/pallas_call | solution.py:478
  14.1 0.0 copy-start.8
  14.1 0.0 copy-start.4
  14.1 0.0 copy-start.5
  14.1 0.0 collective-permute-done.2.part.refs_2_
  14.1 1.5 %collective-permute-done.1.refs_1_ = bf16[96,1536]{1,0:T(8,128)(2,1)S(1)} collective-permute-done((bf16[96,1536]{1,0:T(8,128)(2,1)}, bf16[96,1536]{1,0:T(8,128)(2,1)S(1)}, u32[]{:S(2)}, u32[]{:S(2)}) %collective-permute-start.1) | collective-permute-done | bytes 294944 | tf_op jit(solution)/shard_map/ppermute | solution.py:410
  15.6 0.7 %collective-permute-done.refs_1_ = bf16[4,64,768]{2,1,0:T(8,128)(2,1)S(1)} collective-permute-done((bf16[4,64,768]{2,1,0:T(8,128)(2,1)}, bf16[4,64,768]{2,1,0:T(8,128)(2,1)S(1)}, u32[]{:S(2)}, u32[]{:S(2)}) %collective-permute-start) | collective-permute-done | bytes 393248 | tf_op jit(solution)/shard_map/ppermute | solution.py:404
  16.3 0.0 collective-permute-done.3.shifted_other
  16.3 1.9 %collective-permute-start.11 = (bf16[4,64,768]{2,1,0:T(8,128)(2,1)S(1)}, bf16[4,64,768]{2,1,0:T(8,128)(2,1)S(1)}, u32[]{:S(2)}, u32[]{:S(2)}) collective-permute-start(bf16[4,64,768]{2,1,0:T(8,128)(2,1)S(1)} %collective-permute-done.refs_1_), channel_id=1, source_target_pairs={{0,2},{1,3},{2,6},{3,7},{6,4},{7,5},{4,0},{5,1},{8,10},{9,11},{10,... | collective-permute-start | bytes 1179656 | tf_op jit(solution)/shard_map/ppermute | solution.py:404
  18.3 1.6 %collective-permute-start.4 = (bf16[1376,128]{1,0:T(8,128)(2,1)S(1)}, bf16[1376,128]{1,0:T(8,128)(2,1)S(1)}, u32[]{:S(2)}, u32[]{:S(2)}) collective-permute-start(bf16[1376,128]{1,0:T(8,128)(2,1)S(1)} %join.1), channel_id=1, source_target_pairs={{0,8},{8,0},{16,24},{24,16},{1,9},{9,1},{17,25},{25,17},{2,10},{10... | collective-permute-start | bytes 1056776 | tf_op jit(solution)/shard_map/ppermute | solution.py:410
  19.8 1.5 %collective-permute-start.8 = (bf16[800,128]{1,0:T(8,128)(2,1)S(1)}, bf16[800,128]{1,0:T(8,128)(2,1)S(1)}, u32[]{:S(2)}, u32[]{:S(2)}) collective-permute-start(bf16[800,128]{1,0:T(8,128)(2,1)S(1)} %bias.1.parcel.refs_0_), channel_id=1, source_target_pairs={{0,24},{8,16},{16,8},{24,0},{1,25},{9,17},{17,9},{25,1},{2,26},{10... | collective-permute-start | bytes 614408 | tf_op jit(solution)/shard_map/ppermute | solution.py:410
  21.3 0.5 %collective-permute-start.7 = (bf16[800,128]{1,0:T(8,128)(2,1)S(1)}, bf16[800,128]{1,0:T(8,128)(2,1)S(1)}, u32[]{:S(2)}, u32[]{:S(2)}) collective-permute-start(bf16[800,128]{1,0:T(8,128)(2,1)S(1)} %bias.1.parcel.refs_0_), channel_id=1, source_target_pairs={{0,16},{8,24},{16,0},{24,8},{1,17},{9,25},{17,1},{25,9},{2,18},{10... | collective-permute-start | bytes 614408 | tf_op jit(solution)/shard_map/ppermute | solution.py:410
  21.8 5.7 %collective-permute-done.11.refs_2_ = bf16[4,64,768]{2,1,0:T(8,128)(2,1)S(1)} collective-permute-done((bf16[4,64,768]{2,1,0:T(8,128)(2,1)S(1)}, bf16[4,64,768]{2,1,0:T(8,128)(2,1)S(1)}, u32[]{:S(2)}, u32[]{:S(2)}) %collective-permute-start.11) | collective-permute-done | bytes 393248 | tf_op jit(solution)/shard_map/ppermute | solution.py:404
  27.5 1.4 %collective-permute-start.12 = (bf16[4,64,768]{2,1,0:T(8,128)(2,1)S(1)}, bf16[4,64,768]{2,1,0:T(8,128)(2,1)S(1)}, u32[]{:S(2)}, u32[]{:S(2)}) collective-permute-start(bf16[4,64,768]{2,1,0:T(8,128)(2,1)S(1)} %collective-permute-done.11.refs_2_), channel_id=1, source_target_pairs={{0,2},{1,3},{2,6},{3,7},{6,4},{7,5},{4,0},{5,1},{8,10},{9,11},{10,... | collective-permute-start | bytes 1179656 | tf_op jit(solution)/shard_map/ppermute | solution.py:404
  29.0 4.3 %collective-permute-done.8.refs_3_ = bf16[800,128]{1,0:T(8,128)(2,1)S(1)} collective-permute-done((bf16[800,128]{1,0:T(8,128)(2,1)S(1)}, bf16[800,128]{1,0:T(8,128)(2,1)S(1)}, u32[]{:S(2)}, u32[]{:S(2)}) %collective-permute-start.8) | collective-permute-done | bytes 204832 | tf_op jit(solution)/shard_map/ppermute | solution.py:410
  33.3 0.0 collective-permute-done.7.refs_2_
  33.3 0.0 collective-permute-done.4.refs_3_.refs_1_
  33.3 0.1 sort.1
  33.3 0.1 collective-permute-start.9
  33.4 0.0 copy-done.3
  33.4 0.1 stack.1
  33.5 0.5 %collective-permute-start.5 = (bf16[4,96,384]{2,1,0:T(8,128)(2,1)S(1)}, bf16[4,96,384]{2,1,0:T(8,128)(2,1)S(1)}, u32[]{:S(2)}, u32[]{:S(2)}) collective-permute-start(bf16[4,96,384]{2,1,0:T(8,128)(2,1)S(1)} %get-tuple-element.37.query_mine), channel_id=1, source_target_pairs={{0,1},{1,0},{2,3},{3,2},{4,5},{5,4},{6,7},{7,6},{8,9},{9,8},{10,11... | collective-permute-start | bytes 884744 | tf_op jit(solution)/shard_map/ppermute | solution.py:391
  34.1 0.1 collective-permute-start.6
  34.1 0.4 collective-permute-start.10
  34.6 0.4 collective-permute-done.9.swapped
  34.9 0.5 %collective-permute-start.14 = (bf16[2,96,768]{2,1,0:T(8,128)(2,1)S(1)}, bf16[2,96,768]{2,1,0:T(8,128)(2,1)S(1)}, u32[]{:S(2)}, u32[]{:S(2)}) collective-permute-start(bf16[2,96,768]{2,1,0:T(8,128)(2,1)S(1)} %stack_output.1.refs_0_), channel_id=1, source_target_pairs={{0,16},{8,24},{16,0},{24,8},{1,17},{9,25},{17,1},{25,9},{2,18},{10... | collective-permute-start | bytes 884744 | tf_op jit(solution)/shard_map/ppermute | solution.py:410
  35.5 0.0 copy-done.8
  35.5 0.0 collective-permute-done.5.query_other
  35.5 0.3 collective-permute-done.6.key_other
  35.8 0.4 collective-permute-done.10.swapped_value
  36.2 0.0 copy-done.4
  36.2 0.0 copy-done.5
  36.2 3.7 %early.1 = (f32[4,400,128]{2,1,0:T(8,128)S(1)}, bf16[4,128,384]{2,1,0:T(8,128)(2,1)S(1)}, bf16[768,384]{1,0:T(8,128)(2,1)S(1)}, bf16[384,768]{1,0:T(8,128)(2,1)S(1)}) custom-call(bf16[4,96,384]{2,1,0:T(8,128)(2,1)S(1)} %get-tuple-element.37.query_mine, bf16[4,96,384]{2,1,0:T(8,128)(2,1)S(1)} %get-tuple-element.38.key_mine, ...), custom_call_target="tpu_custom_call" | custom-call | tf_op jit(solution)/shard_map/early/pallas_call | solution.py:530
  39.9 0.0 collective-permute-done.12.block
  39.9 1.2 %late.3 = (f32[1,400,128]{2,1,0:T(8,128)S(1)}, f32[1,400,128]{2,1,0:T(8,128)S(1)}) custom-call(f32[4,400,128]{2,1,0:T(8,128)S(1)} %get-tuple-element.44.partial, bf16[4,128,384]{2,1,0:T(8,128)(2,1)S(1)} %get-tuple-element.45.queries, bf16[768,384]{1,0:T(8,128)(2,1)S(1)} %get-tuple-element.46.key_weight, bf16[384,768]{1,0:T(8,128)(2,1)S(1)} %get-tuple-element.47.value_weight, ...), custom_call_target="tpu_custom_call" | custom-call | tf_op jit(solution)/shard_map/late/pallas_call | solution.py:554
  41.1 0.0 copy-start
  41.1 0.0 copy-start.2
  41.1 0.3 collective-permute-start.15
  41.5 1.2 %late.2 = (f32[1,400,128]{2,1,0:T(8,128)S(1)}, f32[1,400,128]{2,1,0:T(8,128)S(1)}) custom-call(f32[4,400,128]{2,1,0:T(8,128)S(1)} %get-tuple-element.44.partial, bf16[4,128,384]{2,1,0:T(8,128)(2,1)S(1)} %get-tuple-element.45.queries, bf16[768,384]{1,0:T(8,128)(2,1)S(1)} %get-tuple-element.46.key_weight, bf16[384,768]{1,0:T(8,128)(2,1)S(1)} %get-tuple-element.47.value_weight, ...), custom_call_target="tpu_custom_call" | custom-call | tf_op jit(solution)/shard_map/late/pallas_call | solution.py:554
  42.6 0.3 collective-permute-start.13
  43.0 1.0 %collective-permute-done.14.refs_1_ = bf16[2,96,768]{2,1,0:T(8,128)(2,1)S(1)} collective-permute-done((bf16[2,96,768]{2,1,0:T(8,128)(2,1)S(1)}, bf16[2,96,768]{2,1,0:T(8,128)(2,1)S(1)}, u32[]{:S(2)}, u32[]{:S(2)}) %collective-permute-start.14) | collective-permute-done | bytes 294944 | tf_op jit(solution)/shard_map/ppermute | solution.py:410
  44.0 0.0 collective-permute-done.15.got
  44.0 0.0 copy-done
  44.0 0.0 copy-done.2
  44.0 1.0 %finish.2.refs_2_ = bf16[4,64,768]{2,1,0:T(8,128)(2,1)} custom-call(bf16[4,64,768]{2,1,0:T(8,128)(2,1)S(1)} %copy-done, bf16[4,64,768]{2,1,0:T(8,128)(2,1)S(1)} %copy-done.2, f32[1,400,128]{2,1,0:T(8,128)S(1)} %get-tuple-element.51.keep, f32[1,400,128]{2,1,0:T(8,128)S(1)} %collective-permute-done.15.got, bf16[2,96,768]{2,1,0:T(8,128)(2,1)S(1)} %stack_output.1.refs_0_, ...), custom_call_target="tpu_custom_call" | custom-call | tf_op jit(solution)/shard_map/finish/pallas_call | solution.py:567
  45.1 0.0 collective-permute-done.13.got
  45.1 1.0 %finish.3 = bf16[4,64,768]{2,1,0:T(8,128)(2,1)} custom-call(bf16[4,64,768]{2,1,0:T(8,128)(2,1)S(1)} %copy-done, bf16[4,64,768]{2,1,0:T(8,128)(2,1)S(1)} %copy-done.2, f32[1,400,128]{2,1,0:T(8,128)S(1)} %get-tuple-element.48.keep, f32[1,400,128]{2,1,0:T(8,128)S(1)} %collective-permute-done.13.got, ...), custom_call_target="tpu_custom_call", output_to_operand_aliasing={{}: (6, {})} | custom-call | tf_op jit(solution)/shard_map/finish/pallas_call | solution.py:567
  (3 shorter events, 0.1 us)
Async XLA Ops:
  2.9 13.4 %collective-permute-start = (bf16[4,64,768]{2,1,0:T(8,128)(2,1)}, bf16[4,64,768]{2,1,0:T(8,128)(2,1)S(1)}, u32[]{:S(2)}, u32[]{:S(2)}) collective-permute-start(bf16[4,64,768]{2,1,0:T(8,128)(2,1)} %get-tuple-element.30.refs_0_), channel_id=1, source_target_pairs={{0,2},{1,3},{2,6},{3,7},{6,4},{7,5},{4,0},{5,1},{8,10},{9,11},{10,... | collective-permute-start | bytes 1179656 | tf_op jit(solution)/shard_map/ppermute | solution.py:404
  6.0 10.3 %collective-permute-start.3 = (bf16[4,64,768]{2,1,0:T(8,128)(2,1)}, bf16[4,64,768]{2,1,0:T(8,128)(2,1)S(1)}, u32[]{:S(2)}, u32[]{:S(2)}) collective-permute-start(bf16[4,64,768]{2,1,0:T(8,128)(2,1)} %get-tuple-element.33.shifted), channel_id=1, source_target_pairs={{0,1},{1,0},{2,3},{3,2},{4,5},{5,4},{6,7},{7,6},{8,9},{9,8},{10,11... | collective-permute-start | bytes 1179656 | tf_op jit(solution)/shard_map/ppermute | solution.py:391
  6.0 9.6 %collective-permute-start.1 = (bf16[96,1536]{1,0:T(8,128)(2,1)}, bf16[96,1536]{1,0:T(8,128)(2,1)S(1)}, u32[]{:S(2)}, u32[]{:S(2)}) collective-permute-start(bf16[96,1536]{1,0:T(8,128)(2,1)} %get-tuple-element.29.refs_0_), channel_id=1, source_target_pairs={{0,8},{8,0},{16,24},{24,16},{1,9},{9,1},{17,25},{25,17},{2,10},{10... | collective-permute-start | bytes 884744 | tf_op jit(solution)/shard_map/ppermute | solution.py:410
  7.5 6.6 %collective-permute-start.2 = (bf16[96,768]{1,0:T(8,128)(2,1)}, bf16[96,768]{1,0:T(8,128)(2,1)S(1)}, u32[]{:S(2)}, u32[]{:S(2)}) collective-permute-start(bf16[96,768]{1,0:T(8,128)(2,1)} %get-tuple-element.31), channel_id=1, source_target_pairs={{0,16},{8,24},{16,0},{24,8},{1,17},{9,25},{17,1},{25,9},{2,18},{10... | collective-permute-start | bytes 442376 | tf_op jit(solution)/shard_map/ppermute | solution.py:410
  9.0 1.6 %copy-start.1 = (bf16[64,128,128]{2,1,0:T(8,128)(2,1)S(1)}, bf16[64,128,128]{2,1,0:T(8,128)(2,1)}, u32[]{:S(2)}) copy-start(bf16[64,128,128]{2,1,0:T(8,128)(2,1)} %pair.1) | copy-start | bytes 6291460
  10.6 0.9 %copy-start.6 = (bf16[192,384]{1,0:T(8,128)(2,1)S(1)}, bf16[192,384]{1,0:T(8,128)(2,1)}, u32[]{:S(2)}) copy-start(bf16[192,384]{1,0:T(8,128)(2,1)} %value_weight.1) | copy-start | bytes 442372
  11.5 0.7 %copy-start.7 = (bf16[128,8]{0,1:T(8,128)(2,1)S(1)}, bf16[128,8]{0,1:T(8,128)(2,1)}, u32[]{:S(2)}) copy-start(bf16[128,8]{0,1:T(8,128)(2,1)} %param.17) | copy-start | bytes 6148
  12.2 21.2 %copy-start.3 = (bf16[96,1536]{1,0:T(8,128)(2,1)S(1)}, bf16[96,1536]{1,0:T(8,128)(2,1)}, u32[]{:S(2)}) copy-start(bf16[96,1536]{1,0:T(8,128)(2,1)} %get-tuple-element.29.refs_0_) | copy-start | bytes 884740
  14.1 21.4 %copy-start.8 = (bf16[384]{0:T(512)(128)(2,1)S(1)}, bf16[384]{0:T(512)(128)(2,1)}, u32[]{:S(2)}) copy-start(bf16[384]{0:T(512)(128)(2,1)} %param.19) | copy-start | bytes 2308
  14.1 22.1 %copy-start.4 = (bf16[4,64,768]{2,1,0:T(8,128)(2,1)S(1)}, bf16[4,64,768]{2,1,0:T(8,128)(2,1)}, u32[]{:S(2)}) copy-start(bf16[4,64,768]{2,1,0:T(8,128)(2,1)} %get-tuple-element.33.shifted) | copy-start | bytes 1179652
  14.1 22.1 %copy-start.5 = (bf16[4,64,768]{2,1,0:T(8,128)(2,1)S(1)}, bf16[4,64,768]{2,1,0:T(8,128)(2,1)}, u32[]{:S(2)}) copy-start(bf16[4,64,768]{2,1,0:T(8,128)(2,1)} %get-tuple-element.30.refs_0_) | copy-start | bytes 1179652
  16.3 11.2 %collective-permute-start.11 = (bf16[4,64,768]{2,1,0:T(8,128)(2,1)S(1)}, bf16[4,64,768]{2,1,0:T(8,128)(2,1)S(1)}, u32[]{:S(2)}, u32[]{:S(2)}) collective-permute-start(bf16[4,64,768]{2,1,0:T(8,128)(2,1)S(1)} %collective-permute-done.refs_1_), channel_id=1, source_target_pairs={{0,2},{1,3},{2,6},{3,7},{6,4},{7,5},{4,0},{5,1},{8,10},{9,11},{10,... | collective-permute-start | bytes 1179656 | tf_op jit(solution)/shard_map/ppermute | solution.py:404
  18.3 15.0 %collective-permute-start.4 = (bf16[1376,128]{1,0:T(8,128)(2,1)S(1)}, bf16[1376,128]{1,0:T(8,128)(2,1)S(1)}, u32[]{:S(2)}, u32[]{:S(2)}) collective-permute-start(bf16[1376,128]{1,0:T(8,128)(2,1)S(1)} %join.1), channel_id=1, source_target_pairs={{0,8},{8,0},{16,24},{24,16},{1,9},{9,1},{17,25},{25,17},{2,10},{10... | collective-permute-start | bytes 1056776 | tf_op jit(solution)/shard_map/ppermute | solution.py:410
  19.8 13.4 %collective-permute-start.8 = (bf16[800,128]{1,0:T(8,128)(2,1)S(1)}, bf16[800,128]{1,0:T(8,128)(2,1)S(1)}, u32[]{:S(2)}, u32[]{:S(2)}) collective-permute-start(bf16[800,128]{1,0:T(8,128)(2,1)S(1)} %bias.1.parcel.refs_0_), channel_id=1, source_target_pairs={{0,24},{8,16},{16,8},{24,0},{1,25},{9,17},{17,9},{25,1},{2,26},{10... | collective-permute-start | bytes 614408 | tf_op jit(solution)/shard_map/ppermute | solution.py:410
  21.3 12.0 %collective-permute-start.7 = (bf16[800,128]{1,0:T(8,128)(2,1)S(1)}, bf16[800,128]{1,0:T(8,128)(2,1)S(1)}, u32[]{:S(2)}, u32[]{:S(2)}) collective-permute-start(bf16[800,128]{1,0:T(8,128)(2,1)S(1)} %bias.1.parcel.refs_0_), channel_id=1, source_target_pairs={{0,16},{8,24},{16,0},{24,8},{1,17},{9,25},{17,1},{25,9},{2,18},{10... | collective-permute-start | bytes 614408 | tf_op jit(solution)/shard_map/ppermute | solution.py:410
  27.5 12.4 %collective-permute-start.12 = (bf16[4,64,768]{2,1,0:T(8,128)(2,1)S(1)}, bf16[4,64,768]{2,1,0:T(8,128)(2,1)S(1)}, u32[]{:S(2)}, u32[]{:S(2)}) collective-permute-start(bf16[4,64,768]{2,1,0:T(8,128)(2,1)S(1)} %collective-permute-done.11.refs_2_), channel_id=1, source_target_pairs={{0,2},{1,3},{2,6},{3,7},{6,4},{7,5},{4,0},{5,1},{8,10},{9,11},{10,... | collective-permute-start | bytes 1179656 | tf_op jit(solution)/shard_map/ppermute | solution.py:404
  33.3 1.6 %collective-permute-start.9 = (bf16[4,256,128]{2,1,0:T(8,128)(2,1)S(1)}, bf16[4,256,128]{2,1,0:T(8,128)(2,1)S(1)}, u32[]{:S(2)}, u32[]{:S(2)}) collective-permute-start(bf16[4,256,128]{2,1,0:T(8,128)(2,1)S(1)} %get-tuple-element.41), channel_id=1, source_target_pairs={{0,1},{1,0},{2,3},{3,2},{4,5},{5,4},{6,7},{7,6},{8,9},{9,8},{10,11... | collective-permute-start | bytes 786440 | tf_op jit(solution)/shard_map/ppermute | solution.py:391
  33.5 2.0 %collective-permute-start.5 = (bf16[4,96,384]{2,1,0:T(8,128)(2,1)S(1)}, bf16[4,96,384]{2,1,0:T(8,128)(2,1)S(1)}, u32[]{:S(2)}, u32[]{:S(2)}) collective-permute-start(bf16[4,96,384]{2,1,0:T(8,128)(2,1)S(1)} %get-tuple-element.37.query_mine), channel_id=1, source_target_pairs={{0,1},{1,0},{2,3},{3,2},{4,5},{5,4},{6,7},{7,6},{8,9},{9,8},{10,11... | collective-permute-start | bytes 884744 | tf_op jit(solution)/shard_map/ppermute | solution.py:391
  34.1 1.7 %collective-permute-start.6 = (bf16[4,96,384]{2,1,0:T(8,128)(2,1)S(1)}, bf16[4,96,384]{2,1,0:T(8,128)(2,1)S(1)}, u32[]{:S(2)}, u32[]{:S(2)}) collective-permute-start(bf16[4,96,384]{2,1,0:T(8,128)(2,1)S(1)} %get-tuple-element.38.key_mine), channel_id=1, source_target_pairs={{0,1},{1,0},{2,3},{3,2},{4,5},{5,4},{6,7},{7,6},{8,9},{9,8},{10,11... | collective-permute-start | bytes 884744 | tf_op jit(solution)/shard_map/ppermute | solution.py:391
  34.1 2.1 %collective-permute-start.10 = (bf16[4,288,128]{2,1,0:T(8,128)(2,1)S(1)}, bf16[4,288,128]{2,1,0:T(8,128)(2,1)S(1)}, u32[]{:S(2)}, u32[]{:S(2)}) collective-permute-start(bf16[4,288,128]{2,1,0:T(8,128)(2,1)S(1)} %get-tuple-element.42.own_value), channel_id=1, source_target_pairs={{0,1},{1,0},{2,3},{3,2},{4,5},{5,4},{6,7},{7,6},{8,9},{9,8},{10,11... | collective-permute-start | bytes 884744 | tf_op jit(solution)/shard_map/ppermute | solution.py:391
  34.9 9.1 %collective-permute-start.14 = (bf16[2,96,768]{2,1,0:T(8,128)(2,1)S(1)}, bf16[2,96,768]{2,1,0:T(8,128)(2,1)S(1)}, u32[]{:S(2)}, u32[]{:S(2)}) collective-permute-start(bf16[2,96,768]{2,1,0:T(8,128)(2,1)S(1)} %stack_output.1.refs_0_), channel_id=1, source_target_pairs={{0,16},{8,24},{16,0},{24,8},{1,17},{9,25},{17,1},{25,9},{2,18},{10... | collective-permute-start | bytes 884744 | tf_op jit(solution)/shard_map/ppermute | solution.py:410
  41.1 2.9 %copy-start = (bf16[4,64,768]{2,1,0:T(8,128)(2,1)S(1)}, bf16[4,64,768]{2,1,0:T(8,128)(2,1)}, u32[]{:S(2)}) copy-start(bf16[4,64,768]{2,1,0:T(8,128)(2,1)} %activations.3) | copy-start | bytes 1179652
  41.1 2.9 %copy-start.2 = (bf16[4,64,768]{2,1,0:T(8,128)(2,1)S(1)}, bf16[4,64,768]{2,1,0:T(8,128)(2,1)}, u32[]{:S(2)}) copy-start(bf16[4,64,768]{2,1,0:T(8,128)(2,1)} %output_gate.3) | copy-start | bytes 1179652
  41.1 2.9 %collective-permute-start.15 = (f32[1,400,128]{2,1,0:T(8,128)S(1)}, f32[1,400,128]{2,1,0:T(8,128)S(1)}, u32[]{:S(2)}, u32[]{:S(2)}) collective-permute-start(f32[1,400,128]{2,1,0:T(8,128)S(1)} %get-tuple-element.52), channel_id=1, source_target_pairs={{0,1},{1,0},{2,3},{3,2},{4,5},{5,4},{6,7},{7,6},{8,9},{9,8},{10,11... | collective-permute-start | bytes 614408 | tf_op jit(solution)/shard_map/ppermute | solution.py:391
  42.6 2.4 %collective-permute-start.13 = (f32[1,400,128]{2,1,0:T(8,128)S(1)}, f32[1,400,128]{2,1,0:T(8,128)S(1)}, u32[]{:S(2)}, u32[]{:S(2)}) collective-permute-start(f32[1,400,128]{2,1,0:T(8,128)S(1)} %get-tuple-element.49), channel_id=1, source_target_pairs={{0,1},{1,0},{2,3},{3,2},{4,5},{5,4},{6,7},{7,6},{8,9},{9,8},{10,11... | collective-permute-start | bytes 614408 | tf_op jit(solution)/shard_map/ppermute | solution.py:391

commit v6 on v4

--- a/solution.py
+++ b/solution.py
@@ -33,7 +33,6 @@
     output_hbm,
     shifted_hbm,
     sent_hbm,
-    packed_hbm,
     extended_hbm,
     shifted,
     sent,
@@ -49,22 +48,35 @@
     sems_out,
 ):
     samples, rows, features = activations.shape
+    weights = ((query_hbm, query_weight), (key_hbm, key_weight), (output_hbm, output_weight))
+    weight_copies = [
+        pltpu.make_async_copy(source, target, sems.at[1 + 3 * samples + w])
+        for w, (source, target) in enumerate(weights)
+    ]
     copies = [pltpu.make_async_copy(mask_hbm, token_mask, sems.at[0])]
     for s in range(samples):
         for t, (source, target) in enumerate(
             ((activations_hbm, activations), (scale_hbm, cond_scale), (shift_hbm, cond_shift))
         ):
             copies.append(pltpu.make_async_copy(source.at[s], target.at[s], sems.at[1 + 3 * s + t]))
-    copies.append(pltpu.make_async_copy(query_hbm, query_weight, sems.at[1 + 3 * samples]))
-    copies.append(pltpu.make_async_copy(key_hbm, key_weight, sems.at[2 + 3 * samples]))
-    copies.append(pltpu.make_async_copy(output_hbm, output_weight, sems.at[3 + 3 * samples]))
-    for copy in copies:
+    for copy in weight_copies + copies:
         copy.start()
     diagonal = lax.broadcasted_iota(jnp.int32, (rows, rows), 0) == lax.broadcasted_iota(
         jnp.int32, (rows, rows), 1
     )
+    core = lax.rem(lax.axis_index("row"), 2)
+    half, breadth = extended.shape[0], query_weight.shape[1]
+    for copy in weight_copies:
+        copy.wait()
+    for w, weight in enumerate((query_weight, key_weight)):
+        whole = weight[...].astype(jnp.float32)
+        extended[:, w * breadth : (w + 1) * breadth] = jnp.where(
+            core == 0, whole[:half], whole[half:]
+        ).astype(jnp.bfloat16)
+    extended[:, 2 * breadth :] = output_weight[...]
+    written = [pltpu.make_async_copy(extended, extended_hbm, sems_out.at[2 * samples])]
+    written[0].start()
     copies[0].wait()
-    written = []
     for s in range(samples):
         for copy in copies[1 + 3 * s : 4 + 3 * s]:
             copy.wait()
@@ -77,24 +89,6 @@
         for t, (source, target) in enumerate(((sent, sent_hbm), (shifted, shifted_hbm))):
             written.append(pltpu.make_async_copy(source.at[s], target.at[s], sems_out.at[2 * s + t]))
             written[-1].start()
-    core = lax.rem(lax.axis_index("row"), 2)
-    half, breadth = packed_hbm.shape[0], query_weight.shape[1]
-    for w, weight in enumerate((query_weight, key_weight)):
-        copies[1 + 3 * samples + w].wait()
-        whole = weight[...].astype(jnp.float32)
-        extended[0:half, w * breadth : (w + 1) * breadth] = jnp.where(
-            core == 0, whole[:half], whole[half:]
-        ).astype(jnp.bfloat16)
-    written.append(
-        pltpu.make_async_copy(
-            extended.at[0:half, 0 : 2 * breadth], packed_hbm, sems_out.at[2 * samples]
-        )
-    )
-    written[-1].start()
-    copies[-1].wait()
-    extended[:, 2 * breadth :] = output_weight[...]
-    written.append(pltpu.make_async_copy(extended, extended_hbm, sems_out.at[2 * samples + 1]))
-    written[-1].start()
     for copy in written:
         copy.wait()
 
@@ -332,8 +326,11 @@
 
 
 def finish_kernel(heads, first, groups, activations, output_gate, keep, got, *refs):
-    output_parts = [group.at[k] for group in refs[:groups] for k in range(group.shape[0])]
+    direct, *arrived = refs[:groups]
     updated_hbm, updated, output_weight, sems = refs[-4:]
+    output_parts = [direct.at[0]]
+    for k in range(1, 2 ** (direct.shape[0] - 1)):
+        output_parts.append(arrived.pop(0) if k & (k - 1) else direct.at[k.bit_length()])
     part_rows = output_parts[0].shape[0]
     breadth = output_weight.shape[0]
     width = breadth // heads
@@ -432,28 +429,28 @@
     half = query_weight.shape[0] // 2
 
     in_hbm = pl.BlockSpec(memory_space=pltpu.HBM)
-    packed_shape, extended_shape = (half, 2 * head_features), (half, 2 * head_features + features)
+    extended_shape = (half, 2 * head_features + features)
     assert output_weight.shape == (half, 2 * head_features)
-    shifted, sent, packed, extended = pl.pallas_call(
+    shifted, sent, extended = pl.pallas_call(
         shift_kernel,
         in_specs=[in_hbm] * 7,
-        out_specs=[in_hbm] * 4,
+        out_specs=[in_hbm] * 3,
         out_shape=[struct(activations.shape, bf16)] * 2
-        + [struct(packed_shape, bf16), struct(extended_shape, bf16)],
+        + [struct(extended_shape, bf16)],
         scratch_shapes=[pltpu.VMEM(activations.shape, bf16)] * 2
         + [pltpu.VMEM(extended_shape, bf16)]
         + [pltpu.VMEM(activations.shape, bf16)] * 3
         + [pltpu.VMEM(token_mask.shape, jnp.int32)]
         + [pltpu.VMEM(query_weight.shape, bf16)] * 2
         + [pltpu.VMEM(output_weight.shape, bf16)]
-        + [pltpu.SemaphoreType.DMA((3 * samples + 4,)), pltpu.SemaphoreType.DMA((2 * samples + 2,))],
+        + [pltpu.SemaphoreType.DMA((3 * samples + 4,)), pltpu.SemaphoreType.DMA((2 * samples + 1,))],
         compiler_params=pltpu.CompilerParams(vmem_limit_bytes=wide_bytes),
         name="shift",
     )(activations, cond_scale, cond_shift, token_mask, query_weight, key_weight, output_weight)
 
     ring = [sent, next_chip(sent)]
-    direct = [from_noise(extended, 1)] + [from_noise(packed, 2**k) for k in range(1, noise_size.bit_length() - 1)]
-    head_weights, _ = after((bias_weight.T, packed))
+    direct = [from_noise(extended, 2**k) for k in range(noise_size.bit_length() - 1)]
+    head_weights, _ = after((bias_weight.T, extended))
     columns = pair_repr.shape[1]
     tile_rows, piece_rows = heads * rows, head_features // columns * half
     assert output_weight.shape == (half, 2 * head_features)
@@ -477,13 +474,13 @@
         name="stack",
     )(*weights)
     query_other, key_other = swap_cores(query_mine), swap_cores(key_mine)
-    output_mine = pl.pallas_call(
+    output_direct = pl.pallas_call(
         functools.partial(stack_kernel, 1),
-        out_shape=struct((2, half, features), bf16),
+        out_shape=struct((1 + len(direct), half, features), bf16),
         compiler_params=params,
         name="stack_output",
-    )(extended, direct[0])
-    output_mine, _ = after((output_mine, ring[2]))
+    )(extended, *direct)
+    output_direct, _ = after((output_direct, ring[2]))
 
     for _ in range(steps - 3):
         ring.append(next_chip(ring[-1]))
@@ -519,10 +516,11 @@
         compiler_params=params,
         name="early",
     )(query_mine, key_mine, query_other, key_other, bias_row, shifted, shifted_other, own_bias, swapped, own_value, swapped_value, *ring)
-    output_parts = [output_mine]
-    for k in range(1, noise_size.bit_length() - 1):
-        held = jnp.concatenate(output_parts, axis=0) if k > 1 else output_mine
-        output_parts.append(from_noise(held, 2**k))
+    output_parts = [output_direct[i] for i in range(1 + len(direct))]
+    output_parts = from_all_noise(output_parts[0], output_parts[1:], features)
+    forwarded = [k for k in range(noise_size) if k & (k - 1)]
+    partial, *arrived = after((partial, *[output_parts[k] for k in forwarded]))
+    forwarded = [output_direct] + arrived
     keep, got = [], []
     chunks = 2
     each = samples // chunks
@@ -538,14 +536,14 @@
         got.append(swap_cores(give))
     updated = []
     for c in range(chunks):
-        operands = [activations, output_gate, keep[c], got[c], *output_parts, *updated]
+        operands = [activations, output_gate, keep[c], got[c], *forwarded, *updated]
         updated = [
             pl.pallas_call(
-                functools.partial(finish_kernel, heads, c * each, len(output_parts)),
-                in_specs=[pl.BlockSpec(memory_space=pltpu.VMEM)] * (4 + len(output_parts)) + [in_hbm] * len(updated),
+                functools.partial(finish_kernel, heads, c * each, len(forwarded)),
+                in_specs=[pl.BlockSpec(memory_space=pltpu.VMEM)] * (4 + len(forwarded)) + [in_hbm] * len(updated),
                 out_specs=in_hbm,
                 out_shape=struct(activations.shape, bf16),
-                input_output_aliases={4 + len(output_parts): 0} if updated else {},
+                input_output_aliases={4 + len(forwarded): 0} if updated else {},
                 scratch_shapes=[
                     pltpu.VMEM((each, rows, features), bf16),
                     pltpu.VMEM((head_features, features), output_type),

time: 44.3 us -> 46.1 us (1.041)
  waiting for transfers between devices: 10.3 us -> 12.9 us
  starting transfers between devices: 17.3 us -> 16.4 us
    ppermute x7, waiting for transfers between devices: 5.29 us -> 10.5 us  [from_noise(): lax.ppermute(array, 'noise', [(i, i ^ k) for i in range(lax.axis_size('no...]
    ppermute x3, waiting for transfers between devices: 5.03 us -> 1.74 us  [next_chip(): return lax.ppermute(array, 'row', pairs)]
    ppermute x7, starting transfers between devices: 9.57 us -> 7.82 us  [from_noise(): lax.ppermute(array, 'noise', [(i, i ^ k) for i in range(lax.axis_size('no...]
    ppermute x3, starting transfers between devices: 6.4 us -> 7.36 us  [next_chip(): return lax.ppermute(array, 'row', pairs)]
    ppermute x7, waiting for transfers between devices: 0.02 us -> 0.72 us  [swap_cores(): lax.ppermute(array, 'row', [(i, i ^ 1) for i in range(lax.axis_size('row'...]
  transfers between devices with their start and end apart: 17 -> 17, of which waited for: 7 -> 8; matrix products, arithmetic and copies ran while one was open for 0% -> 0% of each run, Pallas kernels for 21% -> 17%
where the time goes in v6:
time: 46.1 us; the launch traced here: 45.9 us
  starting transfers between devices  16.4 us (36%)
  Pallas kernels  13.1 us (28%)
  waiting for transfers between devices  12.9 us (28%)
  local copies, waits for them, and re-layouts  3.24 us (7%)
    ppermute x7, waiting for transfers between devices, from_noise(): lax.ppermute(array, 'noise', [(i, i ^ k) for i in range(lax.axis_size('no...  10.5 us
    ppermute x7, starting transfers between devices, from_noise(): lax.ppermute(array, 'noise', [(i, i ^ k) for i in range(lax.axis_size('no...  7.82 us
    ppermute x3, starting transfers between devices, next_chip(): return lax.ppermute(array, 'row', pairs)  7.36 us
    pallas_call x1, Pallas kernels, body(): pl.pallas_call(functools.partial(early_kernel, steps, heads), out_shape=[...  3.71 us
    unnamed x18, local copies, waits for them, and re-layouts  3.21 us
    pallas_call x1, Pallas kernels, body(): pl.pallas_call(shift_kernel, in_specs=[in_hbm] * 7, out_specs=[in_hbm] *...  2.96 us
    pallas_call x2, Pallas kernels, body(): pl.pallas_call(functools.partial(late_kernel, steps, heads, c * each), ou...  2.35 us
    pallas_call x2, Pallas kernels, body(): pl.pallas_call(functools.partial(finish_kernel, heads, c * each, len(forw...  2.07 us
  transfers between devices with their start and end apart: 17, of which 8 were waited for; matrix products, arithmetic and copies ran while one was open for 0% of the time, Pallas kernels for 17%

profile of v6, /device:TPU:0, one launch (start us, length us, event | category | flops | bytes accessed | tf_op | source)
XLA Modules:
  0.0 45.9 jit_solution(9716609205011866926)
XLA Ops:
  0.0 3.0 %shift.1 = (bf16[4,64,768]{2,1,0:T(8,128)(2,1)}, bf16[4,64,768]{2,1,0:T(8,128)(2,1)}, bf16[96,1536]{1,0:T(8,128)(2,1)}) custom-call(bf16[4,64,768]{2,1,0:T(8,128)(2,1)} %activations.3, bf16[4,64,768]{2,1,0:T(8,128)(2,1)} %scale_hbm.1, bf16[4,64,768]{2,1,0:T(8,128)(2,1)} %shift_hbm.1, s32[4,64]{1,0:T(4,128)} %mask_hbm.1, bf16[192,384]{1,0:T(8,128)(2,1)} %query_hbm.1, ...), custom_call_target="tpu_custom_call" | custom-call | tf_op jit(solution)/shard_map/shift/pallas_call | solution.py:434
  3.0 3.1 %collective-permute-start = (bf16[4,64,768]{2,1,0:T(8,128)(2,1)}, bf16[4,64,768]{2,1,0:T(8,128)(2,1)S(1)}, u32[]{:S(2)}, u32[]{:S(2)}) collective-permute-start(bf16[4,64,768]{2,1,0:T(8,128)(2,1)} %get-tuple-element.31.refs_0_), channel_id=1, source_target_pairs={{0,2},{1,3},{2,6},{3,7},{6,4},{7,5},{4,0},{5,1},{8,10},{9,11},{10,... | collective-permute-start | bytes 1179656 | tf_op jit(solution)/shard_map/ppermute | solution.py:385
  6.0 0.0 collective-permute-start.3
  6.0 1.5 %collective-permute-start.1 = (bf16[96,1536]{1,0:T(8,128)(2,1)}, bf16[96,1536]{1,0:T(8,128)(2,1)S(1)}, u32[]{:S(2)}, u32[]{:S(2)}) collective-permute-start(bf16[96,1536]{1,0:T(8,128)(2,1)} %get-tuple-element.30.refs_0_), channel_id=1, source_target_pairs={{0,8},{8,0},{16,24},{24,16},{1,9},{9,1},{17,25},{25,17},{2,10},{10... | collective-permute-start | bytes 884744 | tf_op jit(solution)/shard_map/ppermute | solution.py:391
  7.5 1.5 %collective-permute-start.2 = (bf16[96,1536]{1,0:T(8,128)(2,1)}, bf16[96,1536]{1,0:T(8,128)(2,1)S(1)}, u32[]{:S(2)}, u32[]{:S(2)}) collective-permute-start(bf16[96,1536]{1,0:T(8,128)(2,1)} %get-tuple-element.30.refs_0_), channel_id=1, source_target_pairs={{0,16},{8,24},{16,0},{24,8},{1,17},{9,25},{17,1},{25,9},{2,18},{10... | collective-permute-start | bytes 884744 | tf_op jit(solution)/shard_map/ppermute | solution.py:391
  9.1 0.0 copy-start.1
  9.1 1.6 %copy-done.1 = bf16[64,128,128]{2,1,0:T(8,128)(2,1)S(1)} copy-done((bf16[64,128,128]{2,1,0:T(8,128)(2,1)S(1)}, bf16[64,128,128]{2,1,0:T(8,128)(2,1)}, u32[]{:S(2)}) %copy-start.1) | copy-done | bytes 2097176
  10.7 0.0 copy-start.6
  10.7 0.9 %copy-done.6 = bf16[192,384]{1,0:T(8,128)(2,1)S(1)} copy-done((bf16[192,384]{1,0:T(8,128)(2,1)S(1)}, bf16[192,384]{1,0:T(8,128)(2,1)}, u32[]{:S(2)}) %copy-start.6) | copy-done | bytes 147480
  11.6 0.0 copy-start.7
  11.6 0.7 %copy-done.7 = bf16[128,8]{0,1:T(8,128)(2,1)S(1)} copy-done((bf16[128,8]{0,1:T(8,128)(2,1)S(1)}, bf16[128,8]{0,1:T(8,128)(2,1)}, u32[]{:S(2)}) %copy-start.7) | copy-done | bytes 2072
  12.2 0.0 copy-start.3
  12.2 1.9 %bias.1.refs_0_ = bf16[800,128]{1,0:T(8,128)(2,1)S(1)} custom-call(bf16[64,128,128]{2,1,0:T(8,128)(2,1)S(1)} %copy-done.1, bf16[192,384]{1,0:T(8,128)(2,1)S(1)} %copy-done.6, bf16[8,128]{1,0:T(8,128)(2,1)S(1)} %bitcast.3), custom_call_target="tpu_custom_call" | custom-call | tf_op jit(solution)/shard_map/bias/pallas_call | solution.py:457
  14.1 0.0 copy-start.8
  14.1 0.0 copy-start.4
  14.1 0.0 copy-start.5
  14.2 1.5 %collective-permute-done.1.refs_1_ = bf16[96,1536]{1,0:T(8,128)(2,1)S(1)} collective-permute-done((bf16[96,1536]{1,0:T(8,128)(2,1)}, bf16[96,1536]{1,0:T(8,128)(2,1)S(1)}, u32[]{:S(2)}, u32[]{:S(2)}) %collective-permute-start.1) | collective-permute-done | bytes 294944 | tf_op jit(solution)/shard_map/ppermute | solution.py:391
  15.7 1.2 %collective-permute-done.2.refs_2_ = bf16[96,1536]{1,0:T(8,128)(2,1)S(1)} collective-permute-done((bf16[96,1536]{1,0:T(8,128)(2,1)}, bf16[96,1536]{1,0:T(8,128)(2,1)S(1)}, u32[]{:S(2)}, u32[]{:S(2)}) %collective-permute-start.2) | collective-permute-done | bytes 294944 | tf_op jit(solution)/shard_map/ppermute | solution.py:391
  16.9 0.0 collective-permute-done.refs_1_
  16.9 0.0 collective-permute-done.3.shifted_other
  16.9 2.6 %collective-permute-start.12 = (bf16[4,64,768]{2,1,0:T(8,128)(2,1)S(1)}, bf16[4,64,768]{2,1,0:T(8,128)(2,1)S(1)}, u32[]{:S(2)}, u32[]{:S(2)}) collective-permute-start(bf16[4,64,768]{2,1,0:T(8,128)(2,1)S(1)} %collective-permute-done.refs_1_), channel_id=1, source_target_pairs={{0,2},{1,3},{2,6},{3,7},{6,4},{7,5},{4,0},{5,1},{8,10},{9,11},{10,... | collective-permute-start | bytes 1179656 | tf_op jit(solution)/shard_map/ppermute | solution.py:385
  19.5 0.6 %collective-permute-start.4 = (bf16[96,768]{1,0:T(8,128)(2,1)S(1)}, bf16[96,768]{1,0:T(8,128)(2,1)S(1)}, u32[]{:S(2)}, u32[]{:S(2)}) collective-permute-start(bf16[96,768]{1,0:T(8,128)(2,1)S(1)} %slice.6), channel_id=1, source_target_pairs={{0,8},{8,0},{16,24},{24,16},{1,9},{9,1},{17,25},{25,17},{2,10},{10... | collective-permute-start | bytes 442376 | tf_op jit(solution)/shard_map/ppermute | solution.py:391
  20.1 1.5 %collective-permute-start.7 = (bf16[800,128]{1,0:T(8,128)(2,1)S(1)}, bf16[800,128]{1,0:T(8,128)(2,1)S(1)}, u32[]{:S(2)}, u32[]{:S(2)}) collective-permute-start(bf16[800,128]{1,0:T(8,128)(2,1)S(1)} %bias.1.refs_0_), channel_id=1, source_target_pairs={{0,8},{8,0},{16,24},{24,16},{1,9},{9,1},{17,25},{25,17},{2,10},{10... | collective-permute-start | bytes 614408 | tf_op jit(solution)/shard_map/ppermute | solution.py:391
  21.6 1.5 %collective-permute-start.8 = (bf16[800,128]{1,0:T(8,128)(2,1)S(1)}, bf16[800,128]{1,0:T(8,128)(2,1)S(1)}, u32[]{:S(2)}, u32[]{:S(2)}) collective-permute-start(bf16[800,128]{1,0:T(8,128)(2,1)S(1)} %bias.1.refs_0_), channel_id=1, source_target_pairs={{0,16},{8,24},{16,0},{24,8},{1,17},{9,25},{17,1},{25,9},{2,18},{10... | collective-permute-start | bytes 614408 | tf_op jit(solution)/shard_map/ppermute | solution.py:391
  23.1 0.5 %collective-permute-start.9 = (bf16[800,128]{1,0:T(8,128)(2,1)S(1)}, bf16[800,128]{1,0:T(8,128)(2,1)S(1)}, u32[]{:S(2)}, u32[]{:S(2)}) collective-permute-start(bf16[800,128]{1,0:T(8,128)(2,1)S(1)} %bias.1.refs_0_), channel_id=1, source_target_pairs={{0,24},{8,16},{16,8},{24,0},{1,25},{9,17},{17,9},{25,1},{2,26},{10... | collective-permute-start | bytes 614408 | tf_op jit(solution)/shard_map/ppermute | solution.py:391
  23.6 2.8 %collective-permute-done.4.refs_3_ = bf16[96,768]{1,0:T(8,128)(2,1)S(1)} collective-permute-done((bf16[96,768]{1,0:T(8,128)(2,1)S(1)}, bf16[96,768]{1,0:T(8,128)(2,1)S(1)}, u32[]{:S(2)}, u32[]{:S(2)}) %collective-permute-start.4) | collective-permute-done | bytes 147488 | tf_op jit(solution)/shard_map/ppermute | solution.py:391
  26.4 0.0 copy-done.3
  26.4 0.1 stack.1
  26.4 0.1 collective-permute-start.5
  26.5 1.7 %collective-permute-done.12.refs_2_ = bf16[4,64,768]{2,1,0:T(8,128)(2,1)S(1)} collective-permute-done((bf16[4,64,768]{2,1,0:T(8,128)(2,1)S(1)}, bf16[4,64,768]{2,1,0:T(8,128)(2,1)S(1)}, u32[]{:S(2)}, u32[]{:S(2)}) %collective-permute-start.12) | collective-permute-done | bytes 393248 | tf_op jit(solution)/shard_map/ppermute | solution.py:385
  28.2 1.7 %collective-permute-start.14 = (bf16[4,64,768]{2,1,0:T(8,128)(2,1)S(1)}, bf16[4,64,768]{2,1,0:T(8,128)(2,1)S(1)}, u32[]{:S(2)}, u32[]{:S(2)}) collective-permute-start(bf16[4,64,768]{2,1,0:T(8,128)(2,1)S(1)} %collective-permute-done.12.refs_2_), channel_id=1, source_target_pairs={{0,2},{1,3},{2,6},{3,7},{6,4},{7,5},{4,0},{5,1},{8,10},{9,11},{10,... | collective-permute-start | bytes 1179656 | tf_op jit(solution)/shard_map/ppermute | solution.py:385
  30.0 0.8 %collective-permute-done.7.refs_1_ = bf16[800,128]{1,0:T(8,128)(2,1)S(1)} collective-permute-done((bf16[800,128]{1,0:T(8,128)(2,1)S(1)}, bf16[800,128]{1,0:T(8,128)(2,1)S(1)}, u32[]{:S(2)}, u32[]{:S(2)}) %collective-permute-start.7) | collective-permute-done | bytes 204832 | tf_op jit(solution)/shard_map/ppermute | solution.py:391
  30.7 0.0 collective-permute-start.6
  30.7 0.0 collective-permute-done.8.refs_2_
  30.7 3.4 %collective-permute-done.9.refs_3_ = bf16[800,128]{1,0:T(8,128)(2,1)S(1)} collective-permute-done((bf16[800,128]{1,0:T(8,128)(2,1)S(1)}, bf16[800,128]{1,0:T(8,128)(2,1)S(1)}, u32[]{:S(2)}, u32[]{:S(2)}) %collective-permute-start.9) | collective-permute-done | bytes 204832 | tf_op jit(solution)/shard_map/ppermute | solution.py:391
  34.2 0.1 sort.1
  34.2 0.1 collective-permute-start.11
  34.3 0.5 %collective-permute-start.10 = (bf16[4,256,128]{2,1,0:T(8,128)(2,1)S(1)}, bf16[4,256,128]{2,1,0:T(8,128)(2,1)S(1)}, u32[]{:S(2)}, u32[]{:S(2)}) collective-permute-start(bf16[4,256,128]{2,1,0:T(8,128)(2,1)S(1)} %get-tuple-element.41), channel_id=1, source_target_pairs={{0,1},{1,0},{2,3},{3,2},{4,5},{5,4},{6,7},{7,6},{8,9},{9,8},{10,11... | collective-permute-start | bytes 786440 | tf_op jit(solution)/shard_map/ppermute | solution.py:372
  34.8 0.0 collective-permute-done.5.query_other
  34.8 0.7 %collective-permute-start.13 = (bf16[96,768]{1,0:T(8,128)(2,1)S(1)}, bf16[96,768]{1,0:T(8,128)(2,1)S(1)}, u32[]{:S(2)}, u32[]{:S(2)}) collective-permute-start(bf16[96,768]{1,0:T(8,128)(2,1)S(1)} %slice_bitcast_fusion), channel_id=1, source_target_pairs={{0,8},{8,0},{16,24},{24,16},{1,9},{9,1},{17,25},{25,17},{2,10},{10... | collective-permute-start | bytes 442376 | tf_op jit(solution)/shard_map/ppermute | solution.py:391
  35.6 0.0 copy-done.8
  35.6 0.0 collective-permute-done.6.key_other
  35.6 0.7 %collective-permute-done.10.swapped = bf16[4,256,128]{2,1,0:T(8,128)(2,1)S(1)} collective-permute-done((bf16[4,256,128]{2,1,0:T(8,128)(2,1)S(1)}, bf16[4,256,128]{2,1,0:T(8,128)(2,1)S(1)}, u32[]{:S(2)}, u32[]{:S(2)}) %collective-permute-start.10) | collective-permute-done | bytes 262176 | tf_op jit(solution)/shard_map/ppermute | solution.py:372
  36.3 0.0 collective-permute-done.11.swapped_value
  36.3 0.0 copy-done.4
  36.3 0.0 copy-done.5
  36.3 3.7 %early.1 = (f32[4,400,128]{2,1,0:T(8,128)S(1)}, bf16[4,128,384]{2,1,0:T(8,128)(2,1)S(1)}, bf16[768,384]{1,0:T(8,128)(2,1)S(1)}, bf16[384,768]{1,0:T(8,128)(2,1)S(1)}) custom-call(bf16[4,96,384]{2,1,0:T(8,128)(2,1)S(1)} %get-tuple-element.36.query_mine, bf16[4,96,384]{2,1,0:T(8,128)(2,1)S(1)} %get-tuple-element.37.key_mine, ...), custom_call_target="tpu_custom_call" | custom-call | tf_op jit(solution)/shard_map/early/pallas_call | solution.py:503
  40.0 0.7 %collective-permute-done.13.refs_1_ = bf16[96,768]{1,0:T(8,128)(2,1)S(1)} collective-permute-done((bf16[96,768]{1,0:T(8,128)(2,1)S(1)}, bf16[96,768]{1,0:T(8,128)(2,1)S(1)}, u32[]{:S(2)}, u32[]{:S(2)}) %collective-permute-start.13) | collective-permute-done | bytes 147488 | tf_op jit(solution)/shard_map/ppermute | solution.py:391
  40.7 0.0 collective-permute-done.14.block
  40.7 1.2 %late.3 = (f32[1,400,128]{2,1,0:T(8,128)S(1)}, f32[1,400,128]{2,1,0:T(8,128)S(1)}) custom-call(f32[4,400,128]{2,1,0:T(8,128)S(1)} %get-tuple-element.46.partial, bf16[4,128,384]{2,1,0:T(8,128)(2,1)S(1)} %get-tuple-element.47.queries, bf16[768,384]{1,0:T(8,128)(2,1)S(1)} %get-tuple-element.48.key_weight, bf16[384,768]{1,0:T(8,128)(2,1)S(1)} %get-tuple-element.49.value_weight, ...), custom_call_target="tpu_custom_call" | custom-call | tf_op jit(solution)/shard_map/late/pallas_call | solution.py:528
  41.9 0.0 copy-start
  41.9 0.0 copy-start.2
  41.9 0.1 collective-permute-start.16
  42.0 1.2 %late.2 = (f32[1,400,128]{2,1,0:T(8,128)S(1)}, f32[1,400,128]{2,1,0:T(8,128)S(1)}) custom-call(f32[4,400,128]{2,1,0:T(8,128)S(1)} %get-tuple-element.46.partial, bf16[4,128,384]{2,1,0:T(8,128)(2,1)S(1)} %get-tuple-element.47.queries, bf16[768,384]{1,0:T(8,128)(2,1)S(1)} %get-tuple-element.48.key_weight, bf16[384,768]{1,0:T(8,128)(2,1)S(1)} %get-tuple-element.49.value_weight, ...), custom_call_target="tpu_custom_call" | custom-call | tf_op jit(solution)/shard_map/late/pallas_call | solution.py:528
  43.2 0.6 %collective-permute-start.15 = (f32[1,400,128]{2,1,0:T(8,128)S(1)}, f32[1,400,128]{2,1,0:T(8,128)S(1)}, u32[]{:S(2)}, u32[]{:S(2)}) collective-permute-start(f32[1,400,128]{2,1,0:T(8,128)S(1)} %get-tuple-element.51), channel_id=1, source_target_pairs={{0,1},{1,0},{2,3},{3,2},{4,5},{5,4},{6,7},{7,6},{8,9},{9,8},{10,11... | collective-permute-start | bytes 614408 | tf_op jit(solution)/shard_map/ppermute | solution.py:372
  43.8 0.0 collective-permute-done.16.got
  43.8 0.0 copy-done
  43.8 0.0 copy-done.2
  43.8 1.0 %finish.2.refs_2_ = bf16[4,64,768]{2,1,0:T(8,128)(2,1)} custom-call(bf16[4,64,768]{2,1,0:T(8,128)(2,1)S(1)} %copy-done, bf16[4,64,768]{2,1,0:T(8,128)(2,1)S(1)} %copy-done.2, f32[1,400,128]{2,1,0:T(8,128)S(1)} %get-tuple-element.53.keep, f32[1,400,128]{2,1,0:T(8,128)S(1)} %collective-permute-done.16.got, bf16[3,96,768]{2,1,0:T(8,128)(2,1)S(1)} %stack_output.1.refs_0_, ...), custom_call_target="tpu_custom_call" | custom-call | tf_op jit(solution)/shard_map/finish/pallas_call | solution.py:541
  44.8 0.0 collective-permute-done.15.got
  44.8 1.0 %finish.3 = bf16[4,64,768]{2,1,0:T(8,128)(2,1)} custom-call(bf16[4,64,768]{2,1,0:T(8,128)(2,1)S(1)} %copy-done, bf16[4,64,768]{2,1,0:T(8,128)(2,1)S(1)} %copy-done.2, f32[1,400,128]{2,1,0:T(8,128)S(1)} %get-tuple-element.50.keep, f32[1,400,128]{2,1,0:T(8,128)S(1)} %collective-permute-done.15.got, ...), custom_call_target="tpu_custom_call", output_to_operand_aliasing={{}: (6, {})} | custom-call | tf_op jit(solution)/shard_map/finish/pallas_call | solution.py:541
  (4 shorter events, 0.1 us)
Async XLA Ops:
  3.0 13.9 %collective-permute-start = (bf16[4,64,768]{2,1,0:T(8,128)(2,1)}, bf16[4,64,768]{2,1,0:T(8,128)(2,1)S(1)}, u32[]{:S(2)}, u32[]{:S(2)}) collective-permute-start(bf16[4,64,768]{2,1,0:T(8,128)(2,1)} %get-tuple-element.31.refs_0_), channel_id=1, source_target_pairs={{0,2},{1,3},{2,6},{3,7},{6,4},{7,5},{4,0},{5,1},{8,10},{9,11},{10,... | collective-permute-start | bytes 1179656 | tf_op jit(solution)/shard_map/ppermute | solution.py:385
  6.0 10.9 %collective-permute-start.3 = (bf16[4,64,768]{2,1,0:T(8,128)(2,1)}, bf16[4,64,768]{2,1,0:T(8,128)(2,1)S(1)}, u32[]{:S(2)}, u32[]{:S(2)}) collective-permute-start(bf16[4,64,768]{2,1,0:T(8,128)(2,1)} %get-tuple-element.33.shifted), channel_id=1, source_target_pairs={{0,1},{1,0},{2,3},{3,2},{4,5},{5,4},{6,7},{7,6},{8,9},{9,8},{10,11... | collective-permute-start | bytes 1179656 | tf_op jit(solution)/shard_map/ppermute | solution.py:372
  6.0 9.6 %collective-permute-start.1 = (bf16[96,1536]{1,0:T(8,128)(2,1)}, bf16[96,1536]{1,0:T(8,128)(2,1)S(1)}, u32[]{:S(2)}, u32[]{:S(2)}) collective-permute-start(bf16[96,1536]{1,0:T(8,128)(2,1)} %get-tuple-element.30.refs_0_), channel_id=1, source_target_pairs={{0,8},{8,0},{16,24},{24,16},{1,9},{9,1},{17,25},{25,17},{2,10},{10... | collective-permute-start | bytes 884744 | tf_op jit(solution)/shard_map/ppermute | solution.py:391
  7.5 9.4 %collective-permute-start.2 = (bf16[96,1536]{1,0:T(8,128)(2,1)}, bf16[96,1536]{1,0:T(8,128)(2,1)S(1)}, u32[]{:S(2)}, u32[]{:S(2)}) collective-permute-start(bf16[96,1536]{1,0:T(8,128)(2,1)} %get-tuple-element.30.refs_0_), channel_id=1, source_target_pairs={{0,16},{8,24},{16,0},{24,8},{1,17},{9,25},{17,1},{25,9},{2,18},{10... | collective-permute-start | bytes 884744 | tf_op jit(solution)/shard_map/ppermute | solution.py:391
  9.1 1.6 %copy-start.1 = (bf16[64,128,128]{2,1,0:T(8,128)(2,1)S(1)}, bf16[64,128,128]{2,1,0:T(8,128)(2,1)}, u32[]{:S(2)}) copy-start(bf16[64,128,128]{2,1,0:T(8,128)(2,1)} %pair.1) | copy-start | bytes 6291460
  10.7 0.9 %copy-start.6 = (bf16[192,384]{1,0:T(8,128)(2,1)S(1)}, bf16[192,384]{1,0:T(8,128)(2,1)}, u32[]{:S(2)}) copy-start(bf16[192,384]{1,0:T(8,128)(2,1)} %value_weight.1) | copy-start | bytes 442372
  11.6 0.7 %copy-start.7 = (bf16[128,8]{0,1:T(8,128)(2,1)S(1)}, bf16[128,8]{0,1:T(8,128)(2,1)}, u32[]{:S(2)}) copy-start(bf16[128,8]{0,1:T(8,128)(2,1)} %param.17) | copy-start | bytes 6148
  12.2 14.1 %copy-start.3 = (bf16[96,1536]{1,0:T(8,128)(2,1)S(1)}, bf16[96,1536]{1,0:T(8,128)(2,1)}, u32[]{:S(2)}) copy-start(bf16[96,1536]{1,0:T(8,128)(2,1)} %get-tuple-element.30.refs_0_) | copy-start | bytes 884740
  14.1 21.4 %copy-start.8 = (bf16[384]{0:T(512)(128)(2,1)S(1)}, bf16[384]{0:T(512)(128)(2,1)}, u32[]{:S(2)}) copy-start(bf16[384]{0:T(512)(128)(2,1)} %param.19) | copy-start | bytes 2308
  14.1 22.1 %copy-start.4 = (bf16[4,64,768]{2,1,0:T(8,128)(2,1)S(1)}, bf16[4,64,768]{2,1,0:T(8,128)(2,1)}, u32[]{:S(2)}) copy-start(bf16[4,64,768]{2,1,0:T(8,128)(2,1)} %get-tuple-element.33.shifted) | copy-start | bytes 1179652
  14.1 22.1 %copy-start.5 = (bf16[4,64,768]{2,1,0:T(8,128)(2,1)S(1)}, bf16[4,64,768]{2,1,0:T(8,128)(2,1)}, u32[]{:S(2)}) copy-start(bf16[4,64,768]{2,1,0:T(8,128)(2,1)} %get-tuple-element.31.refs_0_) | copy-start | bytes 1179652
  16.9 11.3 %collective-permute-start.12 = (bf16[4,64,768]{2,1,0:T(8,128)(2,1)S(1)}, bf16[4,64,768]{2,1,0:T(8,128)(2,1)S(1)}, u32[]{:S(2)}, u32[]{:S(2)}) collective-permute-start(bf16[4,64,768]{2,1,0:T(8,128)(2,1)S(1)} %collective-permute-done.refs_1_), channel_id=1, source_target_pairs={{0,2},{1,3},{2,6},{3,7},{6,4},{7,5},{4,0},{5,1},{8,10},{9,11},{10,... | collective-permute-start | bytes 1179656 | tf_op jit(solution)/shard_map/ppermute | solution.py:385
  19.5 6.8 %collective-permute-start.4 = (bf16[96,768]{1,0:T(8,128)(2,1)S(1)}, bf16[96,768]{1,0:T(8,128)(2,1)S(1)}, u32[]{:S(2)}, u32[]{:S(2)}) collective-permute-start(bf16[96,768]{1,0:T(8,128)(2,1)S(1)} %slice.6), channel_id=1, source_target_pairs={{0,8},{8,0},{16,24},{24,16},{1,9},{9,1},{17,25},{25,17},{2,10},{10... | collective-permute-start | bytes 442376 | tf_op jit(solution)/shard_map/ppermute | solution.py:391
  20.1 10.6 %collective-permute-start.7 = (bf16[800,128]{1,0:T(8,128)(2,1)S(1)}, bf16[800,128]{1,0:T(8,128)(2,1)S(1)}, u32[]{:S(2)}, u32[]{:S(2)}) collective-permute-start(bf16[800,128]{1,0:T(8,128)(2,1)S(1)} %bias.1.refs_0_), channel_id=1, source_target_pairs={{0,8},{8,0},{16,24},{24,16},{1,9},{9,1},{17,25},{25,17},{2,10},{10... | collective-permute-start | bytes 614408 | tf_op jit(solution)/shard_map/ppermute | solution.py:391
  21.6 9.2 %collective-permute-start.8 = (bf16[800,128]{1,0:T(8,128)(2,1)S(1)}, bf16[800,128]{1,0:T(8,128)(2,1)S(1)}, u32[]{:S(2)}, u32[]{:S(2)}) collective-permute-start(bf16[800,128]{1,0:T(8,128)(2,1)S(1)} %bias.1.refs_0_), channel_id=1, source_target_pairs={{0,16},{8,24},{16,0},{24,8},{1,17},{9,25},{17,1},{25,9},{2,18},{10... | collective-permute-start | bytes 614408 | tf_op jit(solution)/shard_map/ppermute | solution.py:391
  23.1 11.1 %collective-permute-start.9 = (bf16[800,128]{1,0:T(8,128)(2,1)S(1)}, bf16[800,128]{1,0:T(8,128)(2,1)S(1)}, u32[]{:S(2)}, u32[]{:S(2)}) collective-permute-start(bf16[800,128]{1,0:T(8,128)(2,1)S(1)} %bias.1.refs_0_), channel_id=1, source_target_pairs={{0,24},{8,16},{16,8},{24,0},{1,25},{9,17},{17,9},{25,1},{2,26},{10... | collective-permute-start | bytes 614408 | tf_op jit(solution)/shard_map/ppermute | solution.py:391
  26.4 8.4 %collective-permute-start.5 = (bf16[4,96,384]{2,1,0:T(8,128)(2,1)S(1)}, bf16[4,96,384]{2,1,0:T(8,128)(2,1)S(1)}, u32[]{:S(2)}, u32[]{:S(2)}) collective-permute-start(bf16[4,96,384]{2,1,0:T(8,128)(2,1)S(1)} %get-tuple-element.36.query_mine), channel_id=1, source_target_pairs={{0,1},{1,0},{2,3},{3,2},{4,5},{5,4},{6,7},{7,6},{8,9},{9,8},{10,11... | collective-permute-start | bytes 884744 | tf_op jit(solution)/shard_map/ppermute | solution.py:372
  28.2 12.5 %collective-permute-start.14 = (bf16[4,64,768]{2,1,0:T(8,128)(2,1)S(1)}, bf16[4,64,768]{2,1,0:T(8,128)(2,1)S(1)}, u32[]{:S(2)}, u32[]{:S(2)}) collective-permute-start(bf16[4,64,768]{2,1,0:T(8,128)(2,1)S(1)} %collective-permute-done.12.refs_2_), channel_id=1, source_target_pairs={{0,2},{1,3},{2,6},{3,7},{6,4},{7,5},{4,0},{5,1},{8,10},{9,11},{10,... | collective-permute-start | bytes 1179656 | tf_op jit(solution)/shard_map/ppermute | solution.py:385
  30.7 4.8 %collective-permute-start.6 = (bf16[4,96,384]{2,1,0:T(8,128)(2,1)S(1)}, bf16[4,96,384]{2,1,0:T(8,128)(2,1)S(1)}, u32[]{:S(2)}, u32[]{:S(2)}) collective-permute-start(bf16[4,96,384]{2,1,0:T(8,128)(2,1)S(1)} %get-tuple-element.37.key_mine), channel_id=1, source_target_pairs={{0,1},{1,0},{2,3},{3,2},{4,5},{5,4},{6,7},{7,6},{8,9},{9,8},{10,11... | collective-permute-start | bytes 884744 | tf_op jit(solution)/shard_map/ppermute | solution.py:372
  34.2 2.0 %collective-permute-start.11 = (bf16[4,288,128]{2,1,0:T(8,128)(2,1)S(1)}, bf16[4,288,128]{2,1,0:T(8,128)(2,1)S(1)}, u32[]{:S(2)}, u32[]{:S(2)}) collective-permute-start(bf16[4,288,128]{2,1,0:T(8,128)(2,1)S(1)} %get-tuple-element.42.own_value), channel_id=1, source_target_pairs={{0,1},{1,0},{2,3},{3,2},{4,5},{5,4},{6,7},{7,6},{8,9},{9,8},{10,11... | collective-permute-start | bytes 884744 | tf_op jit(solution)/shard_map/ppermute | solution.py:372
  34.3 1.9 %collective-permute-start.10 = (bf16[4,256,128]{2,1,0:T(8,128)(2,1)S(1)}, bf16[4,256,128]{2,1,0:T(8,128)(2,1)S(1)}, u32[]{:S(2)}, u32[]{:S(2)}) collective-permute-start(bf16[4,256,128]{2,1,0:T(8,128)(2,1)S(1)} %get-tuple-element.41), channel_id=1, source_target_pairs={{0,1},{1,0},{2,3},{3,2},{4,5},{5,4},{6,7},{7,6},{8,9},{9,8},{10,11... | collective-permute-start | bytes 786440 | tf_op jit(solution)/shard_map/ppermute | solution.py:372
  34.8 5.9 %collective-permute-start.13 = (bf16[96,768]{1,0:T(8,128)(2,1)S(1)}, bf16[96,768]{1,0:T(8,128)(2,1)S(1)}, u32[]{:S(2)}, u32[]{:S(2)}) collective-permute-start(bf16[96,768]{1,0:T(8,128)(2,1)S(1)} %slice_bitcast_fusion), channel_id=1, source_target_pairs={{0,8},{8,0},{16,24},{24,16},{1,9},{9,1},{17,25},{25,17},{2,10},{10... | collective-permute-start | bytes 442376 | tf_op jit(solution)/shard_map/ppermute | solution.py:391
  41.9 1.8 %copy-start = (bf16[4,64,768]{2,1,0:T(8,128)(2,1)S(1)}, bf16[4,64,768]{2,1,0:T(8,128)(2,1)}, u32[]{:S(2)}) copy-start(bf16[4,64,768]{2,1,0:T(8,128)(2,1)} %activations.3) | copy-start | bytes 1179652
  41.9 1.8 %copy-start.2 = (bf16[4,64,768]{2,1,0:T(8,128)(2,1)S(1)}, bf16[4,64,768]{2,1,0:T(8,128)(2,1)}, u32[]{:S(2)}) copy-start(bf16[4,64,768]{2,1,0:T(8,128)(2,1)} %output_gate.3) | copy-start | bytes 1179652
  41.9 1.8 %collective-permute-start.16 = (f32[1,400,128]{2,1,0:T(8,128)S(1)}, f32[1,400,128]{2,1,0:T(8,128)S(1)}, u32[]{:S(2)}, u32[]{:S(2)}) collective-permute-start(f32[1,400,128]{2,1,0:T(8,128)S(1)} %get-tuple-element.54), channel_id=1, source_target_pairs={{0,1},{1,0},{2,3},{3,2},{4,5},{5,4},{6,7},{7,6},{8,9},{9,8},{10,11... | collective-permute-start | bytes 614408 | tf_op jit(solution)/shard_map/ppermute | solution.py:372
  43.2 1.6 %collective-permute-start.15 = (f32[1,400,128]{2,1,0:T(8,128)S(1)}, f32[1,400,128]{2,1,0:T(8,128)S(1)}, u32[]{:S(2)}, u32[]{:S(2)}) collective-permute-start(f32[1,400,128]{2,1,0:T(8,128)S(1)} %get-tuple-element.51), channel_id=1, source_target_pairs={{0,1},{1,0},{2,3},{3,2},{4,5},{5,4},{6,7},{7,6},{8,9},{9,8},{10,11... | collective-permute-start | bytes 614408 | tf_op jit(solution)/shard_map/ppermute | solution.py:372

commit v7 on v6

--- a/solution.py
+++ b/solution.py
@@ -144,7 +144,7 @@
 
 def sort_kernel(*refs):
     stacks = refs[-3:]
-    for k, parcel in enumerate(refs[:-3]):
+    for k, parcel in enumerate(refs[:-3][::-1]):
         at = 0
         for stack in stacks:
             stack[k] = parcel[at : at + stack.shape[1]]
@@ -491,7 +491,7 @@
         out_shape=[struct(shape, bf16) for shape in (tile_shape, tile_shape, piece_shape)],
         compiler_params=params,
         name="sort",
-    )(*parcels)
+    )(*parcels[::-1])
     swapped = swap_cores(other_bias)
     swapped_value = swap_cores(own_value)
 

time: 46.1 us -> 45.1 us (0.978)
  waiting for transfers between devices: 12.9 us -> 11.8 us
    ppermute x7, waiting for transfers between devices: 10.5 us -> 9.52 us  [from_noise(): lax.ppermute(array, 'noise', [(i, i ^ k) for i in range(lax.axis_size('no...]
  transfers between devices with their start and end apart: 17 -> 17, of which waited for: 8 -> 9; matrix products, arithmetic and copies ran while one was open for 0% -> 0% of each run, Pallas kernels for 17% -> 18%
where the time goes in v7:
time: 45.1 us; the launch traced here: 44.9 us
  starting transfers between devices  16.6 us (37%)
  Pallas kernels  13.1 us (29%)
  waiting for transfers between devices  11.8 us (26%)
  local copies, waits for them, and re-layouts  3.24 us (7%)
    ppermute x7, waiting for transfers between devices, from_noise(): lax.ppermute(array, 'noise', [(i, i ^ k) for i in range(lax.axis_size('no...  9.52 us
    ppermute x7, starting transfers between devices, from_noise(): lax.ppermute(array, 'noise', [(i, i ^ k) for i in range(lax.axis_size('no...  8.01 us
    ppermute x3, starting transfers between devices, next_chip(): return lax.ppermute(array, 'row', pairs)  7.36 us
    pallas_call x1, Pallas kernels, body(): pl.pallas_call(functools.partial(early_kernel, steps, heads), out_shape=[...  3.71 us
    unnamed x18, local copies, waits for them, and re-layouts  3.21 us
    pallas_call x1, Pallas kernels, body(): pl.pallas_call(shift_kernel, in_specs=[in_hbm] * 7, out_specs=[in_hbm] *...  2.96 us
    pallas_call x2, Pallas kernels, body(): pl.pallas_call(functools.partial(late_kernel, steps, heads, c * each), ou...  2.35 us
    pallas_call x2, Pallas kernels, body(): pl.pallas_call(functools.partial(finish_kernel, heads, c * each, len(forw...  2.07 us
  transfers between devices with their start and end apart: 17, of which 9 were waited for; matrix products, arithmetic and copies ran while one was open for 0% of the time, Pallas kernels for 18%

profile of v7, /device:TPU:0, one launch (start us, length us, event | category | flops | bytes accessed | tf_op | source)
XLA Modules:
  0.0 44.9 jit_solution(3987283659764860364)
XLA Ops:
  0.0 3.0 %shift.1 = (bf16[4,64,768]{2,1,0:T(8,128)(2,1)}, bf16[4,64,768]{2,1,0:T(8,128)(2,1)}, bf16[96,1536]{1,0:T(8,128)(2,1)}) custom-call(bf16[4,64,768]{2,1,0:T(8,128)(2,1)} %activations.3, bf16[4,64,768]{2,1,0:T(8,128)(2,1)} %scale_hbm.1, bf16[4,64,768]{2,1,0:T(8,128)(2,1)} %shift_hbm.1, s32[4,64]{1,0:T(4,128)} %mask_hbm.1, bf16[192,384]{1,0:T(8,128)(2,1)} %query_hbm.1, ...), custom_call_target="tpu_custom_call" | custom-call | tf_op jit(solution)/shard_map/shift/pallas_call | solution.py:434
  3.0 3.1 %collective-permute-start = (bf16[4,64,768]{2,1,0:T(8,128)(2,1)}, bf16[4,64,768]{2,1,0:T(8,128)(2,1)S(1)}, u32[]{:S(2)}, u32[]{:S(2)}) collective-permute-start(bf16[4,64,768]{2,1,0:T(8,128)(2,1)} %get-tuple-element.31.refs_0_), channel_id=1, source_target_pairs={{0,2},{1,3},{2,6},{3,7},{6,4},{7,5},{4,0},{5,1},{8,10},{9,11},{10,... | collective-permute-start | bytes 1179656 | tf_op jit(solution)/shard_map/ppermute | solution.py:385
  6.0 0.0 collective-permute-start.3
  6.0 1.5 %collective-permute-start.1 = (bf16[96,1536]{1,0:T(8,128)(2,1)}, bf16[96,1536]{1,0:T(8,128)(2,1)S(1)}, u32[]{:S(2)}, u32[]{:S(2)}) collective-permute-start(bf16[96,1536]{1,0:T(8,128)(2,1)} %get-tuple-element.30.refs_0_), channel_id=1, source_target_pairs={{0,8},{8,0},{16,24},{24,16},{1,9},{9,1},{17,25},{25,17},{2,10},{10... | collective-permute-start | bytes 884744 | tf_op jit(solution)/shard_map/ppermute | solution.py:391
  7.5 1.5 %collective-permute-start.2 = (bf16[96,1536]{1,0:T(8,128)(2,1)}, bf16[96,1536]{1,0:T(8,128)(2,1)S(1)}, u32[]{:S(2)}, u32[]{:S(2)}) collective-permute-start(bf16[96,1536]{1,0:T(8,128)(2,1)} %get-tuple-element.30.refs_0_), channel_id=1, source_target_pairs={{0,16},{8,24},{16,0},{24,8},{1,17},{9,25},{17,1},{25,9},{2,18},{10... | collective-permute-start | bytes 884744 | tf_op jit(solution)/shard_map/ppermute | solution.py:391
  9.1 0.0 copy-start.1
  9.1 1.6 %copy-done.1 = bf16[64,128,128]{2,1,0:T(8,128)(2,1)S(1)} copy-done((bf16[64,128,128]{2,1,0:T(8,128)(2,1)S(1)}, bf16[64,128,128]{2,1,0:T(8,128)(2,1)}, u32[]{:S(2)}) %copy-start.1) | copy-done | bytes 2097176
  10.7 0.0 copy-start.6
  10.7 0.9 %copy-done.6 = bf16[192,384]{1,0:T(8,128)(2,1)S(1)} copy-done((bf16[192,384]{1,0:T(8,128)(2,1)S(1)}, bf16[192,384]{1,0:T(8,128)(2,1)}, u32[]{:S(2)}) %copy-start.6) | copy-done | bytes 147480
  11.6 0.0 copy-start.7
  11.6 0.7 %copy-done.7 = bf16[128,8]{0,1:T(8,128)(2,1)S(1)} copy-done((bf16[128,8]{0,1:T(8,128)(2,1)S(1)}, bf16[128,8]{0,1:T(8,128)(2,1)}, u32[]{:S(2)}) %copy-start.7) | copy-done | bytes 2072
  12.2 0.0 copy-start.3
  12.2 1.9 %bias.1.refs_3_ = bf16[800,128]{1,0:T(8,128)(2,1)S(1)} custom-call(bf16[64,128,128]{2,1,0:T(8,128)(2,1)S(1)} %copy-done.1, bf16[192,384]{1,0:T(8,128)(2,1)S(1)} %copy-done.6, bf16[8,128]{1,0:T(8,128)(2,1)S(1)} %bitcast.3), custom_call_target="tpu_custom_call" | custom-call | tf_op jit(solution)/shard_map/bias/pallas_call | solution.py:457
  14.1 0.0 copy-start.8
  14.1 0.0 copy-start.4
  14.1 0.0 copy-start.5
  14.2 1.5 %collective-permute-done.1.refs_1_ = bf16[96,1536]{1,0:T(8,128)(2,1)S(1)} collective-permute-done((bf16[96,1536]{1,0:T(8,128)(2,1)}, bf16[96,1536]{1,0:T(8,128)(2,1)S(1)}, u32[]{:S(2)}, u32[]{:S(2)}) %collective-permute-start.1) | collective-permute-done | bytes 294944 | tf_op jit(solution)/shard_map/ppermute | solution.py:391
  15.7 1.2 %collective-permute-done.2.refs_2_ = bf16[96,1536]{1,0:T(8,128)(2,1)S(1)} collective-permute-done((bf16[96,1536]{1,0:T(8,128)(2,1)}, bf16[96,1536]{1,0:T(8,128)(2,1)S(1)}, u32[]{:S(2)}, u32[]{:S(2)}) %collective-permute-start.2) | collective-permute-done | bytes 294944 | tf_op jit(solution)/shard_map/ppermute | solution.py:391
  16.9 0.0 collective-permute-done.refs_1_
  16.9 0.0 collective-permute-done.3.shifted_other
  16.9 2.6 %collective-permute-start.12 = (bf16[4,64,768]{2,1,0:T(8,128)(2,1)S(1)}, bf16[4,64,768]{2,1,0:T(8,128)(2,1)S(1)}, u32[]{:S(2)}, u32[]{:S(2)}) collective-permute-start(bf16[4,64,768]{2,1,0:T(8,128)(2,1)S(1)} %collective-permute-done.refs_1_), channel_id=1, source_target_pairs={{0,2},{1,3},{2,6},{3,7},{6,4},{7,5},{4,0},{5,1},{8,10},{9,11},{10,... | collective-permute-start | bytes 1179656 | tf_op jit(solution)/shard_map/ppermute | solution.py:385
  19.5 0.6 %collective-permute-start.4 = (bf16[96,768]{1,0:T(8,128)(2,1)S(1)}, bf16[96,768]{1,0:T(8,128)(2,1)S(1)}, u32[]{:S(2)}, u32[]{:S(2)}) collective-permute-start(bf16[96,768]{1,0:T(8,128)(2,1)S(1)} %slice.6), channel_id=1, source_target_pairs={{0,8},{8,0},{16,24},{24,16},{1,9},{9,1},{17,25},{25,17},{2,10},{10... | collective-permute-start | bytes 442376 | tf_op jit(solution)/shard_map/ppermute | solution.py:391
  20.1 2.4 %collective-permute-start.7 = (bf16[800,128]{1,0:T(8,128)(2,1)S(1)}, bf16[800,128]{1,0:T(8,128)(2,1)S(1)}, u32[]{:S(2)}, u32[]{:S(2)}) collective-permute-start(bf16[800,128]{1,0:T(8,128)(2,1)S(1)} %bias.1.refs_3_), channel_id=1, source_target_pairs={{0,24},{8,16},{16,8},{24,0},{1,25},{9,17},{17,9},{25,1},{2,26},{10... | collective-permute-start | bytes 614408 | tf_op jit(solution)/shard_map/ppermute | solution.py:391
  22.6 0.5 %collective-permute-start.8 = (bf16[800,128]{1,0:T(8,128)(2,1)S(1)}, bf16[800,128]{1,0:T(8,128)(2,1)S(1)}, u32[]{:S(2)}, u32[]{:S(2)}) collective-permute-start(bf16[800,128]{1,0:T(8,128)(2,1)S(1)} %bias.1.refs_3_), channel_id=1, source_target_pairs={{0,16},{8,24},{16,0},{24,8},{1,17},{9,25},{17,1},{25,9},{2,18},{10... | collective-permute-start | bytes 614408 | tf_op jit(solution)/shard_map/ppermute | solution.py:391
  23.1 0.5 %collective-permute-start.9 = (bf16[800,128]{1,0:T(8,128)(2,1)S(1)}, bf16[800,128]{1,0:T(8,128)(2,1)S(1)}, u32[]{:S(2)}, u32[]{:S(2)}) collective-permute-start(bf16[800,128]{1,0:T(8,128)(2,1)S(1)} %bias.1.refs_3_), channel_id=1, source_target_pairs={{0,8},{8,0},{16,24},{24,16},{1,9},{9,1},{17,25},{25,17},{2,10},{10... | collective-permute-start | bytes 614408 | tf_op jit(solution)/shard_map/ppermute | solution.py:391
  23.6 2.8 %collective-permute-done.4.refs_3_ = bf16[96,768]{1,0:T(8,128)(2,1)S(1)} collective-permute-done((bf16[96,768]{1,0:T(8,128)(2,1)S(1)}, bf16[96,768]{1,0:T(8,128)(2,1)S(1)}, u32[]{:S(2)}, u32[]{:S(2)}) %collective-permute-start.4) | collective-permute-done | bytes 147488 | tf_op jit(solution)/shard_map/ppermute | solution.py:391
  26.4 0.0 copy-done.3
  26.4 0.1 stack.1
  26.4 0.1 collective-permute-start.5
  26.5 1.7 %collective-permute-done.12.refs_2_ = bf16[4,64,768]{2,1,0:T(8,128)(2,1)S(1)} collective-permute-done((bf16[4,64,768]{2,1,0:T(8,128)(2,1)S(1)}, bf16[4,64,768]{2,1,0:T(8,128)(2,1)S(1)}, u32[]{:S(2)}, u32[]{:S(2)}) %collective-permute-start.12) | collective-permute-done | bytes 393248 | tf_op jit(solution)/shard_map/ppermute | solution.py:385
  28.2 1.7 %collective-permute-start.14 = (bf16[4,64,768]{2,1,0:T(8,128)(2,1)S(1)}, bf16[4,64,768]{2,1,0:T(8,128)(2,1)S(1)}, u32[]{:S(2)}, u32[]{:S(2)}) collective-permute-start(bf16[4,64,768]{2,1,0:T(8,128)(2,1)S(1)} %collective-permute-done.12.refs_2_), channel_id=1, source_target_pairs={{0,2},{1,3},{2,6},{3,7},{6,4},{7,5},{4,0},{5,1},{8,10},{9,11},{10,... | collective-permute-start | bytes 1179656 | tf_op jit(solution)/shard_map/ppermute | solution.py:385
  30.0 1.7 %collective-permute-done.7.refs_0_ = bf16[800,128]{1,0:T(8,128)(2,1)S(1)} collective-permute-done((bf16[800,128]{1,0:T(8,128)(2,1)S(1)}, bf16[800,128]{1,0:T(8,128)(2,1)S(1)}, u32[]{:S(2)}, u32[]{:S(2)}) %collective-permute-start.7) | collective-permute-done | bytes 204832 | tf_op jit(solution)/shard_map/ppermute | solution.py:391
  31.7 0.0 collective-permute-start.6
  31.7 0.8 %collective-permute-done.8.refs_1_ = bf16[800,128]{1,0:T(8,128)(2,1)S(1)} collective-permute-done((bf16[800,128]{1,0:T(8,128)(2,1)S(1)}, bf16[800,128]{1,0:T(8,128)(2,1)S(1)}, u32[]{:S(2)}, u32[]{:S(2)}) %collective-permute-start.8) | collective-permute-done | bytes 204832 | tf_op jit(solution)/shard_map/ppermute | solution.py:391
  32.5 0.7 %collective-permute-done.9.refs_2_ = bf16[800,128]{1,0:T(8,128)(2,1)S(1)} collective-permute-done((bf16[800,128]{1,0:T(8,128)(2,1)S(1)}, bf16[800,128]{1,0:T(8,128)(2,1)S(1)}, u32[]{:S(2)}, u32[]{:S(2)}) %collective-permute-start.9) | collective-permute-done | bytes 204832 | tf_op jit(solution)/shard_map/ppermute | solution.py:391
  33.2 0.1 sort.1
  33.3 0.1 collective-permute-start.11
  33.4 0.5 %collective-permute-start.10 = (bf16[4,256,128]{2,1,0:T(8,128)(2,1)S(1)}, bf16[4,256,128]{2,1,0:T(8,128)(2,1)S(1)}, u32[]{:S(2)}, u32[]{:S(2)}) collective-permute-start(bf16[4,256,128]{2,1,0:T(8,128)(2,1)S(1)} %get-tuple-element.41), channel_id=1, source_target_pairs={{0,1},{1,0},{2,3},{3,2},{4,5},{5,4},{6,7},{7,6},{8,9},{9,8},{10,11... | collective-permute-start | bytes 786440 | tf_op jit(solution)/shard_map/ppermute | solution.py:372
  33.9 0.0 collective-permute-done.5.query_other
  33.9 0.9 %collective-permute-start.13 = (bf16[96,768]{1,0:T(8,128)(2,1)S(1)}, bf16[96,768]{1,0:T(8,128)(2,1)S(1)}, u32[]{:S(2)}, u32[]{:S(2)}) collective-permute-start(bf16[96,768]{1,0:T(8,128)(2,1)S(1)} %slice_bitcast_fusion), channel_id=1, source_target_pairs={{0,8},{8,0},{16,24},{24,16},{1,9},{9,1},{17,25},{25,17},{2,10},{10... | collective-permute-start | bytes 442376 | tf_op jit(solution)/shard_map/ppermute | solution.py:391
  34.8 0.0 copy-done.8
  34.8 0.0 collective-permute-done.6.key_other
  34.8 0.5 %collective-permute-done.10.swapped = bf16[4,256,128]{2,1,0:T(8,128)(2,1)S(1)} collective-permute-done((bf16[4,256,128]{2,1,0:T(8,128)(2,1)S(1)}, bf16[4,256,128]{2,1,0:T(8,128)(2,1)S(1)}, u32[]{:S(2)}, u32[]{:S(2)}) %collective-permute-start.10) | collective-permute-done | bytes 262176 | tf_op jit(solution)/shard_map/ppermute | solution.py:372
  35.3 0.0 collective-permute-done.11.swapped_value
  35.3 0.0 copy-done.4
  35.3 0.0 copy-done.5
  35.3 3.7 %early.1 = (f32[4,400,128]{2,1,0:T(8,128)S(1)}, bf16[4,128,384]{2,1,0:T(8,128)(2,1)S(1)}, bf16[768,384]{1,0:T(8,128)(2,1)S(1)}, bf16[384,768]{1,0:T(8,128)(2,1)S(1)}) custom-call(bf16[4,96,384]{2,1,0:T(8,128)(2,1)S(1)} %get-tuple-element.36.query_mine, bf16[4,96,384]{2,1,0:T(8,128)(2,1)S(1)} %get-tuple-element.37.key_mine, ...), custom_call_target="tpu_custom_call" | custom-call | tf_op jit(solution)/shard_map/early/pallas_call | solution.py:503
  39.0 0.7 %collective-permute-done.13.refs_1_ = bf16[96,768]{1,0:T(8,128)(2,1)S(1)} collective-permute-done((bf16[96,768]{1,0:T(8,128)(2,1)S(1)}, bf16[96,768]{1,0:T(8,128)(2,1)S(1)}, u32[]{:S(2)}, u32[]{:S(2)}) %collective-permute-start.13) | collective-permute-done | bytes 147488 | tf_op jit(solution)/shard_map/ppermute | solution.py:391
  39.8 0.0 collective-permute-done.14.block
  39.8 1.2 %late.3 = (f32[1,400,128]{2,1,0:T(8,128)S(1)}, f32[1,400,128]{2,1,0:T(8,128)S(1)}) custom-call(f32[4,400,128]{2,1,0:T(8,128)S(1)} %get-tuple-element.46.partial, bf16[4,128,384]{2,1,0:T(8,128)(2,1)S(1)} %get-tuple-element.47.queries, bf16[768,384]{1,0:T(8,128)(2,1)S(1)} %get-tuple-element.48.key_weight, bf16[384,768]{1,0:T(8,128)(2,1)S(1)} %get-tuple-element.49.value_weight, ...), custom_call_target="tpu_custom_call" | custom-call | tf_op jit(solution)/shard_map/late/pallas_call | solution.py:528
  41.0 0.0 copy-start
  41.0 0.0 copy-start.2
  41.0 0.1 collective-permute-start.16
  41.1 1.2 %late.2 = (f32[1,400,128]{2,1,0:T(8,128)S(1)}, f32[1,400,128]{2,1,0:T(8,128)S(1)}) custom-call(f32[4,400,128]{2,1,0:T(8,128)S(1)} %get-tuple-element.46.partial, bf16[4,128,384]{2,1,0:T(8,128)(2,1)S(1)} %get-tuple-element.47.queries, bf16[768,384]{1,0:T(8,128)(2,1)S(1)} %get-tuple-element.48.key_weight, bf16[384,768]{1,0:T(8,128)(2,1)S(1)} %get-tuple-element.49.value_weight, ...), custom_call_target="tpu_custom_call" | custom-call | tf_op jit(solution)/shard_map/late/pallas_call | solution.py:528
  42.3 0.6 %collective-permute-start.15 = (f32[1,400,128]{2,1,0:T(8,128)S(1)}, f32[1,400,128]{2,1,0:T(8,128)S(1)}, u32[]{:S(2)}, u32[]{:S(2)}) collective-permute-start(f32[1,400,128]{2,1,0:T(8,128)S(1)} %get-tuple-element.51), channel_id=1, source_target_pairs={{0,1},{1,0},{2,3},{3,2},{4,5},{5,4},{6,7},{7,6},{8,9},{9,8},{10,11... | collective-permute-start | bytes 614408 | tf_op jit(solution)/shard_map/ppermute | solution.py:372
  42.8 0.0 collective-permute-done.16.got
  42.8 0.0 copy-done
  42.8 0.0 copy-done.2
  42.8 1.0 %finish.2.refs_2_ = bf16[4,64,768]{2,1,0:T(8,128)(2,1)} custom-call(bf16[4,64,768]{2,1,0:T(8,128)(2,1)S(1)} %copy-done, bf16[4,64,768]{2,1,0:T(8,128)(2,1)S(1)} %copy-done.2, f32[1,400,128]{2,1,0:T(8,128)S(1)} %get-tuple-element.53.keep, f32[1,400,128]{2,1,0:T(8,128)S(1)} %collective-permute-done.16.got, bf16[3,96,768]{2,1,0:T(8,128)(2,1)S(1)} %stack_output.1.refs_0_, ...), custom_call_target="tpu_custom_call" | custom-call | tf_op jit(solution)/shard_map/finish/pallas_call | solution.py:541
  43.9 0.0 collective-permute-done.15.got
  43.9 1.0 %finish.3 = bf16[4,64,768]{2,1,0:T(8,128)(2,1)} custom-call(bf16[4,64,768]{2,1,0:T(8,128)(2,1)S(1)} %copy-done, bf16[4,64,768]{2,1,0:T(8,128)(2,1)S(1)} %copy-done.2, f32[1,400,128]{2,1,0:T(8,128)S(1)} %get-tuple-element.50.keep, f32[1,400,128]{2,1,0:T(8,128)S(1)} %collective-permute-done.15.got, ...), custom_call_target="tpu_custom_call", output_to_operand_aliasing={{}: (6, {})} | custom-call | tf_op jit(solution)/shard_map/finish/pallas_call | solution.py:541
  (4 shorter events, 0.1 us)
Async XLA Ops:
  3.0 13.9 %collective-permute-start = (bf16[4,64,768]{2,1,0:T(8,128)(2,1)}, bf16[4,64,768]{2,1,0:T(8,128)(2,1)S(1)}, u32[]{:S(2)}, u32[]{:S(2)}) collective-permute-start(bf16[4,64,768]{2,1,0:T(8,128)(2,1)} %get-tuple-element.31.refs_0_), channel_id=1, source_target_pairs={{0,2},{1,3},{2,6},{3,7},{6,4},{7,5},{4,0},{5,1},{8,10},{9,11},{10,... | collective-permute-start | bytes 1179656 | tf_op jit(solution)/shard_map/ppermute | solution.py:385
  6.0 10.9 %collective-permute-start.3 = (bf16[4,64,768]{2,1,0:T(8,128)(2,1)}, bf16[4,64,768]{2,1,0:T(8,128)(2,1)S(1)}, u32[]{:S(2)}, u32[]{:S(2)}) collective-permute-start(bf16[4,64,768]{2,1,0:T(8,128)(2,1)} %get-tuple-element.33.shifted), channel_id=1, source_target_pairs={{0,1},{1,0},{2,3},{3,2},{4,5},{5,4},{6,7},{7,6},{8,9},{9,8},{10,11... | collective-permute-start | bytes 1179656 | tf_op jit(solution)/shard_map/ppermute | solution.py:372
  6.0 9.6 %collective-permute-start.1 = (bf16[96,1536]{1,0:T(8,128)(2,1)}, bf16[96,1536]{1,0:T(8,128)(2,1)S(1)}, u32[]{:S(2)}, u32[]{:S(2)}) collective-permute-start(bf16[96,1536]{1,0:T(8,128)(2,1)} %get-tuple-element.30.refs_0_), channel_id=1, source_target_pairs={{0,8},{8,0},{16,24},{24,16},{1,9},{9,1},{17,25},{25,17},{2,10},{10... | collective-permute-start | bytes 884744 | tf_op jit(solution)/shard_map/ppermute | solution.py:391
  7.5 9.4 %collective-permute-start.2 = (bf16[96,1536]{1,0:T(8,128)(2,1)}, bf16[96,1536]{1,0:T(8,128)(2,1)S(1)}, u32[]{:S(2)}, u32[]{:S(2)}) collective-permute-start(bf16[96,1536]{1,0:T(8,128)(2,1)} %get-tuple-element.30.refs_0_), channel_id=1, source_target_pairs={{0,16},{8,24},{16,0},{24,8},{1,17},{9,25},{17,1},{25,9},{2,18},{10... | collective-permute-start | bytes 884744 | tf_op jit(solution)/shard_map/ppermute | solution.py:391
  9.1 1.6 %copy-start.1 = (bf16[64,128,128]{2,1,0:T(8,128)(2,1)S(1)}, bf16[64,128,128]{2,1,0:T(8,128)(2,1)}, u32[]{:S(2)}) copy-start(bf16[64,128,128]{2,1,0:T(8,128)(2,1)} %pair.1) | copy-start | bytes 6291460
  10.7 0.9 %copy-start.6 = (bf16[192,384]{1,0:T(8,128)(2,1)S(1)}, bf16[192,384]{1,0:T(8,128)(2,1)}, u32[]{:S(2)}) copy-start(bf16[192,384]{1,0:T(8,128)(2,1)} %value_weight.1) | copy-start | bytes 442372
  11.6 0.7 %copy-start.7 = (bf16[128,8]{0,1:T(8,128)(2,1)S(1)}, bf16[128,8]{0,1:T(8,128)(2,1)}, u32[]{:S(2)}) copy-start(bf16[128,8]{0,1:T(8,128)(2,1)} %param.17) | copy-start | bytes 6148
  12.2 14.1 %copy-start.3 = (bf16[96,1536]{1,0:T(8,128)(2,1)S(1)}, bf16[96,1536]{1,0:T(8,128)(2,1)}, u32[]{:S(2)}) copy-start(bf16[96,1536]{1,0:T(8,128)(2,1)} %get-tuple-element.30.refs_0_) | copy-start | bytes 884740
  14.1 20.7 %copy-start.8 = (bf16[384]{0:T(512)(128)(2,1)S(1)}, bf16[384]{0:T(512)(128)(2,1)}, u32[]{:S(2)}) copy-start(bf16[384]{0:T(512)(128)(2,1)} %param.19) | copy-start | bytes 2308
  14.1 21.2 %copy-start.4 = (bf16[4,64,768]{2,1,0:T(8,128)(2,1)S(1)}, bf16[4,64,768]{2,1,0:T(8,128)(2,1)}, u32[]{:S(2)}) copy-start(bf16[4,64,768]{2,1,0:T(8,128)(2,1)} %get-tuple-element.33.shifted) | copy-start | bytes 1179652
  14.1 21.2 %copy-start.5 = (bf16[4,64,768]{2,1,0:T(8,128)(2,1)S(1)}, bf16[4,64,768]{2,1,0:T(8,128)(2,1)}, u32[]{:S(2)}) copy-start(bf16[4,64,768]{2,1,0:T(8,128)(2,1)} %get-tuple-element.31.refs_0_) | copy-start | bytes 1179652
  16.9 11.3 %collective-permute-start.12 = (bf16[4,64,768]{2,1,0:T(8,128)(2,1)S(1)}, bf16[4,64,768]{2,1,0:T(8,128)(2,1)S(1)}, u32[]{:S(2)}, u32[]{:S(2)}) collective-permute-start(bf16[4,64,768]{2,1,0:T(8,128)(2,1)S(1)} %collective-permute-done.refs_1_), channel_id=1, source_target_pairs={{0,2},{1,3},{2,6},{3,7},{6,4},{7,5},{4,0},{5,1},{8,10},{9,11},{10,... | collective-permute-start | bytes 1179656 | tf_op jit(solution)/shard_map/ppermute | solution.py:385
  19.5 6.8 %collective-permute-start.4 = (bf16[96,768]{1,0:T(8,128)(2,1)S(1)}, bf16[96,768]{1,0:T(8,128)(2,1)S(1)}, u32[]{:S(2)}, u32[]{:S(2)}) collective-permute-start(bf16[96,768]{1,0:T(8,128)(2,1)S(1)} %slice.6), channel_id=1, source_target_pairs={{0,8},{8,0},{16,24},{24,16},{1,9},{9,1},{17,25},{25,17},{2,10},{10... | collective-permute-start | bytes 442376 | tf_op jit(solution)/shard_map/ppermute | solution.py:391
  20.1 11.6 %collective-permute-start.7 = (bf16[800,128]{1,0:T(8,128)(2,1)S(1)}, bf16[800,128]{1,0:T(8,128)(2,1)S(1)}, u32[]{:S(2)}, u32[]{:S(2)}) collective-permute-start(bf16[800,128]{1,0:T(8,128)(2,1)S(1)} %bias.1.refs_3_), channel_id=1, source_target_pairs={{0,24},{8,16},{16,8},{24,0},{1,25},{9,17},{17,9},{25,1},{2,26},{10... | collective-permute-start | bytes 614408 | tf_op jit(solution)/shard_map/ppermute | solution.py:391
  22.6 9.9 %collective-permute-start.8 = (bf16[800,128]{1,0:T(8,128)(2,1)S(1)}, bf16[800,128]{1,0:T(8,128)(2,1)S(1)}, u32[]{:S(2)}, u32[]{:S(2)}) collective-permute-start(bf16[800,128]{1,0:T(8,128)(2,1)S(1)} %bias.1.refs_3_), channel_id=1, source_target_pairs={{0,16},{8,24},{16,0},{24,8},{1,17},{9,25},{17,1},{25,9},{2,18},{10... | collective-permute-start | bytes 614408 | tf_op jit(solution)/shard_map/ppermute | solution.py:391
  23.1 10.2 %collective-permute-start.9 = (bf16[800,128]{1,0:T(8,128)(2,1)S(1)}, bf16[800,128]{1,0:T(8,128)(2,1)S(1)}, u32[]{:S(2)}, u32[]{:S(2)}) collective-permute-start(bf16[800,128]{1,0:T(8,128)(2,1)S(1)} %bias.1.refs_3_), channel_id=1, source_target_pairs={{0,8},{8,0},{16,24},{24,16},{1,9},{9,1},{17,25},{25,17},{2,10},{10... | collective-permute-start | bytes 614408 | tf_op jit(solution)/shard_map/ppermute | solution.py:391
  26.4 7.5 %collective-permute-start.5 = (bf16[4,96,384]{2,1,0:T(8,128)(2,1)S(1)}, bf16[4,96,384]{2,1,0:T(8,128)(2,1)S(1)}, u32[]{:S(2)}, u32[]{:S(2)}) collective-permute-start(bf16[4,96,384]{2,1,0:T(8,128)(2,1)S(1)} %get-tuple-element.36.query_mine), channel_id=1, source_target_pairs={{0,1},{1,0},{2,3},{3,2},{4,5},{5,4},{6,7},{7,6},{8,9},{9,8},{10,11... | collective-permute-start | bytes 884744 | tf_op jit(solution)/shard_map/ppermute | solution.py:372
  28.2 11.6 %collective-permute-start.14 = (bf16[4,64,768]{2,1,0:T(8,128)(2,1)S(1)}, bf16[4,64,768]{2,1,0:T(8,128)(2,1)S(1)}, u32[]{:S(2)}, u32[]{:S(2)}) collective-permute-start(bf16[4,64,768]{2,1,0:T(8,128)(2,1)S(1)} %collective-permute-done.12.refs_2_), channel_id=1, source_target_pairs={{0,2},{1,3},{2,6},{3,7},{6,4},{7,5},{4,0},{5,1},{8,10},{9,11},{10,... | collective-permute-start | bytes 1179656 | tf_op jit(solution)/shard_map/ppermute | solution.py:385
  31.7 3.1 %collective-permute-start.6 = (bf16[4,96,384]{2,1,0:T(8,128)(2,1)S(1)}, bf16[4,96,384]{2,1,0:T(8,128)(2,1)S(1)}, u32[]{:S(2)}, u32[]{:S(2)}) collective-permute-start(bf16[4,96,384]{2,1,0:T(8,128)(2,1)S(1)} %get-tuple-element.37.key_mine), channel_id=1, source_target_pairs={{0,1},{1,0},{2,3},{3,2},{4,5},{5,4},{6,7},{7,6},{8,9},{9,8},{10,11... | collective-permute-start | bytes 884744 | tf_op jit(solution)/shard_map/ppermute | solution.py:372
  33.3 2.0 %collective-permute-start.11 = (bf16[4,288,128]{2,1,0:T(8,128)(2,1)S(1)}, bf16[4,288,128]{2,1,0:T(8,128)(2,1)S(1)}, u32[]{:S(2)}, u32[]{:S(2)}) collective-permute-start(bf16[4,288,128]{2,1,0:T(8,128)(2,1)S(1)} %get-tuple-element.42.own_value), channel_id=1, source_target_pairs={{0,1},{1,0},{2,3},{3,2},{4,5},{5,4},{6,7},{7,6},{8,9},{9,8},{10,11... | collective-permute-start | bytes 884744 | tf_op jit(solution)/shard_map/ppermute | solution.py:372
  33.4 1.9 %collective-permute-start.10 = (bf16[4,256,128]{2,1,0:T(8,128)(2,1)S(1)}, bf16[4,256,128]{2,1,0:T(8,128)(2,1)S(1)}, u32[]{:S(2)}, u32[]{:S(2)}) collective-permute-start(bf16[4,256,128]{2,1,0:T(8,128)(2,1)S(1)} %get-tuple-element.41), channel_id=1, source_target_pairs={{0,1},{1,0},{2,3},{3,2},{4,5},{5,4},{6,7},{7,6},{8,9},{9,8},{10,11... | collective-permute-start | bytes 786440 | tf_op jit(solution)/shard_map/ppermute | solution.py:372
  33.9 5.9 %collective-permute-start.13 = (bf16[96,768]{1,0:T(8,128)(2,1)S(1)}, bf16[96,768]{1,0:T(8,128)(2,1)S(1)}, u32[]{:S(2)}, u32[]{:S(2)}) collective-permute-start(bf16[96,768]{1,0:T(8,128)(2,1)S(1)} %slice_bitcast_fusion), channel_id=1, source_target_pairs={{0,8},{8,0},{16,24},{24,16},{1,9},{9,1},{17,25},{25,17},{2,10},{10... | collective-permute-start | bytes 442376 | tf_op jit(solution)/shard_map/ppermute | solution.py:391
  41.0 1.9 %copy-start = (bf16[4,64,768]{2,1,0:T(8,128)(2,1)S(1)}, bf16[4,64,768]{2,1,0:T(8,128)(2,1)}, u32[]{:S(2)}) copy-start(bf16[4,64,768]{2,1,0:T(8,128)(2,1)} %activations.3) | copy-start | bytes 1179652
  41.0 1.8 %copy-start.2 = (bf16[4,64,768]{2,1,0:T(8,128)(2,1)S(1)}, bf16[4,64,768]{2,1,0:T(8,128)(2,1)}, u32[]{:S(2)}) copy-start(bf16[4,64,768]{2,1,0:T(8,128)(2,1)} %output_gate.3) | copy-start | bytes 1179652
  41.0 1.8 %collective-permute-start.16 = (f32[1,400,128]{2,1,0:T(8,128)S(1)}, f32[1,400,128]{2,1,0:T(8,128)S(1)}, u32[]{:S(2)}, u32[]{:S(2)}) collective-permute-start(f32[1,400,128]{2,1,0:T(8,128)S(1)} %get-tuple-element.54), channel_id=1, source_target_pairs={{0,1},{1,0},{2,3},{3,2},{4,5},{5,4},{6,7},{7,6},{8,9},{9,8},{10,11... | collective-permute-start | bytes 614408 | tf_op jit(solution)/shard_map/ppermute | solution.py:372
  42.3 1.6 %collective-permute-start.15 = (f32[1,400,128]{2,1,0:T(8,128)S(1)}, f32[1,400,128]{2,1,0:T(8,128)S(1)}, u32[]{:S(2)}, u32[]{:S(2)}) collective-permute-start(f32[1,400,128]{2,1,0:T(8,128)S(1)} %get-tuple-element.51), channel_id=1, source_target_pairs={{0,1},{1,0},{2,3},{3,2},{4,5},{5,4},{6,7},{7,6},{8,9},{9,8},{10,11... | collective-permute-start | bytes 614408 | tf_op jit(solution)/shard_map/ppermute | solution.py:372
